TPU v7x, 32 devices: a whole 2x2x4 slice. The times are simulated.
32 devices in a mesh: dp: 2 (over core), fsdp: 16 (over z, y, x).
Axes of the slice: x: 2, y: 2, z: 4, core: 2. Of those that a mesh axis runs over, the one named last changes fastest.
Arguments:
- chars: int32 [2, 64, 35, 21], P(None, ('dp', 'fsdp')), may hold values from 0 to 50
- lengths: int32 [2, 64, 35], P(None, ('dp', 'fsdp')), may hold values from 1 to 21
- targets: int32 [2, 64, 35], P(None, ('dp', 'fsdp')), may hold values from 0 to 9999
- resets: int32 [2, 64, 35], P(None, ('dp', 'fsdp')), may hold values 0 or 1
- init_state: float32 [2, 64, 2, 650], P(None, ('dp', 'fsdp')), may hold values from -3 to 3
- window_grad: float32 [2, 64], P(None, ('dp', 'fsdp')), may hold values from -6 to 6
- char_table: bfloat16 [51, 15], replicated, may hold values from -6 to 6
- conv_weight: bfloat16 [105, 1100], replicated, may hold values from -0.875 to 0.875
- conv_bias: bfloat16 [1100], replicated, may hold values from -3 to 3
- highway_flat: bfloat16 [37856, 128], P('fsdp'), may hold values from -6 to 6
- lstm_flat: bfloat16 [35584, 128], P('fsdp'), may hold values from -6 to 6
- soft_flat: bfloat16 [50880, 128], P('fsdp'), may hold values from -6 to 6
Outputs:
- window_loss: float32 [2, 64], P(None, ('dp', 'fsdp'))
- table_grad: float32 [51, 15], replicated
- conv_weight_grad: float32 [105, 1100], replicated
- conv_bias_grad: float32 [1100], replicated
- highway_grad: float32 [37856, 128], P(('dp', 'fsdp'))
- lstm_grad: float32 [35584, 128], P(('dp', 'fsdp'))
- soft_grad: float32 [50880, 128], P(('dp', 'fsdp'))
All inputs are finite; a program needn't handle non-finite values. No bound on the sum of `resets` on one device may be relied on, other than what follows from the above.
Results may differ from a plain program's by a relative error of at most 0.0099.
Values may be sent and summed in bfloat16 or wider, within the bound.
A program may use at most 320 MiB of HBM per device.

v0:
```python
import jax
import jax.numpy as jnp
from jax import lax
from jax.sharding import PartitionSpec as P

H = 650
V = 10000
KMAX = 7


FILTER_CUTS = (1, 3, 6, 10, 14, 18)


def filter_widths(filters):
    column = jnp.arange(filters, dtype=jnp.int32)
    widths = jnp.ones((filters,), jnp.int32)
    for cut_at in FILTER_CUTS:
        widths = widths + (column >= filters * cut_at // 22).astype(jnp.int32)
    return widths


def plain_dot(left, right):
    return jnp.dot(left, right, preferred_element_type=jnp.float32)


def rows_inner(left, right):
    return lax.dot_general(
        left, right, (((0,), (0,)), ((), ())), preferred_element_type=jnp.float32
    )


def cols_inner(left, right):
    return lax.dot_general(
        left, right, (((1,), (1,)), ((), ())), preferred_element_type=jnp.float32
    )


def split_highway(gathered, filters):
    flat_all = gathered.reshape(-1)
    square = filters * filters
    layers = []
    for layer_no in range(2):
        offset = layer_no * (2 * square + 2 * filters)
        w_trans = flat_all[offset : offset + square].reshape(filters, filters)
        b_trans = flat_all[offset + square : offset + square + filters]
        w_gate = flat_all[offset + square + filters : offset + 2 * square + filters].reshape(
            filters, filters
        )
        b_gate = flat_all[offset + 2 * square + filters : offset + 2 * square + 2 * filters]
        layers.append((w_trans, b_trans, w_gate, b_gate))
    return layers


def split_lstm(gathered, filters):
    flat_all = gathered.reshape(-1)
    first_end = filters * 4 * H
    second_end = first_end + 4 * H * H
    return (
        flat_all[:first_end].reshape(filters, 4 * H),
        flat_all[first_end:second_end].reshape(H, 4 * H),
        flat_all[second_end : second_end + 4 * H],
    )


def split_soft(gathered):
    flat_all = gathered.reshape(-1)
    return (flat_all[: H * V].reshape(H, V), flat_all[H * V : H * V + V])


def pack_flat(pieces, row_total):
    joined = jnp.concatenate([each_piece.reshape(-1) for each_piece in pieces])
    return jnp.pad(joined, (0, row_total * 128 - joined.shape[0])).reshape(row_total, 128)


def add_lists(running, fresh):
    if running is None:
        return fresh
    return [left + right for left, right in zip(running, fresh)]


def shards(
    chars,
    lengths,
    targets,
    resets,
    init_state,
    window_grad,
    char_table,
    conv_weight,
    conv_bias,
    highway_flat,
    lstm_flat,
    soft_flat,
):
    micro_count, streams, step_count, letters = chars.shape
    char_count, embed_dim = char_table.shape
    filters = conv_weight.shape[1]
    word_rows = streams * step_count
    fsdp_count = lax.axis_size("fsdp")
    highway_rows = highway_flat.shape[0] * fsdp_count
    lstm_rows = lstm_flat.shape[0] * fsdp_count
    soft_rows = soft_flat.shape[0] * fsdp_count
    widths = filter_widths(filters)
    positions = jnp.arange(letters, dtype=jnp.int32)
    kernel_mask = (
        jnp.arange(KMAX * embed_dim, dtype=jnp.int32)[:, None] // embed_dim < widths[None, :]
    )
    conv_kernel = jnp.where(kernel_mask, conv_weight, jnp.zeros_like(conv_weight))
    bias_conv = conv_bias.astype(jnp.float32)
    vocab_ids = jnp.arange(V, dtype=jnp.int32)
    char_ids = jnp.arange(char_count, dtype=jnp.int32)

    def lstm_run(feature, lstm_w, keep_all, state_now):
        w_input, w_recur, b_lstm = lstm_w
        from_input = (plain_dot(feature, w_input) + b_lstm.astype(jnp.float32)).reshape(
            streams, step_count, 4 * H
        )

        def lstm_step(carried, slices):
            hidden, cell_state = carried
            input_now, keep_now = slices
            hidden = hidden * keep_now[:, None].astype(jnp.bfloat16)
            cell_state = cell_state * keep_now[:, None]
            gate_sums = input_now + plain_dot(hidden, w_recur)
            gate_in = jax.nn.sigmoid(gate_sums[:, :H])
            gate_forget = jax.nn.sigmoid(gate_sums[:, H : 2 * H])
            gate_update = jnp.tanh(gate_sums[:, 2 * H : 3 * H])
            gate_out = jax.nn.sigmoid(gate_sums[:, 3 * H :])
            cell_now = gate_forget * cell_state + gate_in * gate_update
            hidden_now = (gate_out * jnp.tanh(cell_now)).astype(jnp.bfloat16)
            return (
                (hidden_now, cell_now),
                (
                    hidden,
                    cell_state,
                    gate_in,
                    gate_forget,
                    gate_update,
                    gate_out,
                    cell_now,
                    hidden_now,
                ),
            )

        start_state = (state_now[:, 0, :].astype(jnp.bfloat16), state_now[:, 1, :])
        _, history = lax.scan(lstm_step, start_state, (jnp.swapaxes(from_input, 0, 1), keep_all.T))
        return history

    def lstm_backward(history, soft_part, keep_all, w_recur):
        prev_hidden, prev_cell, in_gate, forget, update, out_gate, cell_new, hidden_new = history

        def back_step(carried, slices):
            grad_hidden, grad_cell = carried
            soft_now, cell_prev, gate_in, gate_forget, gate_update, gate_out, cell_now, keep_now = (
                slices
            )
            grad_h = soft_now + grad_hidden
            tanh_cell = jnp.tanh(cell_now)
            grad_c = grad_cell + grad_h * gate_out * (1.0 - tanh_cell * tanh_cell)
            grad_gates = jnp.concatenate(
                [
                    grad_c * gate_update * gate_in * (1.0 - gate_in),
                    grad_c * cell_prev * gate_forget * (1.0 - gate_forget),
                    grad_c * gate_in * (1.0 - gate_update * gate_update),
                    grad_h * tanh_cell * gate_out * (1.0 - gate_out),
                ],
                axis=1,
            ).astype(jnp.bfloat16)
            keep_col = keep_now[:, None]
            return (
                (cols_inner(grad_gates, w_recur) * keep_col, grad_c * gate_forget * keep_col),
                grad_gates,
            )

        zero_state = (jnp.zeros((streams, H), jnp.float32), jnp.zeros((streams, H), jnp.float32))
        _, grad_gates_all = lax.scan(
            back_step,
            zero_state,
            (soft_part, prev_cell, in_gate, forget, update, out_gate, cell_new, keep_all.T),
            reverse=True,
        )
        grad_w_recur = rows_inner(prev_hidden.reshape(-1, H), grad_gates_all.reshape(-1, 4 * H))
        gates_rows = jnp.swapaxes(grad_gates_all, 0, 1).reshape(word_rows, 4 * H)
        return (gates_rows, grad_w_recur)

    table_total = jnp.zeros((char_count, embed_dim), jnp.float32)
    kernel_total = jnp.zeros(conv_weight.shape, jnp.float32)
    bias_total = jnp.zeros((filters,), jnp.float32)
    running_highway = None
    running_lstm = None
    running_soft = None
    shard_highway = None
    shard_lstm = None
    shard_soft = None
    losses = []
    for micro_no in range(micro_count):
        lengths_now = lengths[micro_no]
        present = positions[None, None, :] < lengths_now[:, :, None]
        looked = jnp.take(char_table, chars[micro_no], axis=0)
        embedded = jnp.where(present[..., None], looked, jnp.zeros_like(looked)).reshape(
            word_rows, letters, embed_dim
        )
        padded = jnp.pad(embedded, ((0, 0), (0, KMAX - 1), (0, 0)))
        windows = jnp.concatenate(
            [padded[:, shift_by : shift_by + letters, :] for shift_by in range(KMAX)], axis=2
        ).reshape(word_rows * letters, KMAX * embed_dim)
        activated = jnp.tanh(plain_dot(windows, conv_kernel) + bias_conv).reshape(
            word_rows, letters, filters
        )
        counts = jnp.maximum(lengths_now.reshape(word_rows, 1) - widths[None, :] + 1, 1)
        inside = positions[None, :, None] < counts[:, None, :]
        exp_valid = jnp.where(inside, jnp.exp(activated), 0.0)
        totals = jnp.sum(exp_valid, axis=1)
        pooled = jnp.log(totals) - jnp.log(counts.astype(jnp.float32))
        windows, activated, pool_weight, present, pooled = (
            windows,
            activated,
            exp_valid / totals[:, None, :],
            present,
            pooled.astype(jnp.bfloat16),
        )
        highway_w = split_highway(lax.all_gather(highway_flat, "fsdp", axis=0, tiled=True), filters)
        highway_feature = pooled
        highway_stored = []
        for highway_w_trans, highway_b_trans, highway_w_gate, highway_b_gate in highway_w:
            highway_trans_pre = plain_dot(
                highway_feature, highway_w_trans
            ) + highway_b_trans.astype(jnp.float32)
            highway_gate_now = jax.nn.sigmoid(
                plain_dot(highway_feature, highway_w_gate) + highway_b_gate.astype(jnp.float32)
            )
            highway_stored.append((highway_feature, highway_trans_pre, highway_gate_now))
            highway_feature = (
                highway_gate_now * jax.nn.silu(highway_trans_pre)
                + (1.0 - highway_gate_now) * highway_feature.astype(jnp.float32)
            ).astype(jnp.bfloat16)
        feature = highway_feature
        lstm_w = split_lstm(lax.all_gather(lstm_flat, "fsdp", axis=0, tiled=True), filters)
        keep_all = (1 - resets[micro_no]).astype(jnp.float32)
        history = lstm_run(feature, lstm_w, keep_all, init_state[micro_no])
        soft_w = split_soft(lax.all_gather(soft_flat, "fsdp", axis=0, tiled=True))
        hidden_rows = jnp.swapaxes(history[7], 0, 1).reshape(word_rows, H)
        logits = plain_dot(hidden_rows, soft_w[0]) + soft_w[1].astype(jnp.float32)
        log_total = jax.nn.logsumexp(logits, axis=1)
        target_hit = targets[micro_no].reshape(word_rows, 1) == vocab_ids[None, :]
        picked = jnp.sum(jnp.where(target_hit, logits, 0.0), axis=1)
        losses.append(jnp.mean((log_total - picked).reshape(streams, step_count), axis=1))
        row_scale = jnp.broadcast_to(
            window_grad[micro_no][:, None] / step_count, (streams, step_count)
        ).reshape(word_rows, 1)
        grad_logits = (
            (jnp.exp(logits - log_total[:, None]) - target_hit.astype(jnp.float32)) * row_scale
        ).astype(jnp.bfloat16)
        soft_grads = [
            rows_inner(hidden_rows, grad_logits),
            jnp.sum(grad_logits.astype(jnp.float32), axis=0),
        ]
        soft_part = jnp.swapaxes(
            cols_inner(grad_logits, soft_w[0]).reshape(streams, step_count, H), 0, 1
        )
        gates_rows, grad_w_recur = lstm_backward(history, soft_part, keep_all, lstm_w[1])
        lstm_grads = [
            rows_inner(feature, gates_rows),
            grad_w_recur,
            jnp.sum(gates_rows.astype(jnp.float32), axis=0),
        ]
        grad_feature = cols_inner(gates_rows, lstm_w[0])
        highway_grad_feature = grad_feature
        grad_list = []
        for (layer_in, trans_pre, gate_now), (w_trans, b_trans, w_gate, b_gate) in reversed(
            list(zip(highway_stored, highway_w))
        ):
            sig_trans = jax.nn.sigmoid(trans_pre)
            silu_val = trans_pre * sig_trans
            grad_trans = (
                highway_grad_feature * gate_now * sig_trans * (1.0 + trans_pre * (1.0 - sig_trans))
            ).astype(jnp.bfloat16)
            grad_gate = (
                highway_grad_feature
                * (silu_val - layer_in.astype(jnp.float32))
                * gate_now
                * (1.0 - gate_now)
            ).astype(jnp.bfloat16)
            next_grad = (
                highway_grad_feature * (1.0 - gate_now)
                + cols_inner(grad_trans, w_trans)
                + cols_inner(grad_gate, w_gate)
            )
            grad_list = [
                rows_inner(layer_in, grad_trans),
                jnp.sum(grad_trans.astype(jnp.float32), axis=0),
                rows_inner(layer_in, grad_gate),
                jnp.sum(grad_gate.astype(jnp.float32), axis=0),
            ] + grad_list
            highway_grad_feature = next_grad
        grad_act = highway_grad_feature[:, None, :] * pool_weight
        grad_pre = (
            (grad_act * (1.0 - activated * activated))
            .astype(jnp.bfloat16)
            .reshape(word_rows * letters, filters)
        )
        grad_kernel = jnp.where(kernel_mask, rows_inner(windows, grad_pre), 0.0)
        grad_bias = jnp.sum(grad_pre.astype(jnp.float32), axis=0)
        grad_windows = cols_inner(grad_pre, conv_kernel).reshape(
            word_rows, letters, KMAX, embed_dim
        )
        shifted = jnp.pad(grad_windows, ((0, 0), (KMAX - 1, 0), (0, 0), (0, 0)))
        grad_chars = jnp.zeros((word_rows, letters, embed_dim), jnp.float32)
        for conv_shift_by in range(KMAX):
            grad_chars = (
                grad_chars
                + shifted[
                    :,
                    KMAX - 1 - conv_shift_by : KMAX - 1 - conv_shift_by + letters,
                    conv_shift_by,
                    :,
                ]
            )
        grad_chars = jnp.where(present.reshape(word_rows, letters, 1), grad_chars, 0.0).reshape(
            word_rows * letters, embed_dim
        )
        one_hot = (char_ids[:, None] == chars[micro_no].reshape(1, -1)).astype(jnp.float32)
        grad_table = jnp.dot(
            one_hot, grad_chars, precision=lax.Precision.HIGHEST, preferred_element_type=jnp.float32
        )
        grad_table, grad_kernel, grad_bias = (grad_table, grad_kernel, grad_bias)
        table_total = table_total + grad_table
        kernel_total = kernel_total + grad_kernel
        bias_total = bias_total + grad_bias
        running_highway = add_lists(running_highway, grad_list)
        running_lstm = add_lists(running_lstm, lstm_grads)
        running_soft = add_lists(running_soft, soft_grads)
    flat_highway = pack_flat(running_highway, highway_rows)
    flat_lstm = pack_flat(running_lstm, lstm_rows)
    flat_soft = pack_flat(running_soft, soft_rows)
    shard_highway, shard_lstm, shard_soft = (
        lax.psum_scatter(flat_highway, ("dp", "fsdp"), scatter_dimension=0, tiled=True),
        lax.psum_scatter(flat_lstm, ("dp", "fsdp"), scatter_dimension=0, tiled=True),
        lax.psum_scatter(flat_soft, ("dp", "fsdp"), scatter_dimension=0, tiled=True),
    )
    table_grad, conv_weight_grad, conv_bias_grad = lax.psum(
        (table_total, kernel_total, bias_total), ("dp", "fsdp")
    )
    window_loss = jnp.stack(losses)
    return (
        window_loss,
        table_grad,
        conv_weight_grad,
        conv_bias_grad,
        shard_highway,
        shard_lstm,
        shard_soft,
    )


def solution(mesh):
    in_specs = (
        P(None, ("dp", "fsdp"), None, None),
        P(None, ("dp", "fsdp"), None),
        P(None, ("dp", "fsdp"), None),
        P(None, ("dp", "fsdp"), None),
        P(None, ("dp", "fsdp"), None, None),
        P(None, ("dp", "fsdp")),
        P(),
        P(),
        P(),
        P("fsdp", None),
        P("fsdp", None),
        P("fsdp", None),
    )
    out_specs = (
        P(None, ("dp", "fsdp")),
        P(),
        P(),
        P(),
        P(("dp", "fsdp"), None),
        P(("dp", "fsdp"), None),
        P(("dp", "fsdp"), None),
    )
    return jax.shard_map(shards, mesh=mesh, in_specs=in_specs, out_specs=out_specs, check_vma=False)
```

profile of v0, /device:TPU:0, one launch (start us, length us, event | category | flops | bytes accessed | tf_op | source)
XLA Modules:
  0.0 3002.2 jit_solution(12390536164848093431)
XLA Ops:
  62.2 7.2 exp.74
  71.8 7.5 fusion.188
  79.3 7.1 exp.81
  102.2 7.6 div.129
  113.4 7.2 lt.193
  125.6 7.1 div.124
  136.4 7.2 lt.188
  155.1 12.4 reshape.624
  174.4 84.0 %all-gather.8.cloned.1.call-done = bf16[16,2366,128]{2,1,0:T(8,128)(2,1)} async-done(((bf16[1,2366,128]{2,1,0:T(8,128)(2,1)}), bf16[16,2366,128]{2,1,0:T(8,128)(2,1)}) %all-gather.8.cloned.1.call-update) | async-done | bytes 9691152 | tf_op jit(solution)/shard_map/all_gather | solution.py:222
  258.4 8.6 reshape.618
  267.0 8.8 fusion.181
  284.1 6.9 reshape.619
  323.1 174.1 %while.95 = (s32[]{:T(128)}, bf16[2,650]{1,0:T(2,128)(2,1)S(1)}, f32[2,650]{1,0:T(2,128)S(1)}, bf16[35,2,650]{2,1,0:T(2,128)(2,1)}, f32[35,2,650]{2,1,0:T(2,128)...) while((s32[]{:T(128)}, bf16[2,650]{1,0:T(2,128)(2,1)S(1)}, ...), condition=%wide.region_9.11_spmd, body=%wide.region_8.10_spmd.sunk | while | flops 6808104 | bytes 3576625 | solution.py:146
  515.6 173.5 %while.94 = (s32[]{:T(128)}, bf16[2,650]{1,0:T(2,128)(2,1)S(1)}, f32[2,650]{1,0:T(2,128)S(1)}, bf16[35,2,650]{2,1,0:T(2,128)(2,1)}, f32[35,2,650]{2,1,0:T(2,128)...) while((s32[]{:T(128)}, bf16[2,650]{1,0:T(2,128)(2,1)S(1)}, ...), condition=%wide.region_2.4_spmd, body=%wide.region_1.3_spmd.sunk | while | flops 6808104 | bytes 3576625 | solution.py:146
  695.4 12.4 reshape.628
  709.2 10.0 slice.290
  719.2 20.9 reshape.629
  740.0 21.2 reshape.683
  761.3 7.5 fusion.189
  783.3 10.0 convolution_bitcast_fusion
  794.2 238.7 %while.97 = (s32[]{:T(128)}, f32[2,650]{1,0:T(2,128)}, f32[2,650]{1,0:T(2,128)}, bf16[35,2,2600]{2,1,0:T(2,128)(2,1)}, f32[35,2,650]{2,0,1:T(8,128)}, /*index=5*...) while((s32[]{:T(128)}, f32[2,650]{1,0:T(2,128)}, ...), condition=%wide.region_17.19_spmd.clone, body=%wide.region_16.18_spmd.clone.sunk | while | flops 6800304 | bytes 3547043 | solution.py:176
  1052.7 7.1 mul.679
  1067.6 10.0 convolution_bitcast_fusion.1
  1078.6 237.4 %while.96 = (s32[]{:T(128)}, f32[2,650]{1,0:T(2,128)}, f32[2,650]{1,0:T(2,128)}, bf16[35,2,2600]{2,1,0:T(2,128)(2,1)}, f32[35,2,650]{2,0,1:T(8,128)}, /*index=5*...) while((s32[]{:T(128)}, f32[2,650]{1,0:T(2,128)}, ...), condition=%wide.region_15.17_spmd.clone, body=%wide.region_14.16_spmd.clone.sunk | while | flops 6800304 | bytes 3547043 | solution.py:176
  1318.5 7.1 fusion.195
  1339.6 7.1 mul.655
  1346.8 25.7 convert_reduce_fusion
  1372.5 7.0 sub.309
  1379.5 8.6 multiply_convert_fusion.2
  1388.1 7.0 sub.308
  1395.1 7.9 multiply_convert_fusion.3
  1405.8 10.8 convolution_add_fusion.3
  1416.6 14.7 reshape.640
  1437.6 9.6 reshape.641
  1447.2 143.7 %concatenate.136 = f32[4552600]{0:T(1024)} concatenate(f32[2860000]{0:T(1024)} %reshape.640, f32[1690000]{0:T(1024)} %reshape.641, f32[2600]{0:T(1024)S(1)} %add.617), dimensions={0} | concatenate | bytes 36420800 | tf_op jit(solution)/shard_map/concatenate | solution.py:71
  1590.9 14.7 pad_bitcast_fusion.1
  1635.7 7.3 reshape.635
  1647.3 7.5 reshape.636
  1659.0 7.3 reshape.637
  1670.6 7.4 reshape.638
  1678.0 10.8 fusion.196
  1688.7 17.3 convolution_add_fusion.2
  1706.2 26.5 reshape.643
  1732.8 161.2 %concatenate.135 = f32[4844400]{0:T(1024)} concatenate(f32[1210000]{0:T(1024)} %reshape.635, f32[1100]{0:T(1024)S(1)} %add.608, f32[1210000]{0:T(1024)} %reshape.636, f32[1100]{0:T(1024)S(1)} %add.610, f32[1210000]{0:T(1024)} %reshape.637, f32[1100]{0:T(1024)S(1)} %add.612, f32[1210000]{0:T(1024)} %reshape.638, f32[1100]{0:T(1024)S(1)} %add.614), dimensions={0} | concatenate | bytes 38755200 | tf_op jit(solution)/shard_map/concatenate | solution.py:71
  1894.0 15.6 pad_bitcast_fusion
  1909.7 24.0 fusion.58
  1933.7 1010.1 %fusion.170 = (f32[1184,128]{1,0:T(8,128)S(1)}, f32[1600,128]{1,0:T(8,128)S(1)}) fusion(f32[37856,128]{1,0:T(8,128)} %pad_bitcast_fusion, f32[50880,128]{1,0:T(8,128)} %fusion.58), kind=kCustom, calls=%all-reduce-scatter.2 | all-reduce-scatter fusion | flops 11403266 | bytes 46858240
  2948.7 40.5 %all-reduce.12 = (f32[51,15]{0,1:T(8,128)}, f32[1100]{0:T(1024)}) all-reduce(f32[51,15]{0,1:T(8,128)S(1)} %convolution_add_fusion.30, f32[1100]{0:T(1024)S(1)} %add.606), channel_id=1, replica_groups=mesh['dp'=2,'fsdp'=16] {'dp','fsdp'}, use_global_device_ids=true, to_apply=%region_18.20 | all-reduce | flops 1865 | bytes 14920 | tf_op jit(solution)/shard_map/psum | solution.py:341
  (1694 shorter events, 1114.3 us)
Async XLA Ops:
  7.2 8.9 copy-start.117
  7.2 136.4 %all-gather.6.cloned.1.call-start = ((), (), s32[]{:S(2)}) async-start(), calls=%async_computation.1 | async-start | bytes 9678848 | tf_op jit(solution)/shard_map/all_gather | solution.py:238
  7.9 250.5 %all-gather.8.cloned.1.call-start = ((), (), s32[]{:S(2)}) async-start(), calls=%async_computation.3 | async-start | bytes 10305536 | tf_op jit(solution)/shard_map/all_gather | solution.py:222
  8.7 686.7 %all-gather.10.cloned.1.call-start = ((), (), s32[]{:S(2)}) async-start(), calls=%async_computation.4 | async-start | bytes 13856768 | tf_op jit(solution)/shard_map/all_gather | solution.py:241
  9.4 2984.0 %all-reduce.16.cloned.1.call-start = ((), (), s32[]{:S(2)}) async-start(), calls=%async_computation.2 | async-start | bytes 1032192 | tf_op jit(solution)/shard_map/psum | solution.py:341
  18.0 79.5 %copy-start.76 = (s32[1100]{0:T(1024)}, s32[1100]{0:T(1024)S(1)}, u32[]{:S(2)}) copy-start(s32[1100]{0:T(1024)S(1)} %convert_add_fusion) | copy-start | bytes 13204
  18.0 34.2 %copy-start.111 = (s32[105]{0:T(128)}, s32[105]{0:T(128)S(1)}, u32[]{:S(2)}) copy-start(s32[105]{0:T(128)S(1)} %and_select_fusion) | copy-start | bytes 1264
  33.0 12.0 copy-start.106
  53.3 18.5 copy-start.18
  62.2 7.6 copy-start.48
  62.2 7.8 copy-start.47
  62.2 8.0 copy-start.46
  62.2 8.6 copy-start.78
  69.4 28.1 copy-start.102
  69.5 28.0 copy-start.104
  79.3 7.8 copy-start.119
  79.3 9.2 copy-start.120
  88.5 685.1 %copy-start.113 = (s32[70]{0:T(128)}, s32[70]{0:T(128)S(1)}, u32[]{:S(2)}) copy-start(s32[70]{0:T(128)S(1)} %eq.60) | copy-start | bytes 844
  89.4 20.4 copy-start.17
  89.4 43.4 %copy-start.16 = (s32[70,1100]{1,0:T(8,128)}, s32[70,1100]{1,0:T(8,128)S(1)}, u32[]{:S(2)}) copy-start(s32[70,1100]{1,0:T(8,128)S(1)} %get-tuple-element.1161) | copy-start | bytes 924004
  95.3 26.7 copy-start.14
  761.3 9.7 copy-start
  761.3 9.6 copy-start.50
  761.3 9.6 copy-start.69
  1395.1 8.0 copy-start.19
  1395.1 8.0 copy-start.68
  1395.1 8.0 copy-start.77
  1395.1 8.0 copy-start.112
  1395.1 8.9 copy-start.35
  1405.8 1587.6 %reduce-scatter.9.cloned.1.call-start = ((), (), s32[]{:S(2)}) async-start(), calls=%async_computation.5 | async-start | bytes 18788352
  1416.6 14.7 copy-start.53
  1437.6 9.6 copy-start.89
  1677.9 10.8 copy-start.12
  1677.9 10.8 copy-start.45
  1706.1 26.6 copy-start.97
  1706.1 26.6 copy-start.99
  1706.1 26.6 copy-start.96
  1706.1 26.6 copy-start.98
  1706.1 26.6 copy-start.93
  1706.1 26.6 copy-start.95
  1706.1 26.6 copy-start.92
  1706.1 26.6 copy-start.94
  1706.1 26.7 copy-start.80
  1706.1 26.7 copy-start.81
  1933.7 1015.0 %copy-start.90 = (f32[1100]{0:T(1024)S(1)}, f32[1100]{0:T(1024)}, u32[]{:S(2)}) copy-start(f32[1100]{0:T(1024)} %get-tuple-element.1092) | copy-start | bytes 13204
  1933.7 1015.0 %copy-start.91 = (f32[1100]{0:T(1024)S(1)}, f32[1100]{0:T(1024)}, u32[]{:S(2)}) copy-start(f32[1100]{0:T(1024)} %get-tuple-element.1155) | copy-start | bytes 13204
  2943.8 45.5 %collective-permute-start = (f32[31,128]{1,0:T(8,128)S(1)}, f32[31,128]{1,0:T(8,128)S(1)}, u32[]{:S(2)}, u32[]{:S(2)}) collective-permute-start(f32[31,128]{1,0:T(8,128)S(1)} %slice.296), channel_id=1, source_target_pairs={{0,1},{1,2},{2,3},{3,4},{4,5},{5,6},{6,7},{7,8},{8,9},{9,10},{10,1... | collective-permute-start | bytes 47624
  2945.1 46.1 %collective-permute-start.1 = (f32[310,128]{1,0:T(8,128)S(1)}, f32[310,128]{1,0:T(8,128)S(1)}, u32[]{:S(2)}, u32[]{:S(2)}) collective-permute-start(f32[310,128]{1,0:T(8,128)S(1)} %slice.297), channel_id=1, source_target_pairs={{0,1},{1,2},{2,3},{3,4},{4,5},{5,6},{6,7},{7,8},{8,9},{9,10},{10,1... | collective-permute-start | bytes 476168
  (158 other events, 523.3 us)
Sparse Core Ops, SparseCore 0:
  10.7 121.9 all-gather.5
  135.4 122.9 all-gather.7
  261.1 154.4 all-gather.9
  1405.9 125.7 all-reduce.15
  1605.8 474.0 reduce-scatter.8
where the time goes:
time: 3050 us; the launch traced here: 3000 us
  blocking collectives  1050 us (34%)
  local copies, waits for them, and re-layouts  990 us (32%)
  other arithmetic  489 us (16%)
  matrix products  365 us (12%)
  waiting for transfers between devices  86.1 us (3%)
    unnamed x1, blocking collectives  1010 us
    concatenate x2, local copies, waits for them, and re-layouts, pack_flat(): joined = jnp.concatenate([each_piece.reshape(-1) for each_piece in pieces])  305 us
    dot_general x84, matrix products, cols_inner(): lax.dot_general(left, right, (((1,), (1,)), ((), ())), preferred_element_...  207 us
    dynamic_update_slice x280, other arithmetic, lstm_run(): lax.scan(lstm_step, start_state, (jnp.swapaxes(from_input, 0, 1), keep_al...  191 us
    mul x70, other arithmetic, back_step(): grad_c * gate_forget * keep_col  99.2 us
    dot_general x84, matrix products, plain_dot(): return jnp.dot(left, right, preferred_element_type=jnp.float32)  86.2 us
    all_gather x1, waiting for transfers between devices, shards(): lax.all_gather(highway_flat, 'fsdp', axis=0, tiled=True)  84 us
    reshape x7, local copies, waits for them, and re-layouts, pack_flat(): joined = jnp.concatenate([each_piece.reshape(-1) for each_piece in pieces])  80.4 us
  transfers between devices with their start and end apart: 7, of which 1 were waited for; matrix products, arithmetic and copies ran while one was open for 71% of the time, Pallas kernels for 0%

commit v1 on v0

v1 whole, which is shorter than its diff:
```python
import functools

import jax
import jax.numpy as jnp
import numpy as np
from jax import lax
from jax.experimental import pallas as pl
from jax.experimental.pallas import tpu as pltpu
from jax.sharding import PartitionSpec as P

H = 650
V = 10000
KMAX = 7
LANE = 128
HP = 768
SLOTS = 24
HOT = 384
FILTER_CUTS = (1, 3, 6, 10, 14, 18)
MESH = pl.DeviceIdType.MESH
BF = jnp.bfloat16
F32 = jnp.float32


def up_to(value, unit):
    return -(-value // unit) * unit


def dot(left, right):
    return jnp.dot(left, right, preferred_element_type=F32)


def dot_rows(left, right):
    return lax.dot_general(left, right, (((0,), (0,)), ((), ())), preferred_element_type=F32)


def dot_cols(left, right):
    return lax.dot_general(left, right, (((1,), (1,)), ((), ())), preferred_element_type=F32)


class Windows:
    def __init__(self, flat_rows, width, used, fsdp, dp, by_rows):
        owners = fsdp * dp
        self.width, self.by_rows, self.fsdp, self.dp = width, by_rows, fsdp, dp
        self.entries = flat_rows * LANE // owners
        starts = [o * self.entries // width for o in range(owners)]
        spans = [
            (o * self.entries % width + self.entries - 1) // width + 1 for o in range(owners)
        ]
        rows = max(spans)
        while (dp * rows) % 16 or (by_rows and (dp // 2 * rows) % 16):
            rows += 1
        self.rows = rows
        self.columns = up_to(width, LANE) if by_rows else 2 * up_to(-(-width // 2), LANE)
        self.block = (
            (dp // 2 * rows, self.columns) if by_rows else (dp * rows, self.columns // 2)
        )
        self.shape = (fsdp, 2) + self.block if by_rows else (2, fsdp) + self.block

        def row_map(order):
            rows_of = [
                [starts[o] + i if i < spans[o] and starts[o] + i < used else -1 for i in range(rows)]
                for o in order
            ]
            return np.array(rows_of, np.int32).reshape(-1)

        self.gathered = row_map(range(owners))
        if by_rows:
            order = [
                (2 * jj + h) * fsdp + f
                for f in range(fsdp)
                for h in range(2)
                for jj in range(dp // 2)
            ]
        else:
            order = [d * fsdp + f for f in range(fsdp) for d in range(dp)]
        self.reduced = row_map(order)

    def pick(self, ref, half, slot):
        return ref.at[slot, half] if self.by_rows else ref.at[half, slot]

    def from_flat(self, shard, fsdp_at):
        parts = []
        flat = shard.reshape(-1)
        for j in range(self.dp):
            shift = lax.rem((fsdp_at * self.dp + j) * self.entries, self.width)
            piece = lax.dynamic_update_slice(
                jnp.zeros((self.rows * self.width,), BF),
                flat[j * self.entries : (j + 1) * self.entries],
                (shift,),
            ).reshape(self.rows, self.width)
            parts.append(jnp.pad(piece, ((0, 0), (0, self.columns - self.width))))
        joined = jnp.concatenate(parts, axis=0)
        if self.by_rows:
            return joined.reshape((2,) + self.block)
        half = self.columns // 2
        return jnp.stack([joined[:, :half], joined[:, half:]])

    def to_flat(self, window, dp_at, fsdp_at):
        shift = lax.rem((dp_at * self.fsdp + fsdp_at) * self.entries, self.width)
        flat = window[:, : self.width].reshape(-1)
        return lax.dynamic_slice(flat, (shift,), (self.entries,)).reshape(-1, LANE)


def one_hot_map(rows, row_map):
    return (
        lax.broadcasted_iota(jnp.int32, (rows, row_map.shape[0]), 0) == jnp.asarray(row_map)[None, :]
    ).astype(BF)


def compress(spread, mapping):
    high = lax.reduce_precision(spread, 8, 7)
    both = jnp.concatenate([high.astype(BF), (spread - high).astype(BF)], axis=0)
    product = dot_cols(both, mapping)
    count = spread.shape[0]
    return product[:count] + product[count:]


def place(fsdp, dp):
    d, f = lax.axis_index("dp"), lax.axis_index("fsdp")
    c = lax.rem(d, 2)
    x, y, z = lax.rem(f, 2), lax.rem(f // 2, 2), f // 4
    first, last = x + c * (y - x), y + c * (x - y)
    return d, f, c, z, first, last, 1 + c, 2 - c


def gather_kernel(plans, *refs):
    count = len(plans)
    ins, outs, sems = refs[:count], refs[count : 2 * count], refs[2 * count]
    n, dp = plans[0].fsdp, plans[0].dp
    lengthwise = n // 4
    d, f, c, z, first, last, stride1, stride3 = place(n, dp)
    partner1 = f + stride1 * (1 - 2 * first)
    partner3 = f + stride3 * (1 - 2 * last)
    sibling = (d + 1 - 2 * c, f)
    flip1 = stride1 * (1 - 2 * first)
    flip3 = stride3 * (1 - 2 * last)
    RECV, SIB_RECV, ONE, UP, DOWN, LAST, SIB, LOCAL = range(8)

    def sem(kind, a, block):
        return sems.at[(kind * count + a) * n + block]

    barrier = pltpu.get_barrier_semaphore()
    for target in ((d, partner1), (d, partner3), sibling):
        pl.semaphore_signal(barrier, inc=1, device_id=target, device_id_type=MESH)

    @pl.when(z > 0)
    def _():
        pl.semaphore_signal(barrier, inc=1, device_id=(d, f - 4), device_id_type=MESH)

    @pl.when(z < lengthwise - 1)
    def _():
        pl.semaphore_signal(barrier, inc=1, device_id=(d, f + 4), device_id_type=MESH)

    has_down = (z > 0).astype(jnp.int32)
    has_up = (z < lengthwise - 1).astype(jnp.int32)
    pl.semaphore_wait(barrier, 3 + has_down + has_up)

    def copy(kind, a, block, target, own=False):
        here = plans[a].pick(outs[a], c, block)
        return pltpu.make_async_remote_copy(
            src_ref=ins[a].at[c] if own else here,
            dst_ref=here,
            send_sem=sem(kind, a, block),
            recv_sem=sem(SIB_RECV if kind == SIB else RECV, a, block),
            device_id=target,
            device_id_type=MESH,
        )

    def arrived(a, block, kind=RECV):
        here = plans[a].pick(outs[a], 1 - c if kind == SIB_RECV else c, block)
        pltpu.make_async_remote_copy(
            src_ref=here,
            dst_ref=here,
            send_sem=sem(SIB, a, block),
            recv_sem=sem(kind, a, block),
            device_id=sibling,
            device_id_type=MESH,
        ).wait_recv()

    def sent(kind, a, block):
        copy(kind, a, block, sibling).wait_send()

    def local(a, half):
        return pltpu.make_async_copy(
            ins[a].at[half], plans[a].pick(outs[a], half, f), sem(LOCAL, a, half)
        )

    def send_up(a, block, own=False):
        @pl.when(z < lengthwise - 1)
        def _():
            copy(UP, a, block, (d, f + 4), own).start()

    def send_down(a, block, own=False):
        @pl.when(z > 0)
        def _():
            copy(DOWN, a, block, (d, f - 4), own).start()

    for a in range(count):
        copy(ONE, a, f, (d, partner1), True).start()
        send_up(a, f, True)
        send_down(a, f, True)
        copy(LAST, a, f, (d, partner3), True).start()
    for a in range(count):
        for half in (0, 1):
            local(a, half).start()
    for a in range(count):
        block = partner1
        arrived(a, block)
        send_up(a, block)
        send_down(a, block)
        copy(LAST, a, block, (d, partner3)).start()
        copy(SIB, a, block, sibling).start()

    def across(distance, a):
        for sign in (1,) if distance == 0 else (1, -1):
            at = z - sign * distance

            def take(at=at):
                for flip in (0, 1):
                    block = f + 4 * (at - z) + flip * flip1 + flip3
                    arrived(a, block)
                    copy(SIB, a, block, sibling).start()

            pl.when((at >= 0) & (at < lengthwise))(take)

    for distance in range(1, lengthwise):
        for a in range(count):
            for sign in (1, -1):
                at = z - sign * distance

                def take(at=at, sign=sign):
                    for flip in (0, 1):
                        block = f + 4 * (at - z) + flip * flip1
                        arrived(a, block)
                        (send_up if sign == 1 else send_down)(a, block)
                        copy(LAST, a, block, (d, partner3)).start()
                        copy(SIB, a, block, sibling).start()

                pl.when((at >= 0) & (at < lengthwise))(take)
        for a in range(count):
            across(distance - 1, a)
    for a in range(count):
        across(lengthwise - 1, a)

    for a in range(count):

        def finish(block, _, a=a):
            at = block // 4
            mine = block == f
            bit_x, bit_y = lax.rem(block, 2), lax.rem(block // 2, 2)
            in_plane = bit_y + c * (bit_x - bit_y) == last

            @pl.when(jnp.logical_not(mine))
            def _():
                arrived(a, block, SIB_RECV)
                sent(SIB, a, block)

            @pl.when(in_plane)
            def _():
                sent(LAST, a, block)

                @pl.when((at <= z) & (z < lengthwise - 1))
                def _():
                    sent(UP, a, block)

                @pl.when((at >= z) & (z > 0))
                def _():
                    sent(DOWN, a, block)

            return 0

        lax.fori_loop(0, n, finish, 0)
        sent(ONE, a, f)
        for half in (0, 1):
            local(a, half).wait()


def gather(plans, shards, collective_id):
    n = plans[0].fsdp
    count = len(plans)
    return pl.pallas_call(
        functools.partial(gather_kernel, plans),
        out_shape=[jax.ShapeDtypeStruct(plan.shape, BF) for plan in plans],
        in_specs=[pl.BlockSpec(memory_space=pl.ANY)] * count,
        out_specs=[pl.BlockSpec(memory_space=pl.ANY)] * count,
        scratch_shapes=[pltpu.SemaphoreType.DMA((8 * count * n,))],
        compiler_params=pltpu.CompilerParams(collective_id=collective_id, has_side_effects=True),
    )(*shards)


def reduce_kernel(plans, *refs):
    count = len(plans)
    ins, outs = refs[:count], refs[count : 2 * count]
    scratch = refs[2 * count :]
    held, landed, flow_up, flow_down, near, cross = (
        scratch[k * count : (k + 1) * count] for k in range(6)
    )
    sems = scratch[6 * count]
    n, dp = plans[0].fsdp, plans[0].dp
    lengthwise = n // 4
    d, f, c, z, first, last, stride1, stride3 = place(n, dp)
    partner1 = f + stride1 * (1 - 2 * first)
    partner3 = f + stride3 * (1 - 2 * last)
    sibling = (d + 1 - 2 * c, f)
    SIB, SIB_RECV, LOAD, NEAR, NEAR_RECV, UP, UP_RECV, DOWN, DOWN_RECV, END = range(10)

    def sem(kind, a, block):
        return sems.at[(kind * count + a) * n + block]

    def slot(at, b1, b3):
        return 4 * at + stride1 * b1 + stride3 * b3

    def order(step):
        half = step // 2
        return jnp.where(lax.rem(step, 2) == 0, half, lengthwise - 1 - half)

    barrier = pltpu.get_barrier_semaphore()
    for target in ((d, partner1), (d, partner3), sibling):
        pl.semaphore_signal(barrier, inc=1, device_id=target, device_id_type=MESH)

    @pl.when(z > 0)
    def _():
        pl.semaphore_signal(barrier, inc=1, device_id=(d, f - 4), device_id_type=MESH)

    @pl.when(z < lengthwise - 1)
    def _():
        pl.semaphore_signal(barrier, inc=1, device_id=(d, f + 4), device_id_type=MESH)

    has_down = (z > 0).astype(jnp.int32)
    has_up = (z < lengthwise - 1).astype(jnp.int32)
    pl.semaphore_wait(barrier, 3 + has_down + has_up)

    def remote(src, dst, send, recv, target):
        return pltpu.make_async_remote_copy(
            src_ref=src,
            dst_ref=dst,
            send_sem=send,
            recv_sem=recv,
            device_id=target,
            device_id_type=MESH,
        )

    def to_sibling(a, block):
        return remote(
            plans[a].pick(ins[a], 1 - c, block),
            landed[a].at[block],
            sem(SIB, a, block),
            sem(SIB_RECV, a, block),
            sibling,
        )

    def load(a, block):
        return pltpu.make_async_copy(
            plans[a].pick(ins[a], c, block), held[a].at[block], sem(LOAD, a, block)
        )

    def to_near(a, at, b3):
        return remote(
            held[a].at[slot(at, 1 - first, b3)],
            near[a].at[2 * at + b3],
            sem(NEAR, a, 2 * at + b3),
            sem(NEAR_RECV, a, 2 * at + b3),
            (d, partner1),
        )

    def to_up(a, at, b3):
        return remote(
            held[a].at[slot(at, first, b3)],
            flow_up[a].at[2 * at + b3],
            sem(UP, a, 2 * at + b3),
            sem(UP_RECV, a, 2 * at + b3),
            (d, f + 4),
        )

    def to_down(a, at, b3):
        return remote(
            held[a].at[slot(at, first, b3)],
            flow_down[a].at[2 * at + b3],
            sem(DOWN, a, 2 * at + b3),
            sem(DOWN_RECV, a, 2 * at + b3),
            (d, f - 4),
        )

    def to_cross(a):
        return remote(
            held[a].at[slot(z, first, 1 - last)],
            cross[a],
            sem(END, a, 0),
            sem(END, a, 1),
            (d, partner3),
        )

    def to_pair(a):
        return remote(outs[a].at[c], outs[a].at[c], sem(END, a, 2), sem(END, a, 3), sibling)

    def add_into(a, block, source, at):
        def rows(step, _):
            where = pl.ds(pl.multiple_of(step * 16, 16), 16)
            held[a][block, where, :] = (
                held[a][block, where, :].astype(F32) + source[at, where, :].astype(F32)
            ).astype(BF)
            return 0

        lax.fori_loop(0, plans[a].block[0] // 16, rows, 0)

    def each(body):
        for a in range(count):

            def step(t, _, a=a):
                body(a, order(t // 2), lax.rem(t, 2))
                return 0

            lax.fori_loop(0, 2 * lengthwise, step, 0)

    def begin(b1):
        def body(a, at, b3):
            block = slot(at, b1, b3)
            load(a, block).start()

        return body

    def begin_sibling(b1):
        def body(a, at, b3):
            to_sibling(a, slot(at, b1, b3)).start()

        return body

    each(begin_sibling(1 - first))
    each(begin(1 - first))
    each(begin_sibling(first))
    each(begin(first))

    def first_leg(a, at, b3):
        block = slot(at, 1 - first, b3)
        load(a, block).wait()
        to_sibling(a, block).wait_recv()
        add_into(a, block, landed[a], block)
        to_near(a, at, b3).start()

    def middle_leg(a, at, b3):
        block = slot(at, first, b3)
        load(a, block).wait()
        to_sibling(a, block).wait_recv()
        add_into(a, block, landed[a], block)
        to_near(a, at, b3).wait_recv()
        add_into(a, block, near[a], 2 * at + b3)

        @pl.when(at > z)
        def _():
            @pl.when(z > 0)
            def _():
                to_up(a, at, b3).wait_recv()
                add_into(a, block, flow_up[a], 2 * at + b3)

            to_up(a, at, b3).start()

        @pl.when(at < z)
        def _():
            @pl.when(z < lengthwise - 1)
            def _():
                to_down(a, at, b3).wait_recv()
                add_into(a, block, flow_down[a], 2 * at + b3)

            to_down(a, at, b3).start()

    def gather_own(a, b3):
        block = slot(z, first, b3)

        @pl.when(z > 0)
        def _():
            to_up(a, z, b3).wait_recv()
            add_into(a, block, flow_up[a], 2 * z + b3)

        @pl.when(z < lengthwise - 1)
        def _():
            to_down(a, z, b3).wait_recv()
            add_into(a, block, flow_down[a], 2 * z + b3)

    each(first_leg)
    each(middle_leg)
    for a in range(count):
        gather_own(a, 1 - last)
        to_cross(a).start()
    for a in range(count):
        gather_own(a, last)
        to_cross(a).wait_recv()
        block = slot(z, first, last)

        def rows(step, _, a=a, block=block):
            where = pl.ds(pl.multiple_of(step * 16, 16), 16)
            total = held[a][block, where, :].astype(F32) + cross[a][where, :].astype(F32)
            if plans[a].by_rows:
                outs[a][where, :] = total
            else:
                outs[a][c, where, :] = total
            return 0

        lax.fori_loop(0, plans[a].block[0] // 16, rows, 0)
        if not plans[a].by_rows:
            to_pair(a).start()

    def finish(a, at, b3):
        for b1 in (first, 1 - first):
            to_sibling(a, slot(at, b1, b3)).wait_send()
        to_near(a, at, b3).wait_send()

        @pl.when(at > z)
        def _():
            to_up(a, at, b3).wait_send()

        @pl.when(at < z)
        def _():
            to_down(a, at, b3).wait_send()

    each(finish)
    for a in range(count):
        to_cross(a).wait_send()
        if not plans[a].by_rows:
            to_pair(a).wait()


def reduce_scatter(plans, grads, collective_id):
    n = plans[0].fsdp
    count = len(plans)
    return pl.pallas_call(
        functools.partial(reduce_kernel, plans),
        out_shape=[
            jax.ShapeDtypeStruct(plan.block if plan.by_rows else (2,) + plan.block, F32)
            for plan in plans
        ],
        in_specs=[pl.BlockSpec(memory_space=pl.ANY)] * count,
        out_specs=[pl.BlockSpec(memory_space=pltpu.VMEM)] * count,
        scratch_shapes=[pltpu.VMEM((n,) + plan.block, BF) for plan in plans] * 2
        + [pltpu.VMEM((n // 2,) + plan.block, BF) for plan in plans] * 3
        + [pltpu.VMEM(plan.block, BF) for plan in plans]
        + [pltpu.SemaphoreType.DMA((10 * count * n,))],
        compiler_params=pltpu.CompilerParams(
            collective_id=collective_id, has_side_effects=True, vmem_limit_bytes=60 * 2**20
        ),
    )(*grads)


def hot_rows(index_ref):
    index = index_ref[...]
    lane = lax.broadcasted_iota(jnp.int32, (index.shape[0], HOT), 1)
    hit = lane == index[:, 0:1]
    for q in range(1, KMAX + 1):
        hit = jnp.logical_or(hit, lane == index[:, q : q + 1])
    return hit.astype(F32).astype(BF)


def conv_forward_kernel(filters, index_ref, length_ref, table_ref, kernel_ref, width_ref, out_ref):
    words = length_ref.shape[0]
    windows = dot(hot_rows(index_ref), table_ref[...]).astype(BF)
    chunk = 384
    for at in range(0, kernel_ref.shape[1], chunk):
        columns = slice(at, at + chunk)
        activated = jnp.tanh(dot(windows, kernel_ref[:, columns])).reshape(words, SLOTS, chunk)
        counts = jnp.maximum(length_ref[...] - width_ref[:, columns] + 1, 1)
        position = lax.broadcasted_iota(jnp.int32, (words, SLOTS, chunk), 1)
        inside = position < counts[:, None, :]
        totals = jnp.sum(jnp.where(inside, jnp.exp(activated), 0.0), axis=1)
        pooled = jnp.log(totals) - jnp.log(counts.astype(F32))
        lane = at + lax.broadcasted_iota(jnp.int32, (words, chunk), 1)
        out_ref[:, columns] = jnp.where(
            lane < filters, pooled, jnp.where(lane == filters, 1.0, 0.0)
        ).astype(BF)


def conv_backward_kernel(
    index_ref, length_ref, table_ref, kernel_ref, width_ref, grad_ref, kernel_grad_ref, hot_grad_ref
):
    words = length_ref.shape[0]

    @pl.when(pl.program_id(0) == 0)
    def _():
        kernel_grad_ref[...] = jnp.zeros_like(kernel_grad_ref)
        hot_grad_ref[...] = jnp.zeros_like(hot_grad_ref)

    hot = hot_rows(index_ref)
    windows = dot(hot, table_ref[...]).astype(BF)
    chunk = 384
    grad_windows = jnp.zeros(windows.shape, F32)
    for at in range(0, kernel_ref.shape[1], chunk):
        columns = slice(at, at + chunk)
        activated = jnp.tanh(dot(windows, kernel_ref[:, columns])).reshape(words, SLOTS, chunk)
        counts = jnp.maximum(length_ref[...] - width_ref[:, columns] + 1, 1)
        position = lax.broadcasted_iota(jnp.int32, (words, SLOTS, chunk), 1)
        inside = position < counts[:, None, :]
        weight = jnp.where(inside, jnp.exp(activated), 0.0)
        share = grad_ref[:, columns] / jnp.sum(weight, axis=1)
        grad = (share[:, None, :] * weight * (1.0 - activated * activated)).astype(BF)
        grad = grad.reshape(words * SLOTS, chunk)
        kernel_grad_ref[:, columns] += dot_rows(windows, grad)
        grad_windows += dot_cols(grad, kernel_ref[:, columns])
    hot_grad_ref[...] += dot_rows(hot, grad_windows.astype(BF))


def conv_specs(words, filters_padded):
    return [
        pl.BlockSpec((words * SLOTS, 8), lambda i: (i, 0)),
        pl.BlockSpec((words, 1), lambda i: (i, 0)),
        pl.BlockSpec((HOT, LANE), lambda i: (0, 0)),
        pl.BlockSpec((LANE, filters_padded), lambda i: (0, 0)),
        pl.BlockSpec((1, filters_padded), lambda i: (0, 0)),
    ]


def gate_parts(sums):
    parts = [sums[:, :HP]]
    for g in range(1, 4):
        begin = g * H // LANE * LANE
        moved = sums[:, begin : begin + HP + LANE]
        parts.append(pltpu.roll(moved, HP + LANE - (g * H - begin), 1)[:, :HP])
    return parts


def join_gates(parts, columns):
    rows = parts[0].shape[0]
    total = None
    for g, part in enumerate(parts):
        begin = g * H // LANE * LANE
        wide = jnp.concatenate([part, jnp.zeros((rows, LANE), F32)], axis=1)
        if g * H - begin:
            wide = pltpu.roll(wide, g * H - begin, 1)
        pieces = [wide]
        if begin:
            pieces = [jnp.zeros((rows, begin), F32)] + pieces
        if columns - begin - HP - LANE > 0:
            pieces = pieces + [jnp.zeros((rows, columns - begin - HP - LANE), F32)]
        placed = jnp.concatenate(pieces, axis=1)[:, :columns]
        total = placed if total is None else total + placed
    return total


def lstm_forward_kernel(
    batch, x_ref, w_ref, h0_ref, c0_ref, keep_ref, *outs
):
    hp_ref, cp_ref, i_ref, f_ref, u_ref, o_ref, t_ref, h_ref = outs
    per_tile = 8 // batch
    row = lax.broadcasted_iota(jnp.int32, (8, HP), 0)
    lane = lax.broadcasted_iota(jnp.int32, (8, HP), 1)

    def tile(step, carried):
        h, c = carried
        rows = pl.ds(pl.multiple_of(step * 8, 8), 8)
        x = x_ref[rows, :]
        keep = keep_ref[rows, :]
        saved = None
        for part in range(per_tile):
            hp, cp = h * keep, c * keep
            sums = x + dot(hp.astype(BF), w_ref[...])
            i, f, u, o = gate_parts(sums)
            i, f, u, o = jax.nn.sigmoid(i), jax.nn.sigmoid(f), jnp.tanh(u), jax.nn.sigmoid(o)
            c = f * cp + i * u
            t = jnp.tanh(c)
            h = (o * t).astype(BF).astype(F32)
            now = (hp, cp, i, f, u, o, t, jnp.where(lane < H, h, jnp.where(lane == H, 1.0, 0.0)))
            if saved is None:
                saved = now
            else:
                saved = tuple(jnp.where(row >= part * batch, b, a) for a, b in zip(saved, now))
            h, c = pltpu.roll(h, batch, 0), pltpu.roll(c, batch, 0)
        for ref, value in zip((hp_ref, cp_ref, i_ref, f_ref, u_ref, o_ref, t_ref, h_ref), saved):
            ref[rows, :] = value
        return h, c

    lax.fori_loop(0, x_ref.shape[0] // 8, tile, (h0_ref[...], c0_ref[...]))


def lstm_backward_kernel(
    batch, dh_ref, w_ref, keep_ref, cp_ref, i_ref, f_ref, u_ref, o_ref, t_ref, dz_ref
):
    per_tile = 8 // batch
    tiles = dh_ref.shape[0] // 8
    row = lax.broadcasted_iota(jnp.int32, (8, dz_ref.shape[1]), 0)
    real = lax.broadcasted_iota(jnp.int32, (8, HP), 1) < H

    def tile(step, carried):
        dh_carry, dc_carry = carried
        rows = pl.ds(pl.multiple_of((tiles - 1 - step) * 8, 8), 8)
        keep = keep_ref[rows, :]
        i, f, u, o, t = (r[rows, :] for r in (i_ref, f_ref, u_ref, o_ref, t_ref))
        soft = dh_ref[rows, :]
        to_c = o * (1.0 - t * t)
        to_i = jnp.where(real, u * i * (1.0 - i), 0.0)
        to_f = jnp.where(real, cp_ref[rows, :] * f * (1.0 - f), 0.0)
        to_u = jnp.where(real, i * (1.0 - u * u), 0.0)
        to_o = jnp.where(real, t * o * (1.0 - o), 0.0)
        back = f * keep
        saved = None
        for part in reversed(range(per_tile)):
            dh = jnp.where(real, soft + dh_carry, 0.0)
            dc = dc_carry + dh * to_c
            dz = join_gates([dc * to_i, dc * to_f, dc * to_u, dh * to_o], dz_ref.shape[1])
            saved = dz if saved is None else jnp.where(row >= (part + 1) * batch, saved, dz)
            dh_carry = dot(dz.astype(BF), w_ref[...]) * keep
            dc_carry = dc * back
            dh_carry, dc_carry = (
                pltpu.roll(dh_carry, 8 - batch, 0),
                pltpu.roll(dc_carry, 8 - batch, 0),
            )
        dz_ref[rows, :] = saved
        return dh_carry, dc_carry

    zero = jnp.zeros((8, HP), F32)
    lax.fori_loop(0, tiles, tile, (zero, zero))


def in_vmem(kernel, out_shapes, *operands):
    return pl.pallas_call(
        kernel,
        out_shape=out_shapes,
        in_specs=[pl.BlockSpec(memory_space=pltpu.VMEM)] * len(operands),
        out_specs=jax.tree.map(lambda _: pl.BlockSpec(memory_space=pltpu.VMEM), out_shapes),
        compiler_params=pltpu.CompilerParams(vmem_limit_bytes=48 * 2**20),
    )(*operands)


def softmax_kernel(
    vocab,
    blocks,
    h_ref,
    h_back_ref,
    w_ref,
    target_ref,
    scale_ref,
    loss_ref,
    grad_h_ref,
    grad_w_ref,
    logits,
    top,
    total,
    picked,
):
    phase, at = pl.program_id(0), pl.program_id(1)
    width = w_ref.shape[-1]
    rows = h_ref.shape[0]
    w = w_ref[...].reshape(-1, width)
    column = at * width + lax.broadcasted_iota(jnp.int32, (rows, width), 1)
    where = pl.ds(pl.multiple_of(at * width, width), width)
    hit = column == target_ref[...]

    @pl.when((phase == 0) & (at == 0))
    def _():
        top[...] = jnp.full_like(top, -1e30)
        total[...] = jnp.zeros_like(total)
        picked[...] = jnp.zeros_like(picked)

    @pl.when(phase == 0)
    def _():
        now = jnp.where(column < vocab, dot(h_ref[...], w), -1e30)
        logits[:, where] = now
        before = top[...]
        after = jnp.maximum(before, jnp.max(now, axis=1, keepdims=True))
        total[...] = total[...] * jnp.exp(before - after) + jnp.sum(
            jnp.exp(now - after), axis=1, keepdims=True
        )
        top[...] = after
        picked[...] += jnp.sum(jnp.where(hit, now, 0.0), axis=1, keepdims=True)

    @pl.when((phase == 1) & (at == 0))
    def _():
        log_total = top[...] + jnp.log(total[...])
        loss_ref[...] = log_total - picked[...]
        top[...] = log_total
        grad_h_ref[...] = jnp.zeros_like(grad_h_ref)

    @pl.when(phase == 1)
    def _():
        share = jnp.exp(logits[:, where] - top[...])
        grad = ((share - hit.astype(F32)) * scale_ref[...]).astype(BF)
        grad_w_ref[...] = dot_rows(h_back_ref[...], grad).astype(BF).reshape(grad_w_ref.shape)
        grad_h_ref[...] += dot_cols(grad, w)


def word_softmax(plan, h, h_back, weights, target, scale):
    rows, depth = h.shape
    n = plan.fsdp
    per_slot, half = plan.block
    width = 512
    while half % width:
        width -= LANE
    per_half = half // width
    whole = lambda p, j: (0, 0)
    return pl.pallas_call(
        functools.partial(softmax_kernel, plan.width, 2 * per_half),
        out_shape=[
            jax.ShapeDtypeStruct((rows, 1), F32),
            jax.ShapeDtypeStruct((rows, depth), F32),
            jax.ShapeDtypeStruct(plan.shape, BF),
        ],
        grid=(2, 2 * per_half),
        in_specs=[
            pl.BlockSpec((rows, depth), whole),
            pl.BlockSpec((rows, depth), whole),
            pl.BlockSpec(
                (n, 1, per_slot, width), lambda p, j: (0, j // per_half, 0, j % per_half)
            ),
            pl.BlockSpec((rows, 1), whole),
            pl.BlockSpec((rows, 1), whole),
        ],
        out_specs=[
            pl.BlockSpec((rows, 1), whole),
            pl.BlockSpec((rows, depth), whole),
            pl.BlockSpec(
                (1, n, per_slot, width),
                lambda p, j: (p * (j // per_half), 0, 0, p * (j % per_half)),
            ),
        ],
        scratch_shapes=[
            pltpu.VMEM((rows, 2 * half), F32),
            pltpu.VMEM((rows, 1), F32),
            pltpu.VMEM((rows, 1), F32),
            pltpu.VMEM((rows, 1), F32),
        ],
        compiler_params=pltpu.CompilerParams(vmem_limit_bytes=48 * 2**20),
    )(h, h_back, weights, target, scale)


def shards(
    fsdp_count,
    dp_count,
    chars,
    lengths,
    targets,
    resets,
    init_state,
    window_grad,
    char_table,
    conv_weight,
    conv_bias,
    highway_flat,
    lstm_flat,
    soft_flat,
):
    micro_count, streams, step_count, letters = chars.shape
    char_count, embed_dim = char_table.shape
    filters = conv_weight.shape[1]
    batch = micro_count * streams
    words = step_count * batch
    rows = up_to(words, 16)
    fp = up_to(filters + 1, LANE)
    dp_at, fsdp_at = lax.axis_index("dp"), lax.axis_index("fsdp")
    highway = Windows(
        highway_flat.shape[0] * fsdp_count, filters, 4 * (filters + 1), fsdp_count, dp_count, True
    )
    lstm_used = filters + H + 1
    lstm = Windows(
        lstm_flat.shape[0] * fsdp_count, 4 * H, lstm_used, fsdp_count, dp_count, False
    )
    soft = Windows(soft_flat.shape[0] * fsdp_count, V, H + 1, fsdp_count, dp_count, False)

    soft_own = soft.from_flat(soft_flat, fsdp_at)
    soft_all = lax.all_gather(soft_own, "fsdp", axis=0)
    highway_all, lstm_all = gather(
        [highway, lstm],
        [highway.from_flat(highway_flat, fsdp_at), lstm.from_flat(lstm_flat, fsdp_at)],
        1,
    )
    highway_all = highway_all.reshape(-1, highway.columns)
    lstm_all = lstm_all.reshape(2, -1, lstm.columns // 2)

    def by_step(array):
        return jnp.moveaxis(array.reshape((batch, step_count) + array.shape[3:]), 1, 0).reshape(
            (words,) + array.shape[3:]
        )

    def pad_rows(array, value=0):
        return jnp.pad(
            array,
            [(0, rows - words)] + [(0, 0)] * (array.ndim - 1),
            constant_values=value,
        )

    word_chars = pad_rows(by_step(chars))
    word_lengths = pad_rows(by_step(lengths))[:, None]
    position = jnp.arange(letters, dtype=jnp.int32)[None, :]
    codes = jnp.where(position < word_lengths, word_chars, -1)
    codes = jnp.pad(codes, ((0, 0), (0, SLOTS + KMAX - letters)), constant_values=-1)
    index = jnp.stack(
        [
            jnp.where(
                codes[:, q : q + SLOTS] >= 0, codes[:, q : q + SLOTS] + q * char_count, -1
            )
            for q in range(KMAX)
        ]
        + [jnp.full((rows, SLOTS), KMAX * char_count, jnp.int32)],
        axis=2,
    ).reshape(rows * SLOTS, KMAX + 1)
    column = np.arange(fp)
    widths = np.ones((fp,), np.int32)
    for cut_at in FILTER_CUTS:
        widths = widths + ((column >= filters * cut_at // 22) & (column < filters))
    widths = widths.astype(np.int32)
    kernel_mask = jnp.asarray(
        np.arange(KMAX * embed_dim)[:, None] // embed_dim < widths[None, :filters]
    )
    ones_row = KMAX * embed_dim
    kernel = jnp.concatenate(
        [jnp.where(kernel_mask, conv_weight, jnp.zeros_like(conv_weight)), conv_bias[None, :]], axis=0
    )
    kernel = jnp.pad(kernel, ((0, LANE - ones_row - 1), (0, fp - filters)))
    spread_table = jnp.concatenate(
        [
            jnp.pad(char_table, ((0, 0), (q * embed_dim, LANE - (q + 1) * embed_dim)))
            for q in range(KMAX)
        ]
        + [jnp.zeros((1, LANE), BF).at[0, ones_row].set(1.0)],
        axis=0,
    )
    spread_table = jnp.pad(spread_table, ((0, HOT - KMAX * char_count - 1), (0, 0)))
    conv_inputs = (index, word_lengths, spread_table, kernel, jnp.asarray(widths)[None, :])
    word_block = 16
    feature = pl.pallas_call(
        functools.partial(conv_forward_kernel, filters),
        out_shape=jax.ShapeDtypeStruct((rows, fp), BF),
        grid=(rows // word_block,),
        in_specs=conv_specs(word_block, fp),
        out_specs=pl.BlockSpec((word_block, fp), lambda i: (i, 0)),
        compiler_params=pltpu.CompilerParams(vmem_limit_bytes=48 * 2**20),
    )(*conv_inputs)

    filter_lane = jnp.arange(fp)[None, :]
    each_layer = 2 * (filters + 1)
    owner_rows = highway.rows

    def layer_map(row_map, layer):
        at = row_map - layer * each_layer
        inside = (row_map >= 0) & (at >= 0) & (at < each_layer)
        is_gate = inside & (at >= filters + 1)
        source = np.where(inside, np.where(is_gate, at - filters - 1, at), -1)
        return source.astype(np.int32), inside & ~is_gate, is_gate

    layers = []
    for layer in range(2):
        source, is_trans, is_gate = layer_map(highway.gathered, layer)
        live = np.nonzero(source.reshape(-1, owner_rows).max(axis=1) >= 0)[0]
        begin, end = int(live[0]) * owner_rows, (int(live[-1]) + 1) * owner_rows
        begin = begin // 16 * 16
        end = min(up_to(end, 16), source.shape[0])
        weights = highway_all[begin:end]
        mapping = one_hot_map(fp, source[begin:end])
        trans_mask = jnp.asarray(is_trans[begin:end].astype(np.float32))[None, :]
        gate_mask = jnp.asarray(is_gate[begin:end].astype(np.float32))[None, :]
        spread = dot(feature, mapping)
        both = jnp.concatenate([spread * trans_mask, spread * gate_mask], axis=0).astype(BF)
        sums = dot(both, weights)
        trans, gate = sums[:rows], jax.nn.sigmoid(sums[rows:])
        layers.append((feature, trans, gate, weights, mapping, trans_mask, gate_mask))
        value = gate * jax.nn.silu(trans) + (1.0 - gate) * feature.astype(F32)
        feature = jnp.where(
            filter_lane < filters, value, jnp.where(filter_lane == filters, 1.0, 0.0)
        ).astype(BF)

    lp = up_to(lstm_used, LANE)
    first_h = np.nonzero(lstm.gathered >= filters)[0][0] // 16 * 16
    last_x = min(up_to(int(np.nonzero((lstm.gathered >= 0) & (lstm.gathered < filters))[0][-1]) + 1, 16), lstm.gathered.shape[0])
    lstm_map = one_hot_map(lp, lstm.gathered)
    no_hidden = jnp.concatenate(
        [
            feature[:, :filters],
            jnp.zeros((rows, H), BF),
            jnp.ones((rows, 1), BF),
            jnp.zeros((rows, lp - lstm_used), BF),
        ],
        axis=1,
    )
    spread_x = dot(no_hidden, lstm_map).astype(BF)
    from_input = jnp.concatenate([dot(spread_x, lstm_all[0]), dot(spread_x, lstm_all[1])], axis=1)
    hidden_source = lstm.gathered[first_h:] - filters
    hidden_map = one_hot_map(HP, np.where((hidden_source >= 0) & (hidden_source < H), hidden_source, -1))
    recur = jnp.concatenate(
        [dot(hidden_map, lstm_all[h, first_h:]).astype(BF) for h in range(2)], axis=1
    )
    recur_t = jnp.concatenate(
        [
            lax.dot_general(
                lstm_all[h, first_h:],
                hidden_map,
                (((0,), (1,)), ((), ())),
                preferred_element_type=F32,
            ).astype(BF)
            for h in range(2)
        ],
        axis=0,
    )
    keep = pad_rows(by_step(1 - resets).astype(F32))[:, None]
    start = init_state.reshape(batch, 2, H)
    start = jnp.pad(start, ((0, 8 - batch), (0, 0), (0, HP - H)))
    states = [jax.ShapeDtypeStruct((rows, HP), F32)] * 8
    hp, cp, gate_i, gate_f, gate_u, gate_o, tanh_c, hidden = in_vmem(
        functools.partial(lstm_forward_kernel, batch),
        states,
        from_input,
        recur,
        start[:, 0].astype(BF).astype(F32),
        start[:, 1],
        keep,
    )

    hidden = hidden.astype(BF)
    soft_map = one_hot_map(HP, soft.gathered)
    spread_h = dot(hidden, soft_map).astype(BF)
    spread_h_back = dot(hidden, one_hot_map(HP, soft.reduced)).astype(BF)
    row_scale = jnp.broadcast_to(
        window_grad.reshape(1, batch) / step_count, (step_count, batch)
    ).reshape(words, 1)
    word_loss, grad_spread, soft_grad = word_softmax(
        soft,
        spread_h,
        spread_h_back,
        soft_all,
        pad_rows(by_step(targets), -1)[:, None],
        pad_rows(row_scale),
    )
    window_loss = jnp.mean(word_loss[:words, 0].reshape(step_count, batch), axis=0).reshape(
        micro_count, streams
    )
    grad_hidden = compress(grad_spread, soft_map)
    soft_part = reduce_scatter([soft], [soft_grad], 2)[0]

    dz = in_vmem(
        functools.partial(lstm_backward_kernel, batch),
        jax.ShapeDtypeStruct((rows, lstm.columns), F32),
        grad_hidden,
        recur_t,
        keep,
        cp,
        gate_i,
        gate_f,
        gate_u,
        gate_o,
        tanh_c,
    ).astype(BF)
    half = lstm.columns // 2
    lstm_in = jnp.concatenate(
        [
            feature[:, :filters],
            hp[:, :H].astype(BF),
            jnp.ones((rows, 1), BF),
            jnp.zeros((rows, lp - lstm_used), BF),
        ],
        axis=1,
    )
    lstm_in = dot(lstm_in, one_hot_map(lp, lstm.reduced)).astype(BF)
    lstm_grad = jnp.stack(
        [dot_rows(lstm_in, dz[:, h * half : (h + 1) * half]).astype(BF) for h in range(2)]
    ).reshape(lstm.shape)
    grad_spread = dot_cols(dz[:, :half], lstm_all[0, :last_x]) + dot_cols(
        dz[:, half:], lstm_all[1, :last_x]
    )
    input_source = lstm.gathered[:last_x]
    grad = compress(
        grad_spread, one_hot_map(fp, np.where(input_source < filters, input_source, -1))
    )

    grads_of, inputs_of = [], []
    for layer in (1, 0):
        layer_in, trans, gate, weights, mapping, trans_mask, gate_mask = layers[layer]
        sig = jax.nn.sigmoid(trans)
        silu = trans * sig
        grad = jnp.where(filter_lane < filters, grad, 0.0)
        grad_trans = (grad * gate * sig * (1.0 + trans * (1.0 - sig))).astype(BF)
        grad_gate = (grad * (silu - layer_in.astype(F32)) * gate * (1.0 - gate)).astype(BF)
        pair = jnp.concatenate([grad_trans, grad_gate], axis=0)
        spread = dot_cols(pair, weights)
        grad = grad * (1.0 - gate) + compress(
            spread[:rows] * trans_mask + spread[rows:] * gate_mask, mapping
        )
        source, is_trans, is_gate = layer_map(highway.reduced, layer)
        spread_in = dot(layer_in, one_hot_map(fp, source))
        inputs_of = [
            (spread_in * jnp.asarray(is_trans.astype(np.float32))[None, :]).astype(BF),
            (spread_in * jnp.asarray(is_gate.astype(np.float32))[None, :]).astype(BF),
        ] + inputs_of
        grads_of = [pair] + grads_of
    highway_grad = (
        dot_rows(jnp.concatenate(inputs_of, axis=0), jnp.concatenate(grads_of, axis=0))
        .astype(BF)
        .reshape(highway.shape)
    )

    grad = jnp.where(filter_lane < filters, grad, 0.0)
    kernel_grad, hot_grad = pl.pallas_call(
        conv_backward_kernel,
        out_shape=[
            jax.ShapeDtypeStruct((LANE, fp), F32),
            jax.ShapeDtypeStruct((HOT, LANE), F32),
        ],
        grid=(rows // word_block,),
        in_specs=conv_specs(word_block, fp) + [pl.BlockSpec((word_block, fp), lambda i: (i, 0))],
        out_specs=[
            pl.BlockSpec((LANE, fp), lambda i: (0, 0)),
            pl.BlockSpec((HOT, LANE), lambda i: (0, 0)),
        ],
        compiler_params=pltpu.CompilerParams(vmem_limit_bytes=48 * 2**20),
    )(*conv_inputs, grad)
    table_grad = sum(
        hot_grad[q * char_count : (q + 1) * char_count, q * embed_dim : (q + 1) * embed_dim]
        for q in range(KMAX)
    )
    kernel_grad, table_grad = lax.psum((kernel_grad, table_grad), ("dp", "fsdp"))
    conv_weight_grad = jnp.where(kernel_mask, kernel_grad[:ones_row, :filters], 0.0)
    conv_bias_grad = kernel_grad[ones_row, :filters]

    highway_part, lstm_part = reduce_scatter([highway, lstm], [highway_grad, lstm_grad], 3)

    def own_window(plan, part):
        if dp_count > 2:
            groups = [list(range(h, dp_count, 2)) for h in range(2)]
            part = lax.psum(part, "dp", axis_index_groups=groups)
        if plan.by_rows:
            at = dp_at // 2
        else:
            part = jnp.concatenate([part[0], part[1]], axis=1)
            at = dp_at
        window = lax.dynamic_slice_in_dim(part, at * plan.rows, plan.rows, 0)
        return plan.to_flat(window, dp_at, fsdp_at)

    return (
        window_loss,
        table_grad,
        conv_weight_grad,
        conv_bias_grad,
        own_window(highway, highway_part),
        own_window(lstm, lstm_part),
        own_window(soft, soft_part),
    )


def solution(mesh):
    in_specs = (
        P(None, ("dp", "fsdp"), None, None),
        P(None, ("dp", "fsdp"), None),
        P(None, ("dp", "fsdp"), None),
        P(None, ("dp", "fsdp"), None),
        P(None, ("dp", "fsdp"), None, None),
        P(None, ("dp", "fsdp")),
        P(),
        P(),
        P(),
        P("fsdp", None),
        P("fsdp", None),
        P("fsdp", None),
    )
    out_specs = (
        P(None, ("dp", "fsdp")),
        P(),
        P(),
        P(),
        P(("dp", "fsdp"), None),
        P(("dp", "fsdp"), None),
        P(("dp", "fsdp"), None),
    )
    return jax.shard_map(
        functools.partial(shards, mesh.shape["fsdp"], mesh.shape["dp"]),
        mesh=mesh,
        in_specs=in_specs,
        out_specs=out_specs,
        check_vma=False,
    )
```

time: 3050 us -> 971 us (0.32); the launches traced: 3000 us -> 961 us
  blocking collectives: 1050 us -> 65.2 us
  local copies, waits for them, and re-layouts: 990 us -> 77.7 us
  Pallas kernels: 0 us -> 593 us
  other arithmetic: 489 us -> 28.3 us
  matrix products: 365 us -> 100 us
    unnamed x1 -> x0, blocking collectives: 1010 us -> none
    pallas_call x0 -> x8, Pallas kernels: none -> 593 us  [the longest x1 227 us: gather(): pl.pallas_call(functools.partial(gather_kernel, plans), out_shape=[jax.Sh...]
    concatenate x160 -> x3, local copies, waits for them, and re-layouts: 339 us -> 4.62 us  [the longest x1 2.35 us: shards(): jnp.concatenate([feature[:, :filters], hp[:, :H].astype(BF), jnp.ones((ro...]
    dot_general x186 -> x27, matrix products: 365 us -> 100 us  [the longest x14 49 us: dot(): return jnp.dot(left, right, preferred_element_type=F32)]
    reshape x29 -> x19, local copies, waits for them, and re-layouts: 233 us -> 13 us  [the longest x3 5.64 us: to_flat(): flat = window[:, :self.width].reshape(-1)]
    dynamic_update_slice x280 -> x0, other arithmetic: 191 us -> none  [lstm_run(): lax.scan(lstm_step, start_state, (jnp.swapaxes(from_input, 0, 1), keep_al...]
    dynamic_slice x140 -> x0, local copies, waits for them, and re-layouts: 122 us -> none  [the longest x70 65.5 us: lstm_run(): lax.scan(lstm_step, start_state, (jnp.swapaxes(from_input, 0, 1), keep_al...]
    mul x70 -> x0, other arithmetic: 99.2 us -> none  [back_step(): grad_c * gate_forget * keep_col]
  transfers between devices with their start and end apart: 7 -> 2, of which waited for: 1 -> 1; matrix products, arithmetic and copies ran while one was open for 71% -> 11% of each run, Pallas kernels for 0% -> 28%
where the time goes in v1:
time: 971 us; the launch traced here: 961 us
  Pallas kernels  593 us (61%)
  matrix products  100 us (10%)
  waiting for transfers between devices  80.7 us (8%)
  local copies, waits for them, and re-layouts  77.7 us (8%)
  blocking collectives  65.2 us (7%)
  other arithmetic  28.3 us (3%)
  between operations  16.5 us (2%)
    pallas_call x1, Pallas kernels, gather(): pl.pallas_call(functools.partial(gather_kernel, plans), out_shape=[jax.Sh...  227 us
    pallas_call x2, Pallas kernels, reduce_scatter(): pl.pallas_call(functools.partial(reduce_kernel, plans), out_shape=[jax.Sh...  219 us
    psum x1, waiting for transfers between devices, shards(): lax.psum((kernel_grad, table_grad), ('dp', 'fsdp'))  80.6 us
    psum x1, blocking collectives, shards(): lax.psum((kernel_grad, table_grad), ('dp', 'fsdp'))  65.2 us
    pallas_call x2, Pallas kernels, in_vmem(): pl.pallas_call(kernel, out_shape=out_shapes, in_specs=[pl.BlockSpec(memor...  61.2 us
    dot_general x14, matrix products, dot(): return jnp.dot(left, right, preferred_element_type=F32)  49 us
    pallas_call x1, Pallas kernels, word_softmax(): pl.pallas_call(functools.partial(softmax_kernel, plan.width, 2 * per_half...  44 us
    pallas_call x1, Pallas kernels, shards(): pl.pallas_call(conv_backward_kernel, out_shape=[jax.ShapeDtypeStruct((LAN...  26.4 us
  transfers between devices with their start and end apart: 2, of which 1 were waited for; matrix products, arithmetic and copies ran while one was open for 11% of the time, Pallas kernels for 28%

profile of v1, /device:TPU:0, one launch (start us, length us, event | category | flops | bytes accessed | tf_op | source)
XLA Modules:
  0.0 961.3 jit_solution(7358574102570578689)
XLA Ops:
  8.5 3.8 dynamic_update_slice.23
  13.1 3.8 dynamic_update_slice.22
  19.1 2.7 dynamic_update_slice.21
  22.3 2.7 dynamic_update_slice.20
  25.6 2.9 dynamic_update_slice.19
  29.2 2.9 dynamic_update_slice.18
  34.6 227.2 %shard_map.352 = (bf16[16,2,144,1152]{3,2,1,0:T(8,128)(2,1)}, bf16[2,16,112,1408]{3,2,1,0:T(8,128)(2,1)}) custom-call(bf16[2,144,1152]{2,1,0:T(8,128)(2,1)} %bitcast.115, bf16[2,112,1408]{2,1,0:T(8,128)(2,1)} %pad_maximum_fusion.5.refs_1_), custom_call_target="tpu_custom_call" | custom-call | tf_op jit(solution)/shard_map/pallas_call | solution.py:281
  261.9 5.3 slice.267
  276.1 14.9 %shard_map.351 = bf16[144,1152]{1,0:T(8,128)(2,1)S(1)} custom-call(s32[3456,8]{1,0:T(8,128)S(1)} %copy.85.index_ref, s32[144,1]{1,0:T(8,128)S(1)} %copy.86.length_ref, bf16[384,128]{1,0:T(8,128)(2,1)S(1)} %pad.98.table_ref, bf16[128,1152]{1,0:T(8,128)(2,1)S(1)} %fusion.128.kernel_ref, s32[1,1152]{1,0:T(1,128)S(1)} %copy-done.14), custom_call_target="tpu_custom_call" | custom-call | tf_op jit(solution)/shard_map/pallas_call | solution.py:915
  291.0 2.5 multiply_convert_fusion.7
  293.5 4.6 fusion.49
  300.0 2.7 multiply_convert_fusion.5
  302.7 2.1 fusion.26
  307.2 3.8 fusion.33
  311.1 8.6 fusion.148
  319.7 3.6 fusion.150
  325.3 3.5 convolution_convert_fusion.5
  328.8 3.5 convolution_convert_fusion.6
  332.3 2.3 pad_maximum_fusion.1.w_ref
  334.6 29.7 %shard_map.353 = (f32[144,768]{1,0:T(8,128)S(1)}, f32[144,768]{1,0:T(8,128)S(1)}, f32[144,768]{1,0:T(8,128)S(1)}, f32[144,768]{1,0:T(8,128)S(1)}, f32[144,768]{1...) custom-call(f32[144,2816]{1,0:T(8,128)S(1)} %pad_maximum_fusion.3.x_ref, ...), custom_call_target="tpu_custom_call" | custom-call | tf_op jit(solution)/shard_map/pallas_call | solution.py:711
  368.8 2.4 concatenate.92
  371.2 2.4 fusion.67.h_back_ref
  373.6 2.3 fusion.68.h_ref
  375.9 4.3 fusion.32
  380.2 3.5 convolution_convert_fusion.3
  383.7 3.5 convolution_convert_fusion.4
  387.3 6.3 multiply_convert_fusion.1
  393.7 6.5 multiply_convert_fusion.3
  400.1 2.3 pad_maximum_fusion.2.w_ref
  406.0 44.0 %shard_map.354 = (f32[144,1]{1,0:T(8,128)S(1)}, f32[144,768]{1,0:T(8,128)S(1)}, bf16[2,16,48,5120]{3,2,1,0:T(8,128)(2,1)}) custom-call(bf16[144,768]{1,0:T(8,128)(2,1)S(1)} %copy-done.11, bf16[144,768]{1,0:T(8,128)(2,1)S(1)} %copy-done.10, bf16[16,2,48,5120]{3,2,1,0:T(8,128)(2,1)} %bitcast.105, s32[144,1]{1,0:T(8,128)S(1)} %copy-done.9, f32[144,1]{1,0:T(8,128)S(1)} %copy-done.8), custom_call_target="tpu_custom_call" | custom-call | tf_op jit(solution)/shard_map/pallas_call | solution.py:786
  451.5 31.6 %shard_map.355 = f32[144,2816]{1,0:T(8,128)S(1)} custom-call(f32[144,768]{1,0:T(8,128)S(1)} %slice_add_fusion.3.dh_ref, bf16[2816,768]{1,0:T(8,128)(2,1)} %pad_maximum_fusion.2.w_ref, f32[144,1]{1,0:T(8,128)S(1)} %copy.89.keep_ref, f32[144,768]{1,0:T(8,128)S(1)} %get-tuple-element.41.cp_ref, f32[144,768]{1,0:T(8,128)S(1)} %get-tuple-element.42.i_ref, ...), custom_call_target="tpu_custom_call" | custom-call | tf_op jit(solution)/shard_map/pallas_call | solution.py:711
  484.1 4.0 convolution_convert_fusion.2
  488.1 3.9 convolution_convert_fusion.1
  492.0 3.8 fusion.28
  495.8 93.6 %shard_map.358 = f32[2,48,5120]{2,1,0:T(8,128)} custom-call(bf16[2,16,48,5120]{3,2,1,0:T(8,128)(2,1)} %get-tuple-element.52.refs_0_), custom_call_target="tpu_custom_call" | custom-call | tf_op jit(solution)/shard_map/pallas_call | solution.py:525
  592.0 2.9 reshape.236
  594.9 3.3 reduce-precision_convert_fusion.2
  601.6 4.8 fusion.24
  607.1 2.5 fusion.4
  612.1 8.7 pad_maximum_fusion.refs_1_
  620.9 6.4 fusion.107
  627.4 11.4 %convolution_convert_fusion = bf16[4608,1152]{1,0:T(8,128)(2,1)} fusion(bf16[144,4608]{1,0:T(8,128)(2,1)S(1)} %copy-done.75, bf16[144,4608]{1,0:T(8,128)(2,1)S(1)} %copy-done.74, bf16[144,4608]{1,0:T(8,128)(2,1)S(1)} %copy-done.77, bf16[144,4608]{1,0:T(8,128)(2,1)S(1)} %copy-done.76, bf16[144,1152]{1,0:T(8,128)(2,1)S(1)} %copy-done.40, ...), kind=kOutput, calls=%fused_computation.4 | convolution fusion | flops 6147145728 | bytes 17252352 | tf_op jit(solution)/shard_map/dot_general | solution.py:33
  638.8 125.6 %shard_map.357 = (f32[144,1152]{1,0:T(8,128)}, f32[2,112,1408]{2,1,0:T(8,128)}) custom-call(bf16[16,2,144,1152]{3,2,1,0:T(8,128)(2,1)} %bitcast.106, bf16[2,16,112,1408]{3,2,1,0:T(8,128)(2,1)} %pad_maximum_fusion.refs_1_), custom_call_target="tpu_custom_call" | custom-call | tf_op jit(solution)/shard_map/pallas_call | solution.py:525
  766.7 2.3 reshape.234
  771.0 2.0 fusion.8
  773.3 26.4 %shard_map.356 = (f32[128,1152]{1,0:T(8,128)}, f32[384,128]{1,0:T(8,128)S(1)}) custom-call(s32[3456,8]{1,0:T(8,128)S(1)} %copy.85.index_ref, s32[144,1]{1,0:T(8,128)S(1)} %copy.86.length_ref, bf16[384,128]{1,0:T(8,128)(2,1)S(1)} %pad.98.table_ref, bf16[128,1152]{1,0:T(8,128)(2,1)S(1)} %fusion.128.kernel_ref, s32[1,1152]{1,0:T(1,128)S(1)} %copy-done.14, ...), custom_call_target="tpu_custom_call" | custom-call | tf_op jit(solution)/shard_map/pallas_call | solution.py:1085
  802.8 65.2 %psum.14 = f32[51,15]{1,0:T(8,128)S(1)} all-reduce(f32[51,15]{1,0:T(8,128)S(1)} %slice_add_fusion.4), channel_id=1, replica_groups=mesh['dp'=2,'fsdp'=16] {'dp','fsdp'}, use_global_device_ids=true, to_apply=%region_2.3 | all-reduce | flops 765 | bytes 6120 | tf_op jit(solution)/shard_map/psum | solution.py:1103
  870.4 80.6 %all-reduce.24.cloned.1.call-done = f32[128,1152]{1,0:T(8,128)} async-done(((f32[128,1152]{1,0:T(8,128)}), f32[128,1152]{1,0:T(8,128)}) %all-reduce.24.cloned.1.call-update) | async-done | bytes 589840 | tf_op jit(solution)/shard_map/psum | solution.py:1103
  (279 shorter events, 55.5 us)
Async XLA Ops:
  7.2 395.2 %all-gather.3.cloned.1.call-start = ((), (), s32[]{:S(2)}) async-start(), calls=%async_computation.1 | async-start | bytes 16711680 | tf_op jit(solution)/shard_map/all_gather | solution.py:855
  18.8 6.6 copy-start.30
  18.9 932.2 %all-reduce.24.cloned.1.call-start = ((), (), s32[]{:S(2)}) async-start(), calls=%async_computation | async-start | bytes 1179648 | tf_op jit(solution)/shard_map/psum | solution.py:1103
  261.9 5.3 copy-start.56
  261.9 5.5 copy-start.44
  267.2 3.5 copy-start.45
  267.2 3.6 copy-start.58
  267.2 4.4 copy-start.57
  267.6 8.3 copy-start.32
  267.6 8.3 copy-start.43
  268.5 7.5 copy-start.14
  270.7 20.2 %copy-start.46 = (f32[2304]{0:T(1024)S(1)}, f32[2304]{0:T(1024)}, u32[]{:S(2)}) copy-start(f32[2304]{0:T(1024)} %constant.175.clone) | copy-start | bytes 27652
  270.8 20.2 %copy-start.47 = (f32[2304]{0:T(1024)S(1)}, f32[2304]{0:T(1024)}, u32[]{:S(2)}) copy-start(f32[2304]{0:T(1024)} %constant.176.clone) | copy-start | bytes 27652
  270.8 20.2 %copy-start.65 = (s32[2304]{0:T(1024)S(1)}, s32[2304]{0:T(1024)}, u32[]{:S(2)}) copy-start(s32[2304]{0:T(1024)} %constant.174.clone) | copy-start | bytes 27652
  291.0 11.7 %slice-start = ((s8[10616832]{0:T(1024)(128)(4,1)}), s8[4194304]{0:T(1024)(128)(4,1)S(1)}, s32[]{:S(2)}) async-start(s8[10616832]{0:T(1024)(128)(4,1)} %bitcast.117), calls=%async_computation.2 | async-start | bytes 8388608
  293.5 9.2 slice-start.1
  299.2 3.5 slice-start.2
  305.9 5.2 copy-start.24
  305.9 5.2 copy-start.35
  305.9 5.2 copy-start.36
  319.7 3.9 copy-start.16
  368.1 5.5 copy-start.71
  371.2 4.7 copy-start.34
  375.9 4.3 copy-start.73
  383.7 3.6 copy-start.27
  383.7 3.6 copy-start.62
  383.7 3.6 copy-start.63
  383.7 3.6 copy-start.64
  387.3 6.4 copy-start.59
  387.3 6.4 copy-start.60
  387.3 6.4 copy-start.61
  450.0 33.0 %copy-start.12 = (f32[144,1]{1,0:T(8,128)}, f32[144,1]{1,0:T(8,128)S(1)}, u32[]{:S(2)}) copy-start(f32[144,1]{1,0:T(8,128)S(1)} %get-tuple-element.39) | copy-start | bytes 1732
  594.9 3.3 copy-start.69
  601.6 4.8 copy-start.50
  601.6 4.8 copy-start.52
  620.8 6.5 copy-start.38
  620.8 6.5 copy-start.40
  620.8 6.5 copy-start.41
  620.8 6.5 copy-start.42
  620.8 6.5 copy-start.74
  620.9 6.5 copy-start.75
  620.9 6.5 copy-start.76
  620.9 6.5 copy-start.77
  764.4 4.5 copy-start.48
  766.7 4.3 copy-start.66
  773.2 26.6 %copy-start.13 = (f32[144,1]{1,0:T(8,128)S(1)}, f32[144,1]{1,0:T(8,128)}, u32[]{:S(2)}) copy-start(f32[144,1]{1,0:T(8,128)} %copy-done.12) | copy-start | bytes 1732
  773.3 26.9 %copy-start.23 = (f32[240000]{0:T(1024)S(1)}, f32[240000]{0:T(1024)}, u32[]{:S(2)}) copy-start(f32[240000]{0:T(1024)} %reshape.236) | copy-start | bytes 2880004
  800.1 150.9 %copy-start.33 = (pred[105,1100]{1,0:T(8,128)(4,1)S(1)}, pred[105,1100]{1,0:T(8,128)(4,1)}, u32[]{:S(2)}) copy-start(pred[105,1100]{1,0:T(8,128)(4,1)} %constant.172.clone) | copy-start | bytes 346504
  (35 other events, 47.2 us)
Sparse Core Ops, SparseCore 0:
  19.0 246.2 all-gather.2
  799.9 151.1 all-reduce.23

commit v2 on v1

--- a/solution.py
+++ b/solution.py
@@ -75,6 +75,8 @@
             order = [d * fsdp + f for f in range(fsdp) for d in range(dp)]
         self.reduced = row_map(order)
 
+    dtype = BF
+
     def pick(self, ref, half, slot):
         return ref.at[slot, half] if self.by_rows else ref.at[half, slot]
 
@@ -115,32 +117,10 @@
     return product[:count] + product[count:]
 
 
-def place(fsdp, dp):
-    d, f = lax.axis_index("dp"), lax.axis_index("fsdp")
-    c = lax.rem(d, 2)
-    x, y, z = lax.rem(f, 2), lax.rem(f // 2, 2), f // 4
-    first, last = x + c * (y - x), y + c * (x - y)
-    return d, f, c, z, first, last, 1 + c, 2 - c
-
-
-def gather_kernel(plans, *refs):
-    count = len(plans)
-    ins, outs, sems = refs[:count], refs[count : 2 * count], refs[2 * count]
-    n, dp = plans[0].fsdp, plans[0].dp
-    lengthwise = n // 4
-    d, f, c, z, first, last, stride1, stride3 = place(n, dp)
-    partner1 = f + stride1 * (1 - 2 * first)
-    partner3 = f + stride3 * (1 - 2 * last)
-    sibling = (d + 1 - 2 * c, f)
-    flip1 = stride1 * (1 - 2 * first)
-    flip3 = stride3 * (1 - 2 * last)
-    RECV, SIB_RECV, ONE, UP, DOWN, LAST, SIB, LOCAL = range(8)
-
-    def sem(kind, a, block):
-        return sems.at[(kind * count + a) * n + block]
-
+def greet(place_of, lengthwise):
+    d, f, z = place_of.d, place_of.f, place_of.z
     barrier = pltpu.get_barrier_semaphore()
-    for target in ((d, partner1), (d, partner3), sibling):
+    for target in (place_of.partner1, place_of.partner3, place_of.sibling):
         pl.semaphore_signal(barrier, inc=1, device_id=target, device_id_type=MESH)
 
     @pl.when(z > 0)
@@ -155,393 +135,477 @@
     has_up = (z < lengthwise - 1).astype(jnp.int32)
     pl.semaphore_wait(barrier, 3 + has_down + has_up)
 
-    def copy(kind, a, block, target, own=False):
-        here = plans[a].pick(outs[a], c, block)
-        return pltpu.make_async_remote_copy(
-            src_ref=ins[a].at[c] if own else here,
-            dst_ref=here,
-            send_sem=sem(kind, a, block),
-            recv_sem=sem(SIB_RECV if kind == SIB else RECV, a, block),
-            device_id=target,
-            device_id_type=MESH,
-        )
-
-    def arrived(a, block, kind=RECV):
-        here = plans[a].pick(outs[a], 1 - c if kind == SIB_RECV else c, block)
-        pltpu.make_async_remote_copy(
-            src_ref=here,
-            dst_ref=here,
-            send_sem=sem(SIB, a, block),
-            recv_sem=sem(kind, a, block),
-            device_id=sibling,
-            device_id_type=MESH,
+
+class Place:
+    def __init__(self):
+        self.d, self.f = lax.axis_index("dp"), lax.axis_index("fsdp")
+        self.c = lax.rem(self.d, 2)
+        x, y, self.z = lax.rem(self.f, 2), lax.rem(self.f // 2, 2), self.f // 4
+        self.first = x + self.c * (y - x)
+        self.last = y + self.c * (x - y)
+        self.stride1, self.stride3 = 1 + self.c, 2 - self.c
+        self.flip1 = self.stride1 * (1 - 2 * self.first)
+        self.flip3 = self.stride3 * (1 - 2 * self.last)
+        self.partner1 = (self.d, self.f + self.flip1)
+        self.partner3 = (self.d, self.f + self.flip3)
+        self.sibling = (self.d + 1 - 2 * self.c, self.f)
+
+    def last_bit(self, block):
+        bit_x, bit_y = lax.rem(block, 2), lax.rem(block // 2, 2)
+        return bit_y + self.c * (bit_x - bit_y)
+
+
+def remote(src, dst, send, recv, target):
+    return pltpu.make_async_remote_copy(
+        src_ref=src,
+        dst_ref=dst,
+        send_sem=send,
+        recv_sem=recv,
+        device_id=target,
+        device_id_type=MESH,
+    )
+
+
+class Gather:
+    def __init__(self, plans, own, outs, sems, shared):
+        self.plans, self.own, self.outs, self.sems, self.shared = plans, own, outs, sems, shared
+        self.n = plans[0].fsdp
+        self.lengthwise = self.n // 4
+        self.at = Place()
+
+    RECV, SIB_RECV, ONE, UP, DOWN, LAST, SIB, LOCAL = range(8)
+
+    @staticmethod
+    def semaphores(plans):
+        return pltpu.SemaphoreType.DMA((8 * len(plans) * plans[0].fsdp,))
+
+    def sem(self, kind, a, block):
+        return self.sems.at[(kind * len(self.plans) + a) * self.n + block]
+
+    def source(self, a, half):
+        return self.own[a].at[half] if self.shared else self.own[a]
+
+    def copy(self, kind, a, block, target, own=False):
+        here = self.plans[a].pick(self.outs[a], self.at.c, block)
+        return remote(
+            self.source(a, self.at.c) if own else here,
+            here,
+            self.sem(kind, a, block),
+            self.sem(self.SIB_RECV if kind == self.SIB else self.RECV, a, block),
+            target,
+        )
+
+    def arrived(self, a, block, kind=RECV):
+        c = self.at.c
+        here = self.plans[a].pick(self.outs[a], 1 - c if kind == self.SIB_RECV else c, block)
+        remote(
+            here, here, self.sem(self.SIB, a, block), self.sem(kind, a, block), self.at.sibling
         ).wait_recv()
 
-    def sent(kind, a, block):
-        copy(kind, a, block, sibling).wait_send()
-
-    def local(a, half):
+    def sent(self, kind, a, block):
+        self.copy(kind, a, block, self.at.sibling).wait_send()
+
+    def local(self, a, half):
         return pltpu.make_async_copy(
-            ins[a].at[half], plans[a].pick(outs[a], half, f), sem(LOCAL, a, half)
-        )
-
-    def send_up(a, block, own=False):
-        @pl.when(z < lengthwise - 1)
+            self.source(a, half),
+            self.plans[a].pick(self.outs[a], half, self.at.f),
+            self.sem(self.LOCAL, a, half if self.shared else 0),
+        )
+
+    def send_up(self, a, block, own=False):
+        @pl.when(self.at.z < self.lengthwise - 1)
         def _():
-            copy(UP, a, block, (d, f + 4), own).start()
-
-    def send_down(a, block, own=False):
-        @pl.when(z > 0)
+            self.copy(self.UP, a, block, (self.at.d, self.at.f + 4), own).start()
+
+    def send_down(self, a, block, own=False):
+        @pl.when(self.at.z > 0)
         def _():
-            copy(DOWN, a, block, (d, f - 4), own).start()
-
+            self.copy(self.DOWN, a, block, (self.at.d, self.at.f - 4), own).start()
+
+    def begin(self, a):
+        at = self.at
+        self.copy(self.ONE, a, at.f, at.partner1, True).start()
+        self.send_up(a, at.f, True)
+        self.send_down(a, at.f, True)
+        self.copy(self.LAST, a, at.f, at.partner3, True).start()
+        if self.shared:
+            for half in (0, 1):
+                self.local(a, half).start()
+        else:
+            self.copy(self.SIB, a, at.f, at.sibling, True).start()
+            self.local(a, at.c).start()
+
+    def near(self, a):
+        at = self.at
+        block = at.f + at.flip1
+        self.arrived(a, block)
+        self.send_up(a, block)
+        self.send_down(a, block)
+        self.copy(self.LAST, a, block, at.partner3).start()
+        self.copy(self.SIB, a, block, at.sibling).start()
+
+    def line(self, a, distance):
+        for sign in (1, -1):
+            z = self.at.z - sign * distance
+
+            def take(sign=sign):
+                for flip in (0, 1):
+                    block = self.at.f - 4 * sign * distance + flip * self.at.flip1
+                    self.arrived(a, block)
+                    (self.send_up if sign == 1 else self.send_down)(a, block)
+                    self.copy(self.LAST, a, block, self.at.partner3).start()
+                    self.copy(self.SIB, a, block, self.at.sibling).start()
+
+            pl.when((z >= 0) & (z < self.lengthwise))(take)
+
+    def across(self, a, distance):
+        for sign in (1,) if distance == 0 else (1, -1):
+            z = self.at.z - sign * distance
+
+            def take(sign=sign):
+                for flip in (0, 1):
+                    block = (
+                        self.at.f - 4 * sign * distance + flip * self.at.flip1 + self.at.flip3
+                    )
+                    self.arrived(a, block)
+                    self.copy(self.SIB, a, block, self.at.sibling).start()
+
+            pl.when((z >= 0) & (z < self.lengthwise))(take)
+
+    def steps(self):
+        count = len(self.plans)
+        steps = [functools.partial(self.near, a) for a in range(count)]
+        for distance in range(1, self.lengthwise):
+            steps += [functools.partial(self.line, a, distance) for a in range(count)]
+            steps += [functools.partial(self.across, a, distance - 1) for a in range(count)]
+        steps += [functools.partial(self.across, a, self.lengthwise - 1) for a in range(count)]
+        return steps
+
+    def finish(self):
+        at = self.at
+        for a in range(len(self.plans)):
+
+            def block_done(block, _, a=a):
+                z = block // 4
+
+                def from_sibling():
+                    self.arrived(a, block, self.SIB_RECV)
+                    self.sent(self.SIB, a, block)
+
+                if self.shared:
+                    pl.when(jnp.logical_not(block == at.f))(from_sibling)
+                else:
+                    from_sibling()
+
+                @pl.when(at.last_bit(block) == at.last)
+                def _():
+                    self.sent(self.LAST, a, block)
+
+                    @pl.when((z <= at.z) & (at.z < self.lengthwise - 1))
+                    def _():
+                        self.sent(self.UP, a, block)
+
+                    @pl.when((z >= at.z) & (at.z > 0))
+                    def _():
+                        self.sent(self.DOWN, a, block)
+
+                return 0
+
+            lax.fori_loop(0, self.n, block_done, 0)
+            self.sent(self.ONE, a, at.f)
+            if self.shared:
+                for half in (0, 1):
+                    self.local(a, half).wait()
+            else:
+                self.local(a, at.c).wait()
+
+
+def gather_kernel(plans, *refs):
+    count = len(plans)
+    work = Gather(plans, refs[:count], refs[count : 2 * count], refs[2 * count], True)
+    greet(work.at, work.lengthwise)
     for a in range(count):
-        copy(ONE, a, f, (d, partner1), True).start()
-        send_up(a, f, True)
-        send_down(a, f, True)
-        copy(LAST, a, f, (d, partner3), True).start()
-    for a in range(count):
-        for half in (0, 1):
-            local(a, half).start()
-    for a in range(count):
-        block = partner1
-        arrived(a, block)
-        send_up(a, block)
-        send_down(a, block)
-        copy(LAST, a, block, (d, partner3)).start()
-        copy(SIB, a, block, sibling).start()
-
-    def across(distance, a):
-        for sign in (1,) if distance == 0 else (1, -1):
-            at = z - sign * distance
-
-            def take(at=at):
-                for flip in (0, 1):
-                    block = f + 4 * (at - z) + flip * flip1 + flip3
-                    arrived(a, block)
-                    copy(SIB, a, block, sibling).start()
-
-            pl.when((at >= 0) & (at < lengthwise))(take)
-
-    for distance in range(1, lengthwise):
-        for a in range(count):
-            for sign in (1, -1):
-                at = z - sign * distance
-
-                def take(at=at, sign=sign):
-                    for flip in (0, 1):
-                        block = f + 4 * (at - z) + flip * flip1
-                        arrived(a, block)
-                        (send_up if sign == 1 else send_down)(a, block)
-                        copy(LAST, a, block, (d, partner3)).start()
-                        copy(SIB, a, block, sibling).start()
-
-                pl.when((at >= 0) & (at < lengthwise))(take)
-        for a in range(count):
-            across(distance - 1, a)
-    for a in range(count):
-        across(lengthwise - 1, a)
-
-    for a in range(count):
-
-        def finish(block, _, a=a):
-            at = block // 4
-            mine = block == f
-            bit_x, bit_y = lax.rem(block, 2), lax.rem(block // 2, 2)
-            in_plane = bit_y + c * (bit_x - bit_y) == last
-
-            @pl.when(jnp.logical_not(mine))
-            def _():
-                arrived(a, block, SIB_RECV)
-                sent(SIB, a, block)
-
-            @pl.when(in_plane)
-            def _():
-                sent(LAST, a, block)
-
-                @pl.when((at <= z) & (z < lengthwise - 1))
-                def _():
-                    sent(UP, a, block)
-
-                @pl.when((at >= z) & (z > 0))
-                def _():
-                    sent(DOWN, a, block)
-
-            return 0
-
-        lax.fori_loop(0, n, finish, 0)
-        sent(ONE, a, f)
-        for half in (0, 1):
-            local(a, half).wait()
+        work.begin(a)
+    for step in work.steps():
+        step()
+    work.finish()
 
 
 def gather(plans, shards, collective_id):
-    n = plans[0].fsdp
     count = len(plans)
     return pl.pallas_call(
         functools.partial(gather_kernel, plans),
-        out_shape=[jax.ShapeDtypeStruct(plan.shape, BF) for plan in plans],
+        out_shape=[jax.ShapeDtypeStruct(plan.shape, plan.dtype) for plan in plans],
         in_specs=[pl.BlockSpec(memory_space=pl.ANY)] * count,
         out_specs=[pl.BlockSpec(memory_space=pl.ANY)] * count,
-        scratch_shapes=[pltpu.SemaphoreType.DMA((8 * count * n,))],
+        scratch_shapes=[Gather.semaphores(plans)],
         compiler_params=pltpu.CompilerParams(collective_id=collective_id, has_side_effects=True),
     )(*shards)
 
 
+class Reduce:
+    SIB, SIB_RECV, LOAD, NEAR, NEAR_RECV, UP, UP_RECV, DOWN, DOWN_RECV, END = range(10)
+
+    def __init__(self, plans, ins, totals, scratch):
+        count = len(plans)
+        self.plans, self.ins, self.totals = plans, ins, totals
+        self.held, self.landed, self.flow_up, self.flow_down, self.close, self.cross = (
+            scratch[k * count : (k + 1) * count] for k in range(6)
+        )
+        self.sems = scratch[6 * count]
+        self.n = plans[0].fsdp
+        self.lengthwise = self.n // 4
+        self.at = Place()
+
+    @staticmethod
+    def scratch(plans):
+        n = plans[0].fsdp
+        return (
+            [pltpu.VMEM((n,) + plan.block, plan.dtype) for plan in plans] * 2
+            + [pltpu.VMEM((n // 2,) + plan.block, plan.dtype) for plan in plans] * 3
+            + [pltpu.VMEM(plan.block, plan.dtype) for plan in plans]
+            + [pltpu.SemaphoreType.DMA((10 * len(plans) * n,))]
+        )
+
+    def sem(self, kind, a, block):
+        return self.sems.at[(kind * len(self.plans) + a) * self.n + block]
+
+    def slot(self, z, b1, b3):
+        return 4 * z + self.at.stride1 * b1 + self.at.stride3 * b3
+
+    def item(self, t):
+        pair, b3 = t // 2, lax.rem(t, 2)
+        half = pair // 2
+        z = jnp.where(lax.rem(pair, 2) == 0, half, self.lengthwise - 1 - half)
+        return z, b3
+
+    def to_sibling(self, a, block):
+        return remote(
+            self.plans[a].pick(self.ins[a], 1 - self.at.c, block),
+            self.landed[a].at[block],
+            self.sem(self.SIB, a, block),
+            self.sem(self.SIB_RECV, a, block),
+            self.at.sibling,
+        )
+
+    def load(self, a, block):
+        return pltpu.make_async_copy(
+            self.plans[a].pick(self.ins[a], self.at.c, block),
+            self.held[a].at[block],
+            self.sem(self.LOAD, a, block),
+        )
+
+    def to_near(self, a, z, b3):
+        return remote(
+            self.held[a].at[self.slot(z, 1 - self.at.first, b3)],
+            self.close[a].at[2 * z + b3],
+            self.sem(self.NEAR, a, 2 * z + b3),
+            self.sem(self.NEAR_RECV, a, 2 * z + b3),
+            self.at.partner1,
+        )
+
+    def along(self, up, a, z, b3):
+        return remote(
+            self.held[a].at[self.slot(z, self.at.first, b3)],
+            (self.flow_up if up else self.flow_down)[a].at[2 * z + b3],
+            self.sem(self.UP if up else self.DOWN, a, 2 * z + b3),
+            self.sem(self.UP_RECV if up else self.DOWN_RECV, a, 2 * z + b3),
+            (self.at.d, self.at.f + (4 if up else -4)),
+        )
+
+    def to_cross(self, a):
+        return remote(
+            self.held[a].at[self.slot(self.at.z, self.at.first, 1 - self.at.last)],
+            self.cross[a],
+            self.sem(self.END, a, 0),
+            self.sem(self.END, a, 1),
+            self.at.partner3,
+        )
+
+    def rows(self, a, body):
+        unit = 16
+
+        def step(i, _):
+            body(pl.ds(pl.multiple_of(i * unit, unit), unit))
+            return 0
+
+        if self.plans[a].block[0] < unit:
+            body(slice(None))
+        else:
+            lax.fori_loop(0, self.plans[a].block[0] // unit, step, 0)
+
+    def add(self, a, block, sources):
+        held = self.held[a]
+
+        def body(where):
+            total = held[block, where, :].astype(F32)
+            for ref, at in sources:
+                total += ref[at, where, :].astype(F32)
+            held[block, where, :] = total.astype(held.dtype)
+
+        self.rows(a, body)
+
+    def begin(self, a):
+        for flip in (1, 0):
+            b1 = self.at.first + flip * (1 - 2 * self.at.first)
+
+            def start(t, _, b1=b1):
+                z, b3 = self.item(t)
+                block = self.slot(z, b1, b3)
+                self.to_sibling(a, block).start()
+                self.load(a, block).start()
+                return 0
+
+            lax.fori_loop(0, 2 * self.lengthwise, start, 0)
+
+    def first_leg(self, a, t):
+        z, b3 = self.item(t)
+        block = self.slot(z, 1 - self.at.first, b3)
+        self.load(a, block).wait()
+        self.to_sibling(a, block).wait_recv()
+        self.add(a, block, [(self.landed[a], block)])
+        self.to_near(a, z, b3).start()
+
+    def middle_leg(self, a, t):
+        z, b3 = self.item(t)
+        block = self.slot(z, self.at.first, b3)
+        flow = 2 * z + b3
+        base = [(self.landed[a], block), (self.close[a], flow)]
+        self.load(a, block).wait()
+        self.to_sibling(a, block).wait_recv()
+        self.to_near(a, z, b3).wait_recv()
+
+        def onward(up):
+            incoming = self.at.z > 0 if up else self.at.z < self.lengthwise - 1
+
+            @pl.when(incoming)
+            def _():
+                self.along(up, a, z, b3).wait_recv()
+                flows = self.flow_up if up else self.flow_down
+                self.add(a, block, base + [(flows[a], flow)])
+
+            @pl.when(jnp.logical_not(incoming))
+            def _():
+                self.add(a, block, base)
+
+            self.along(up, a, z, b3).start()
+
+        pl.when(z > self.at.z)(functools.partial(onward, True))
+        pl.when(z < self.at.z)(functools.partial(onward, False))
+
+        @pl.when(z == self.at.z)
+        def _():
+            self.add(a, block, base)
+
+    def own(self, a, b3):
+        z = self.at.z
+        block = self.slot(z, self.at.first, b3)
+        for up in (True, False):
+
+            @pl.when(z > 0 if up else z < self.lengthwise - 1)
+            def _(up=up):
+                self.along(up, a, z, b3).wait_recv()
+                flows = self.flow_up if up else self.flow_down
+                self.add(a, block, [(flows[a], 2 * z + b3)])
+
+    def cross_over(self, a):
+        self.own(a, 1 - self.at.last)
+        self.to_cross(a).start()
+
+    def last_leg(self, a):
+        self.own(a, self.at.last)
+        self.to_cross(a).wait_recv()
+        block = self.slot(self.at.z, self.at.first, self.at.last)
+
+        def body(where):
+            total = self.held[a][block, where, :].astype(F32) + self.cross[a][where, :].astype(F32)
+            self.totals[a][where, :] = total
+
+        self.rows(a, body)
+
+    def finish(self, a):
+        def done(t, _):
+            z, b3 = self.item(t)
+            for b1 in (self.at.first, 1 - self.at.first):
+                self.to_sibling(a, self.slot(z, b1, b3)).wait_send()
+            self.to_near(a, z, b3).wait_send()
+            for up in (True, False):
+
+                @pl.when(z > self.at.z if up else z < self.at.z)
+                def _(up=up):
+                    self.along(up, a, z, b3).wait_send()
+
+            return 0
+
+        lax.fori_loop(0, 2 * self.lengthwise, done, 0)
+        self.to_cross(a).wait_send()
+
+
+def pair_exchange(plans, totals, outs, sems, at):
+    copies = []
+    for a, plan in enumerate(plans):
+        if not plan.by_rows:
+            copies.append(
+                remote(
+                    totals[a], outs[a].at[at.c], sems.at[2 * a], sems.at[2 * a + 1], at.sibling
+                )
+            )
+    return copies
+
+
 def reduce_kernel(plans, *refs):
     count = len(plans)
-    ins, outs = refs[:count], refs[count : 2 * count]
-    scratch = refs[2 * count :]
-    held, landed, flow_up, flow_down, near, cross = (
-        scratch[k * count : (k + 1) * count] for k in range(6)
-    )
-    sems = scratch[6 * count]
-    n, dp = plans[0].fsdp, plans[0].dp
-    lengthwise = n // 4
-    d, f, c, z, first, last, stride1, stride3 = place(n, dp)
-    partner1 = f + stride1 * (1 - 2 * first)
-    partner3 = f + stride3 * (1 - 2 * last)
-    sibling = (d + 1 - 2 * c, f)
-    SIB, SIB_RECV, LOAD, NEAR, NEAR_RECV, UP, UP_RECV, DOWN, DOWN_RECV, END = range(10)
-
-    def sem(kind, a, block):
-        return sems.at[(kind * count + a) * n + block]
-
-    def slot(at, b1, b3):
-        return 4 * at + stride1 * b1 + stride3 * b3
-
-    def order(step):
-        half = step // 2
-        return jnp.where(lax.rem(step, 2) == 0, half, lengthwise - 1 - half)
-
-    barrier = pltpu.get_barrier_semaphore()
-    for target in ((d, partner1), (d, partner3), sibling):
-        pl.semaphore_signal(barrier, inc=1, device_id=target, device_id_type=MESH)
-
-    @pl.when(z > 0)
-    def _():
-        pl.semaphore_signal(barrier, inc=1, device_id=(d, f - 4), device_id_type=MESH)
-
-    @pl.when(z < lengthwise - 1)
-    def _():
-        pl.semaphore_signal(barrier, inc=1, device_id=(d, f + 4), device_id_type=MESH)
-
-    has_down = (z > 0).astype(jnp.int32)
-    has_up = (z < lengthwise - 1).astype(jnp.int32)
-    pl.semaphore_wait(barrier, 3 + has_down + has_up)
-
-    def remote(src, dst, send, recv, target):
-        return pltpu.make_async_remote_copy(
-            src_ref=src,
-            dst_ref=dst,
-            send_sem=send,
-            recv_sem=recv,
-            device_id=target,
-            device_id_type=MESH,
-        )
-
-    def to_sibling(a, block):
-        return remote(
-            plans[a].pick(ins[a], 1 - c, block),
-            landed[a].at[block],
-            sem(SIB, a, block),
-            sem(SIB_RECV, a, block),
-            sibling,
-        )
-
-    def load(a, block):
-        return pltpu.make_async_copy(
-            plans[a].pick(ins[a], c, block), held[a].at[block], sem(LOAD, a, block)
-        )
-
-    def to_near(a, at, b3):
-        return remote(
-            held[a].at[slot(at, 1 - first, b3)],
-            near[a].at[2 * at + b3],
-            sem(NEAR, a, 2 * at + b3),
-            sem(NEAR_RECV, a, 2 * at + b3),
-            (d, partner1),
-        )
-
-    def to_up(a, at, b3):
-        return remote(
-            held[a].at[slot(at, first, b3)],
-            flow_up[a].at[2 * at + b3],
-            sem(UP, a, 2 * at + b3),
-            sem(UP_RECV, a, 2 * at + b3),
-            (d, f + 4),
-        )
-
-    def to_down(a, at, b3):
-        return remote(
-            held[a].at[slot(at, first, b3)],
-            flow_down[a].at[2 * at + b3],
-            sem(DOWN, a, 2 * at + b3),
-            sem(DOWN_RECV, a, 2 * at + b3),
-            (d, f - 4),
-        )
-
-    def to_cross(a):
-        return remote(
-            held[a].at[slot(z, first, 1 - last)],
-            cross[a],
-            sem(END, a, 0),
-            sem(END, a, 1),
-            (d, partner3),
-        )
-
-    def to_pair(a):
-        return remote(outs[a].at[c], outs[a].at[c], sem(END, a, 2), sem(END, a, 3), sibling)
-
-    def add_into(a, block, source, at):
-        def rows(step, _):
-            where = pl.ds(pl.multiple_of(step * 16, 16), 16)
-            held[a][block, where, :] = (
-                held[a][block, where, :].astype(F32) + source[at, where, :].astype(F32)
-            ).astype(BF)
+    ins, outs, scratch = refs[:count], refs[count : 2 * count], refs[2 * count :]
+    totals = [out if plan.by_rows else out.at[Place().c] for plan, out in zip(plans, outs)]
+    work = Reduce(plans, ins, totals, scratch[:-1])
+    at, items = work.at, 2 * work.lengthwise
+    greet(at, work.lengthwise)
+    for a in range(count):
+        work.begin(a)
+
+    def leg(body, a, begin, end):
+        def step(t, _):
+            body(a, t)
             return 0
 
-        lax.fori_loop(0, plans[a].block[0] // 16, rows, 0)
-
-    def each(body):
-        for a in range(count):
-
-            def step(t, _, a=a):
-                body(a, order(t // 2), lax.rem(t, 2))
-                return 0
-
-            lax.fori_loop(0, 2 * lengthwise, step, 0)
-
-    def begin(b1):
-        def body(a, at, b3):
-            block = slot(at, b1, b3)
-            load(a, block).start()
-
-        return body
-
-    def begin_sibling(b1):
-        def body(a, at, b3):
-            to_sibling(a, slot(at, b1, b3)).start()
-
-        return body
-
-    each(begin_sibling(1 - first))
-    each(begin(1 - first))
-    each(begin_sibling(first))
-    each(begin(first))
-
-    def first_leg(a, at, b3):
-        block = slot(at, 1 - first, b3)
-        load(a, block).wait()
-        to_sibling(a, block).wait_recv()
-        add_into(a, block, landed[a], block)
-        to_near(a, at, b3).start()
-
-    def middle_leg(a, at, b3):
-        block = slot(at, first, b3)
-        load(a, block).wait()
-        to_sibling(a, block).wait_recv()
-        add_into(a, block, landed[a], block)
-        to_near(a, at, b3).wait_recv()
-        add_into(a, block, near[a], 2 * at + b3)
-
-        @pl.when(at > z)
-        def _():
-            @pl.when(z > 0)
-            def _():
-                to_up(a, at, b3).wait_recv()
-                add_into(a, block, flow_up[a], 2 * at + b3)
-
-            to_up(a, at, b3).start()
-
-        @pl.when(at < z)
-        def _():
-            @pl.when(z < lengthwise - 1)
-            def _():
-                to_down(a, at, b3).wait_recv()
-                add_into(a, block, flow_down[a], 2 * at + b3)
-
-            to_down(a, at, b3).start()
-
-    def gather_own(a, b3):
-        block = slot(z, first, b3)
-
-        @pl.when(z > 0)
-        def _():
-            to_up(a, z, b3).wait_recv()
-            add_into(a, block, flow_up[a], 2 * z + b3)
-
-        @pl.when(z < lengthwise - 1)
-        def _():
-            to_down(a, z, b3).wait_recv()
-            add_into(a, block, flow_down[a], 2 * z + b3)
-
-    each(first_leg)
-    each(middle_leg)
+        lax.fori_loop(begin, end, step, 0)
+
     for a in range(count):
-        gather_own(a, 1 - last)
-        to_cross(a).start()
+        leg(work.first_leg, a, 0, items)
     for a in range(count):
-        gather_own(a, last)
-        to_cross(a).wait_recv()
-        block = slot(z, first, last)
-
-        def rows(step, _, a=a, block=block):
-            where = pl.ds(pl.multiple_of(step * 16, 16), 16)
-            total = held[a][block, where, :].astype(F32) + cross[a][where, :].astype(F32)
-            if plans[a].by_rows:
-                outs[a][where, :] = total
-            else:
-                outs[a][c, where, :] = total
-            return 0
-
-        lax.fori_loop(0, plans[a].block[0] // 16, rows, 0)
-        if not plans[a].by_rows:
-            to_pair(a).start()
-
-    def finish(a, at, b3):
-        for b1 in (first, 1 - first):
-            to_sibling(a, slot(at, b1, b3)).wait_send()
-        to_near(a, at, b3).wait_send()
-
-        @pl.when(at > z)
-        def _():
-            to_up(a, at, b3).wait_send()
-
-        @pl.when(at < z)
-        def _():
-            to_down(a, at, b3).wait_send()
-
-    each(finish)
+        leg(work.middle_leg, a, 0, items)
     for a in range(count):
-        to_cross(a).wait_send()
-        if not plans[a].by_rows:
-            to_pair(a).wait()
+        work.cross_over(a)
+    copies = pair_exchange(plans, totals, outs, scratch[-1], at)
+    for a in range(count):
+        work.last_leg(a)
+    for copy in copies:
+        copy.start()
+    for a in range(count):
+        work.finish(a)
+    for copy in copies:
+        copy.wait()
+
+
+def reduce_out(plan):
+    return jax.ShapeDtypeStruct(plan.block if plan.by_rows else (2,) + plan.block, F32)
 
 
 def reduce_scatter(plans, grads, collective_id):
-    n = plans[0].fsdp
     count = len(plans)
     return pl.pallas_call(
         functools.partial(reduce_kernel, plans),
-        out_shape=[
-            jax.ShapeDtypeStruct(plan.block if plan.by_rows else (2,) + plan.block, F32)
-            for plan in plans
-        ],
+        out_shape=[reduce_out(plan) for plan in plans],
         in_specs=[pl.BlockSpec(memory_space=pl.ANY)] * count,
         out_specs=[pl.BlockSpec(memory_space=pltpu.VMEM)] * count,
-        scratch_shapes=[pltpu.VMEM((n,) + plan.block, BF) for plan in plans] * 2
-        + [pltpu.VMEM((n // 2,) + plan.block, BF) for plan in plans] * 3
-        + [pltpu.VMEM(plan.block, BF) for plan in plans]
-        + [pltpu.SemaphoreType.DMA((10 * count * n,))],
+        scratch_shapes=Reduce.scratch(plans) + [pltpu.SemaphoreType.DMA((2 * count,))],
         compiler_params=pltpu.CompilerParams(
             collective_id=collective_id, has_side_effects=True, vmem_limit_bytes=60 * 2**20
         ),
     )(*grads)
 
 
-def hot_rows(index_ref):
-    index = index_ref[...]
+def hot_rows(index):
     lane = lax.broadcasted_iota(jnp.int32, (index.shape[0], HOT), 1)
     hit = lane == index[:, 0:1]
     for q in range(1, KMAX + 1):
@@ -551,7 +615,7 @@
 
 def conv_forward_kernel(filters, index_ref, length_ref, table_ref, kernel_ref, width_ref, out_ref):
     words = length_ref.shape[0]
-    windows = dot(hot_rows(index_ref), table_ref[...]).astype(BF)
+    windows = dot(hot_rows(index_ref[...]), table_ref[...]).astype(BF)
     chunk = 384
     for at in range(0, kernel_ref.shape[1], chunk):
         columns = slice(at, at + chunk)
@@ -567,28 +631,21 @@
         ).astype(BF)
 
 
-def conv_backward_kernel(
-    index_ref, length_ref, table_ref, kernel_ref, width_ref, grad_ref, kernel_grad_ref, hot_grad_ref
-):
-    words = length_ref.shape[0]
-
-    @pl.when(pl.program_id(0) == 0)
-    def _():
-        kernel_grad_ref[...] = jnp.zeros_like(kernel_grad_ref)
-        hot_grad_ref[...] = jnp.zeros_like(hot_grad_ref)
-
-    hot = hot_rows(index_ref)
+def conv_backward_block(index, lengths, refs, grad_ref, where, kernel_grad_ref, hot_grad_ref):
+    table_ref, kernel_ref, width_ref = refs
+    words = lengths.shape[0]
+    hot = hot_rows(index)
     windows = dot(hot, table_ref[...]).astype(BF)
     chunk = 384
     grad_windows = jnp.zeros(windows.shape, F32)
     for at in range(0, kernel_ref.shape[1], chunk):
         columns = slice(at, at + chunk)
         activated = jnp.tanh(dot(windows, kernel_ref[:, columns])).reshape(words, SLOTS, chunk)
-        counts = jnp.maximum(length_ref[...] - width_ref[:, columns] + 1, 1)
+        counts = jnp.maximum(lengths - width_ref[:, columns] + 1, 1)
         position = lax.broadcasted_iota(jnp.int32, (words, SLOTS, chunk), 1)
         inside = position < counts[:, None, :]
         weight = jnp.where(inside, jnp.exp(activated), 0.0)
-        share = grad_ref[:, columns] / jnp.sum(weight, axis=1)
+        share = grad_ref[where, columns] / jnp.sum(weight, axis=1)
         grad = (share[:, None, :] * weight * (1.0 - activated * activated)).astype(BF)
         grad = grad.reshape(words * SLOTS, chunk)
         kernel_grad_ref[:, columns] += dot_rows(windows, grad)
@@ -604,6 +661,144 @@
         pl.BlockSpec((LANE, filters_padded), lambda i: (0, 0)),
         pl.BlockSpec((1, filters_padded), lambda i: (0, 0)),
     ]
+
+
+class Dense:
+    by_rows = False
+    dtype = F32
+
+    def __init__(self, rows, columns, fsdp):
+        self.fsdp = fsdp
+        self.filled = rows
+        self.block = (up_to(-(-rows // fsdp), 8), columns // 2)
+        self.shape = (2, fsdp) + self.block
+
+    def pick(self, ref, half, slot):
+        return ref.at[half, slot]
+
+
+WORD_BLOCK = 16
+
+
+def tail_kernel(plans, blocks, *refs):
+    conv, rest = plans[0], plans[1:]
+    count = len(plans)
+    ins, refs = refs[: count - 1], refs[count - 1 :]
+    index_ref, length_ref, table_ref, kernel_ref, width_ref, grad_ref, mask_ref, fold_ref = refs[:8]
+    outs, refs = refs[8 : 8 + count], refs[8 + count :]
+    conv_out, rest_outs = outs[0], outs[1:]
+    kernel_grad, hot_grad, conv_in, conv_total = refs[:4]
+    pair_sems, gather_sems = refs[4:6]
+    at = Place()
+    totals = [conv_total] + [
+        out if plan.by_rows else out.at[at.c] for plan, out in zip(rest, rest_outs)
+    ]
+    work = Reduce(plans, [conv_in] + list(ins), totals, refs[6:])
+    items = 2 * work.lengthwise
+    greet(at, work.lengthwise)
+    for a in range(1, count):
+        work.begin(a)
+    kernel_grad[...] = jnp.zeros_like(kernel_grad)
+    hot_grad[...] = jnp.zeros_like(hot_grad)
+    conv_in[...] = jnp.zeros_like(conv_in)
+
+    def compute(i):
+        words = pl.ds(pl.multiple_of(i * WORD_BLOCK, WORD_BLOCK), WORD_BLOCK)
+        slots = pl.ds(pl.multiple_of(i * WORD_BLOCK * SLOTS, WORD_BLOCK * SLOTS), WORD_BLOCK * SLOTS)
+        conv_backward_block(
+            index_ref[slots, :],
+            length_ref[words, :],
+            (table_ref, kernel_ref, width_ref),
+            grad_ref,
+            words,
+            kernel_grad,
+            hot_grad,
+        )
+
+    lead = 2
+
+    def together(t, _):
+        @pl.when(t < items)
+        def _():
+            for a in range(1, count):
+                work.first_leg(a, t)
+
+        pl.when(t < blocks)(functools.partial(compute, t))
+
+        @pl.when((t >= lead) & (t < items + lead))
+        def _():
+            for a in range(1, count):
+                work.middle_leg(a, t - lead)
+
+        return 0
+
+    lax.fori_loop(0, max(items + lead, blocks), together, 0)
+
+    wide = kernel_ref.shape[1]
+    kernel_grad[:, wide:] = jnp.dot(
+        fold_ref[...],
+        hot_grad[...] * mask_ref[...],
+        precision=lax.Precision.HIGHEST,
+        preferred_element_type=F32,
+    )
+    depth, half = conv.block
+    for block in range(conv.filled // depth):
+        for h in range(2):
+            conv_in[h, block] = kernel_grad[
+                block * depth : (block + 1) * depth, h * half : (h + 1) * half
+            ]
+    work.begin(0)
+
+    def leg(body):
+        def step(t, _):
+            body(0, t)
+            return 0
+
+        lax.fori_loop(0, items, step, 0)
+
+    leg(work.first_leg)
+    leg(work.middle_leg)
+    for a in range(count):
+        work.cross_over(a)
+    work.last_leg(0)
+    spread = Gather([conv], [conv_total], [conv_out], gather_sems, False)
+    spread.begin(0)
+    copies = pair_exchange(rest, totals[1:], rest_outs, pair_sems, at)
+    for a in range(1, count):
+        work.last_leg(a)
+    for copy in copies:
+        copy.start()
+    for step in spread.steps():
+        step()
+    spread.finish()
+    for a in range(count):
+        work.finish(a)
+    for copy in copies:
+        copy.wait()
+
+
+def tail(plans, grads, conv_inputs, grad, mask, fold, collective_id):
+    conv, rest = plans[0], plans[1:]
+    words = grad.shape[0]
+    return pl.pallas_call(
+        functools.partial(tail_kernel, plans, words // WORD_BLOCK),
+        out_shape=[jax.ShapeDtypeStruct(conv.shape, F32)] + [reduce_out(plan) for plan in rest],
+        in_specs=[pl.BlockSpec(memory_space=pl.ANY)] * len(rest)
+        + [pl.BlockSpec(memory_space=pltpu.VMEM)] * 8,
+        out_specs=[pl.BlockSpec(memory_space=pltpu.VMEM)] * len(plans),
+        scratch_shapes=[
+            pltpu.VMEM((conv.filled, 2 * conv.block[1]), F32),
+            pltpu.VMEM((HOT, LANE), F32),
+            pltpu.VMEM(conv.shape, F32),
+            pltpu.VMEM(conv.block, F32),
+            pltpu.SemaphoreType.DMA((2 * len(rest),)),
+            Gather.semaphores([conv]),
+        ]
+        + Reduce.scratch(plans),
+        compiler_params=pltpu.CompilerParams(
+            collective_id=collective_id, has_side_effects=True, vmem_limit_bytes=60 * 2**20
+        ),
+    )(*grads, *conv_inputs, grad, mask, fold)
 
 
 def gate_parts(sums):
@@ -852,12 +1047,13 @@
     soft = Windows(soft_flat.shape[0] * fsdp_count, V, H + 1, fsdp_count, dp_count, False)
 
     soft_own = soft.from_flat(soft_flat, fsdp_at)
-    soft_all = lax.all_gather(soft_own, "fsdp", axis=0)
     highway_all, lstm_all = gather(
         [highway, lstm],
         [highway.from_flat(highway_flat, fsdp_at), lstm.from_flat(lstm_flat, fsdp_at)],
         1,
     )
+    highway_all, soft_own = lax.optimization_barrier((highway_all, soft_own))
+    soft_all = lax.all_gather(soft_own, "fsdp", axis=0)
     highway_all = highway_all.reshape(-1, highway.columns)
     lstm_all = lstm_all.reshape(2, -1, lstm.columns // 2)
 
@@ -911,7 +1107,7 @@
     )
     spread_table = jnp.pad(spread_table, ((0, HOT - KMAX * char_count - 1), (0, 0)))
     conv_inputs = (index, word_lengths, spread_table, kernel, jnp.asarray(widths)[None, :])
-    word_block = 16
+    word_block = WORD_BLOCK
     feature = pl.pallas_call(
         functools.partial(conv_forward_kernel, filters),
         out_shape=jax.ShapeDtypeStruct((rows, fp), BF),
@@ -1082,29 +1278,31 @@
     )
 
     grad = jnp.where(filter_lane < filters, grad, 0.0)
-    kernel_grad, hot_grad = pl.pallas_call(
-        conv_backward_kernel,
-        out_shape=[
-            jax.ShapeDtypeStruct((LANE, fp), F32),
-            jax.ShapeDtypeStruct((HOT, LANE), F32),
-        ],
-        grid=(rows // word_block,),
-        in_specs=conv_specs(word_block, fp) + [pl.BlockSpec((word_block, fp), lambda i: (i, 0))],
-        out_specs=[
-            pl.BlockSpec((LANE, fp), lambda i: (0, 0)),
-            pl.BlockSpec((HOT, LANE), lambda i: (0, 0)),
-        ],
-        compiler_params=pltpu.CompilerParams(vmem_limit_bytes=48 * 2**20),
-    )(*conv_inputs, grad)
-    table_grad = sum(
-        hot_grad[q * char_count : (q + 1) * char_count, q * embed_dim : (q + 1) * embed_dim]
-        for q in range(KMAX)
-    )
-    kernel_grad, table_grad = lax.psum((kernel_grad, table_grad), ("dp", "fsdp"))
-    conv_weight_grad = jnp.where(kernel_mask, kernel_grad[:ones_row, :filters], 0.0)
-    conv_bias_grad = kernel_grad[ones_row, :filters]
-
-    highway_part, lstm_part = reduce_scatter([highway, lstm], [highway_grad, lstm_grad], 3)
+    hot_row, hot_lane = np.arange(HOT), np.arange(LANE)
+    hot_mask = (hot_row[:, None] // char_count == hot_lane[None, :] // embed_dim) & (
+        hot_row[:, None] < KMAX * char_count
+    )
+    hot_fold = (hot_row[None, :] % char_count == np.arange(LANE)[:, None]) & (
+        hot_row[None, :] < KMAX * char_count
+    )
+    conv = Dense(LANE, up_to(fp + LANE, 2 * LANE), fsdp_count)
+    conv_grad, highway_part, lstm_part = tail(
+        [conv, highway, lstm],
+        [highway_grad, lstm_grad],
+        conv_inputs,
+        grad,
+        jnp.asarray(hot_mask.astype(np.float32)),
+        jnp.asarray(hot_fold.astype(np.float32)),
+        3,
+    )
+    conv_grad = jnp.concatenate(
+        [conv_grad[h].reshape(-1, conv.block[1])[:LANE] for h in range(2)], axis=1
+    )
+    conv_weight_grad = jnp.where(kernel_mask, conv_grad[:ones_row, :filters], 0.0)
+    conv_bias_grad = conv_grad[ones_row, :filters]
+    table_grad = jnp.sum(
+        conv_grad[:char_count, fp : fp + KMAX * embed_dim].reshape(char_count, KMAX, embed_dim), axis=1
+    )
 
     def own_window(plan, part):
         if dp_count > 2:

time: 971 us -> 755 us (0.78)
  the two profiles are of different devices: /device:TPU:0 before, /device:TPU:21 now
where the time goes in v2:
time: 755 us; the launch traced here: 746 us
  Pallas kernels  493 us (65%)
  matrix products  88.1 us (12%)
  local copies, waits for them, and re-layouts  67.5 us (9%)
  waiting for transfers between devices  55.3 us (7%)
  other arithmetic  24.5 us (3%)
  between operations  16.8 us (2%)
    pallas_call x1, Pallas kernels, tail(): pl.pallas_call(functools.partial(tail_kernel, plans, words // WORD_BLOCK)...  160 us
    pallas_call x1, Pallas kernels, reduce_scatter(): pl.pallas_call(functools.partial(reduce_kernel, plans), out_shape=[reduce...  124 us
    pallas_call x1, Pallas kernels, gather(): pl.pallas_call(functools.partial(gather_kernel, plans), out_shape=[jax.Sh...  86.9 us
    pallas_call x2, Pallas kernels, in_vmem(): pl.pallas_call(kernel, out_shape=out_shapes, in_specs=[pl.BlockSpec(memor...  61.6 us
    all_gather x1, waiting for transfers between devices, shards(): soft_all = lax.all_gather(soft_own, 'fsdp', axis=0)  55.3 us
    dot_general x14, matrix products, dot(): return jnp.dot(left, right, preferred_element_type=F32)  46.8 us
    pallas_call x1, Pallas kernels, word_softmax(): pl.pallas_call(functools.partial(softmax_kernel, plan.width, 2 * per_half...  45 us
    dot_general x3, matrix products, dot_rows(): lax.dot_general(left, right, (((0,), (0,)), ((), ())), preferred_element_...  21.4 us
  transfers between devices with their start and end apart: 1, of which 1 were waited for; matrix products, arithmetic and copies ran while one was open for 12% of the time, Pallas kernels for 6%

profile of v2, /device:TPU:21, one launch (start us, length us, event | category | flops | bytes accessed | tf_op | source)
XLA Modules:
  0.0 745.6 jit_solution(13480691334636538691)
XLA Ops:
  8.4 2.7 dynamic_update_slice.21
  11.6 2.7 dynamic_update_slice.20
  15.0 2.9 dynamic_update_slice.19
  18.6 2.9 dynamic_update_slice.18
  22.3 3.8 dynamic_update_slice.23
  26.9 3.8 dynamic_update_slice.22
  33.4 86.9 %shard_map.370 = (bf16[16,2,144,1152]{3,2,1,0:T(8,128)(2,1)}, bf16[2,16,112,1408]{3,2,1,0:T(8,128)(2,1)}) custom-call(bf16[2,144,1152]{2,1,0:T(8,128)(2,1)} %bitcast.125, bf16[2,112,1408]{2,1,0:T(8,128)(2,1)} %pad_maximum_fusion.5.refs_1_), custom_call_target="tpu_custom_call" | custom-call | tf_op jit(solution)/shard_map/pallas_call | solution.py:336
  121.4 5.2 slice.261
  133.6 1.2 scatter.4
  136.1 14.9 %shard_map.369 = bf16[144,1152]{1,0:T(8,128)(2,1)S(1)} custom-call(s32[3456,8]{1,0:T(8,128)S(1)} %copy.86.index_ref.refs_2_, s32[144,1]{1,0:T(8,128)S(1)} %copy.87.length_ref.refs_3_, bf16[384,128]{1,0:T(8,128)(2,1)S(1)} %pad.98.table_ref.refs_4_, bf16[128,1152]{1,0:T(8,128)(2,1)S(1)} %fusion.130.kernel_ref.refs_5_, s32[1,1152]{1,0:T(1,128)S(1)} %copy-done.10), custom_call_target="tpu_custom_call" | custom-call | tf_op jit(solution)/shard_map/pallas_call | solution.py:1111
  151.1 2.5 multiply_convert_fusion.7
  153.6 4.6 fusion.49
  160.0 2.7 multiply_convert_fusion.5
  162.8 2.1 fusion.26
  166.6 2.8 fusion.33
  169.4 9.5 %fusion.151 = (bf16[1,16,112,1408]{3,2,1,0:T(8,128)(2,1)}, bf16[1,16,112,1408]{3,2,1,0:T(8,128)(2,1)}) fusion(bf16[2,16,112,1408]{3,2,1,0:T(8,128)(2,1)} %get-tuple-element.39), kind=kLoop, calls=%fused_computation.266 | loop fusion | bytes 20185088 | tf_op jit(solution)/shard_map/slice | solution.py:1166
  179.0 3.6 fusion.153
  184.6 3.5 convolution_convert_fusion.5
  188.1 3.5 convolution_convert_fusion.6
  191.7 2.3 pad_maximum_fusion.1.w_ref
  194.0 29.7 %shard_map.371 = (f32[144,768]{1,0:T(8,128)S(1)}, f32[144,768]{1,0:T(8,128)S(1)}, f32[144,768]{1,0:T(8,128)S(1)}, f32[144,768]{1,0:T(8,128)S(1)}, f32[144,768]{1...) custom-call(f32[144,2816]{1,0:T(8,128)S(1)} %pad_maximum_fusion.3.x_ref, ...), custom_call_target="tpu_custom_call" | custom-call | tf_op jit(solution)/shard_map/pallas_call | solution.py:906
  224.4 2.4 concatenate.93
  226.9 2.0 fusion.67.h_back_ref
  228.9 2.0 fusion.68.h_ref
  230.9 3.6 fusion.32
  234.5 3.5 convolution_convert_fusion.3
  238.0 3.5 convolution_convert_fusion.4
  241.6 6.3 multiply_convert_fusion.1
  247.9 6.7 multiply_convert_fusion.3
  254.6 2.3 pad_maximum_fusion.2.w_ref
  256.9 55.3 %all-gather.3.cloned.1.call-done = bf16[32,48,5120]{2,1,0:T(8,128)(2,1)} async-done(((bf16[2,48,5120]{2,1,0:T(8,128)(2,1)}), bf16[32,48,5120]{2,1,0:T(8,128)(2,1)}) %all-gather.3.cloned.1.call-update) | async-done | bytes 15728656 | tf_op jit(solution)/shard_map/all_gather | solution.py:1056
  315.9 45.0 %shard_map.372 = (f32[144,1]{1,0:T(8,128)S(1)}, f32[144,768]{1,0:T(8,128)S(1)}, bf16[2,16,48,5120]{3,2,1,0:T(8,128)(2,1)}) custom-call(bf16[144,768]{1,0:T(8,128)(2,1)S(1)} %copy-done.7, bf16[144,768]{1,0:T(8,128)(2,1)S(1)} %copy-done.6, bf16[16,2,48,5120]{3,2,1,0:T(8,128)(2,1)} %bitcast.111, s32[144,1]{1,0:T(8,128)S(1)} %copy-done.5, f32[144,1]{1,0:T(8,128)S(1)} %copy-done.4), custom_call_target="tpu_custom_call" | custom-call | tf_op jit(solution)/shard_map/pallas_call | solution.py:981
  361.6 31.9 %shard_map.373 = f32[144,2816]{1,0:T(8,128)S(1)} custom-call(f32[144,768]{1,0:T(8,128)S(1)} %slice_add_fusion.3.dh_ref, bf16[2816,768]{1,0:T(8,128)(2,1)} %pad_maximum_fusion.2.w_ref, f32[144,1]{1,0:T(8,128)S(1)} %copy.90.keep_ref, f32[144,768]{1,0:T(8,128)S(1)} %get-tuple-element.44.cp_ref, f32[144,768]{1,0:T(8,128)S(1)} %get-tuple-element.45.i_ref, ...), custom_call_target="tpu_custom_call" | custom-call | tf_op jit(solution)/shard_map/pallas_call | solution.py:906
  394.7 3.8 convolution_convert_fusion.2
  398.6 4.2 convolution_convert_fusion.1
  402.8 1.2 reduce-precision_convert_fusion.2
  404.0 1.3 fusion.23
  406.2 2.1 fusion.24
  409.1 2.5 fusion.4
  412.7 2.1 fusion.107
  415.5 2.0 fusion.8
  418.6 8.9 %pad_maximum_fusion.refs_1_ = bf16[2,16,112,1408]{3,2,1,0:T(8,128)(2,1)} fusion(bf16[1,16,112,1408]{3,2,1,0:T(8,128)(2,1)} %bitcast.108, bf16[1,16,112,1408]{3,2,1,0:T(8,128)(2,1)} %bitcast.107), kind=kLoop, calls=%fused_computation.17 | loop fusion | flops 5046272 | bytes 20185088 | tf_op jit(solution)/shard_map/stack | solution.py:1243
  427.5 13.3 %convolution_convert_fusion = bf16[4608,1152]{1,0:T(8,128)(2,1)} fusion(bf16[144,4608]{1,0:T(8,128)(2,1)} %get-tuple-element.70, bf16[144,4608]{1,0:T(8,128)(2,1)S(1)} %copy-done.59, bf16[144,4608]{1,0:T(8,128)(2,1)} %get-tuple-element.68, bf16[144,4608]{1,0:T(8,128)(2,1)} %get-tuple-element.67, bf16[144,1152]{1,0:T(8,128)(2,1)S(1)} %multiply_convert_fusion.9, ...), kind=kOutput, calls=%fused_computation.4 | convolution fusion | flops 6147145728 | bytes 17252352 | tf_op jit(solution)/shard_map/dot_general | solution.py:33
  440.8 160.5 %shard_map.374 = (f32[2,16,8,640]{3,2,1,0:T(8,128)}, f32[144,1152]{1,0:T(8,128)}, f32[2,112,1408]{2,1,0:T(8,128)}) custom-call(bf16[16,2,144,1152]{3,2,1,0:T(8,128)(2,1)} %bitcast.112, bf16[2,16,112,1408]{3,2,1,0:T(8,128)(2,1)} %pad_maximum_fusion.refs_1_, s32[3456,8]{1,0:T(8,128)} %copy-done, s32[144,1]{1,0:T(8,128)} %copy-done.3, ...), custom_call_target="tpu_custom_call" | custom-call | tf_op jit(solution)/shard_map/pallas_call | solution.py:783
  603.9 124.4 %shard_map.375 = f32[2,48,5120]{2,1,0:T(8,128)} custom-call(bf16[2,16,48,5120]{3,2,1,0:T(8,128)(2,1)} %get-tuple-element.54.refs_0_), custom_call_target="tpu_custom_call" | custom-call | tf_op jit(solution)/shard_map/pallas_call | solution.py:596
  728.4 1.6 slice_bitcast_fusion.12
  731.9 1.6 reshape.236
  735.1 1.2 dynamic-slice_bitcast_fusion
  (260 shorter events, 39.6 us)
Async XLA Ops:
  7.2 305.0 %all-gather.3.cloned.1.call-start = ((), (), s32[]{:S(2)}) async-start(), calls=%async_computation | async-start | bytes 16711680 | tf_op jit(solution)/shard_map/all_gather | solution.py:1056
  11.1 3.8 copy-start.22
  14.9 7.3 copy-start.21
  121.4 5.3 copy-start.40
  121.4 5.5 copy-start.28
  126.7 3.3 copy-start.37
  126.7 3.4 copy-start.39
  126.7 3.7 copy-start.29
  126.7 3.8 copy-start.42
  126.7 4.6 copy-start.41
  127.1 8.8 %copy-start.23 = (pred[105,1100]{1,0:T(8,128)(4,1)S(1)}, pred[105,1100]{1,0:T(8,128)(4,1)}, u32[]{:S(2)}) copy-start(pred[105,1100]{1,0:T(8,128)(4,1)} %constant.176.clone) | copy-start | bytes 346504
  127.2 8.8 %copy-start.27 = (bf16[105,1100]{1,0:T(8,128)(2,1)S(1)}, bf16[105,1100]{1,0:T(8,128)(2,1)}, u32[]{:S(2)}) copy-start(bf16[105,1100]{1,0:T(8,128)(2,1)} %param.43) | copy-start | bytes 693004
  128.1 8.0 %copy-start.10 = (s32[1,1152]{1,0:T(1,128)S(1)}, s32[1,1152]{1,0:T(1,128)}, u32[]{:S(2)}) copy-start(s32[1,1152]{1,0:T(1,128)} %constant.250.width_ref.refs_6_) | copy-start | bytes 13828
  129.0 21.9 %copy-start = (s32[3456,8]{1,0:T(8,128)}, s32[3456,8]{1,0:T(8,128)S(1)}, u32[]{:S(2)}) copy-start(s32[3456,8]{1,0:T(8,128)S(1)} %copy.86.index_ref.refs_2_) | copy-start | bytes 331780
  130.1 21.0 %copy-start.3 = (s32[144,1]{1,0:T(8,128)}, s32[144,1]{1,0:T(8,128)S(1)}, u32[]{:S(2)}) copy-start(s32[144,1]{1,0:T(8,128)S(1)} %copy.87.length_ref.refs_3_) | copy-start | bytes 1732
  130.5 20.6 %copy-start.30 = (f32[2304]{0:T(1024)S(1)}, f32[2304]{0:T(1024)}, u32[]{:S(2)}) copy-start(f32[2304]{0:T(1024)} %constant.179.clone) | copy-start | bytes 27652
  130.5 20.6 %copy-start.31 = (f32[2304]{0:T(1024)S(1)}, f32[2304]{0:T(1024)}, u32[]{:S(2)}) copy-start(f32[2304]{0:T(1024)} %constant.180.clone) | copy-start | bytes 27652
  130.5 20.6 %copy-start.49 = (s32[2304]{0:T(1024)S(1)}, s32[2304]{0:T(1024)}, u32[]{:S(2)}) copy-start(s32[2304]{0:T(1024)} %constant.178.clone) | copy-start | bytes 27652
  136.0 17.6 %copy-start.2 = (bf16[384,128]{1,0:T(8,128)(2,1)}, bf16[384,128]{1,0:T(8,128)(2,1)S(1)}, u32[]{:S(2)}) copy-start(bf16[384,128]{1,0:T(8,128)(2,1)S(1)} %pad.98.table_ref.refs_4_) | copy-start | bytes 294916
  136.1 17.5 %copy-start.1 = (bf16[128,1152]{1,0:T(8,128)(2,1)}, bf16[128,1152]{1,0:T(8,128)(2,1)S(1)}, u32[]{:S(2)}) copy-start(bf16[128,1152]{1,0:T(8,128)(2,1)S(1)} %fusion.130.kernel_ref.refs_5_) | copy-start | bytes 884740
  151.1 11.7 %slice-start.5 = ((s8[10616832]{0:T(1024)(128)(4,1)}), s8[4194304]{0:T(1024)(128)(4,1)S(1)}, s32[]{:S(2)}) async-start(s8[10616832]{0:T(1024)(128)(4,1)} %bitcast.126), calls=%async_computation.6 | async-start | bytes 8388608
  153.6 9.1 %slice-start.6 = ((s8[10616832]{0:T(1024)(128)(4,1)}), s8[4194304]{0:T(1024)(128)(4,1)S(1)}, s32[]{:S(2)}) async-start(s8[10616832]{0:T(1024)(128)(4,1)} %bitcast.126), calls=%async_computation.7 | async-start | bytes 8388608
  159.3 3.5 slice-start.7
  159.7 3.1 copy-start.18
  165.9 3.5 copy-start.17
  166.0 3.4 copy-start.26
  179.0 4.0 copy-start.11
  226.9 4.0 copy-start.54
  226.9 4.0 copy-start.25
  230.9 3.6 copy-start.58
  238.0 3.6 copy-start.19
  238.0 3.6 copy-start.46
  238.0 3.6 copy-start.47
  238.0 3.6 copy-start.48
  241.6 6.3 copy-start.43
  241.6 6.3 copy-start.44
  241.6 6.3 copy-start.45
  315.9 45.1 %copy-start.56 = (s32[768]{0:T(1024)S(1)}, s32[768]{0:T(1024)}, u32[]{:S(2)}) copy-start(s32[768]{0:T(1024)} %constant.186.clone) | copy-start | bytes 9220
  315.9 77.7 %slice-start = ((s8[10092544]{0:T(1024)(128)(4,1)}), s8[4194304]{0:T(1024)(128)(4,1)S(1)}, s32[]{:S(2)}) async-start(s8[10092544]{0:T(1024)(128)(4,1)} %bitcast.117), calls=%async_computation.1 | async-start | bytes 8388608
  315.9 77.7 %slice-start.1 = ((s8[10092544]{0:T(1024)(128)(4,1)}), s8[4194304]{0:T(1024)(128)(4,1)S(1)}, s32[]{:S(2)}) async-start(s8[10092544]{0:T(1024)(128)(4,1)} %bitcast.117), calls=%async_computation.2 | async-start | bytes 8388608
  360.9 32.6 %copy-start.8 = (f32[144,1]{1,0:T(8,128)}, f32[144,1]{1,0:T(8,128)S(1)}, u32[]{:S(2)}) copy-start(f32[144,1]{1,0:T(8,128)S(1)} %get-tuple-element.42) | copy-start | bytes 1732
  361.6 32.0 %slice-start.2 = ((s8[10092544]{0:T(1024)(128)(4,1)}), s8[1703936]{0:T(1024)(128)(4,1)S(1)}, s32[]{:S(2)}) async-start(s8[10092544]{0:T(1024)(128)(4,1)} %bitcast.117), calls=%async_computation.3 | async-start | bytes 3407872
  398.6 7.6 %slice-start.8 = ((s8[10616832]{0:T(1024)(128)(4,1)}), s8[4194304]{0:T(1024)(128)(4,1)S(1)}, s32[]{:S(2)}) async-start(s8[10616832]{0:T(1024)(128)(4,1)} %bitcast.129), calls=%async_computation.9 | async-start | bytes 8388608
  398.6 7.6 %slice-start.9 = ((s8[10616832]{0:T(1024)(128)(4,1)}), s8[4194304]{0:T(1024)(128)(4,1)S(1)}, s32[]{:S(2)}) async-start(s8[10616832]{0:T(1024)(128)(4,1)} %bitcast.129), calls=%async_computation.10 | async-start | bytes 8388608
  408.4 4.2 slice-start.3
  409.1 3.6 slice-start.4
  418.6 8.9 %copy-start.59 = (bf16[144,4608]{1,0:T(8,128)(2,1)S(1)}, bf16[144,4608]{1,0:T(8,128)(2,1)}, u32[]{:S(2)}) copy-start(bf16[144,4608]{1,0:T(8,128)(2,1)} %get-tuple-element.69) | copy-start | bytes 3981316
  440.8 162.2 %copy-start.24 = (pred[105,1100]{1,0:T(8,128)(4,1)S(1)}, pred[105,1100]{1,0:T(8,128)(4,1)}, u32[]{:S(2)}) copy-start(pred[105,1100]{1,0:T(8,128)(4,1)} %constant.176.clone) | copy-start | bytes 346504
  (24 other events, 32.7 us)
Sparse Core Ops, SparseCore 0:
  121.5 190.6 all-gather.2

commit v3 on v2

--- a/solution.py
+++ b/solution.py
@@ -38,8 +38,9 @@
 
 
 class Windows:
-    def __init__(self, flat_rows, width, used, fsdp, dp, by_rows):
+    def __init__(self, flat_rows, width, used, fsdp, dp, by_rows, parts=2):
         owners = fsdp * dp
+        self.parts = parts
         self.width, self.by_rows, self.fsdp, self.dp = width, by_rows, fsdp, dp
         self.entries = flat_rows * LANE // owners
         starts = [o * self.entries // width for o in range(owners)]
@@ -50,11 +51,11 @@
         while (dp * rows) % 16 or (by_rows and (dp // 2 * rows) % 16):
             rows += 1
         self.rows = rows
-        self.columns = up_to(width, LANE) if by_rows else 2 * up_to(-(-width // 2), LANE)
+        self.columns = up_to(width, LANE) if by_rows else parts * up_to(-(-width // parts), LANE)
         self.block = (
-            (dp // 2 * rows, self.columns) if by_rows else (dp * rows, self.columns // 2)
-        )
-        self.shape = (fsdp, 2) + self.block if by_rows else (2, fsdp) + self.block
+            (dp // 2 * rows, self.columns) if by_rows else (dp * rows, self.columns // parts)
+        )
+        self.shape = (fsdp, 2) + self.block if by_rows else (parts, fsdp) + self.block
 
         def row_map(order):
             rows_of = [
@@ -94,8 +95,8 @@
         joined = jnp.concatenate(parts, axis=0)
         if self.by_rows:
             return joined.reshape((2,) + self.block)
-        half = self.columns // 2
-        return jnp.stack([joined[:, :half], joined[:, half:]])
+        part = self.columns // self.parts
+        return jnp.stack([joined[:, p * part : (p + 1) * part] for p in range(self.parts)])
 
     def to_flat(self, window, dp_at, fsdp_at):
         shift = lax.rem((dp_at * self.fsdp + fsdp_at) * self.entries, self.width)
@@ -828,13 +829,183 @@
     return total
 
 
+class Line:
+    def __init__(self, n):
+        self.at = Place()
+        self.length = n // 4
+        self.me = 2 * self.at.z + self.at.c
+
+    def peer(self, z, other_core=False):
+        at = self.at
+        return (at.d + (1 - 2 * at.c if other_core else 0), at.f + 4 * (z - at.z))
+
+    def others(self, body):
+        def step(z, _):
+            pl.when(z != self.at.z)(functools.partial(body, z))
+            return 0
+
+        lax.fori_loop(0, self.length, step, 0)
+
+    def chips(self, body):
+        def step(z, _):
+            body(z)
+            return 0
+
+        lax.fori_loop(0, self.length, step, 0)
+
+    def greet(self, across, both_cores):
+        barrier = pltpu.get_barrier_semaphore()
+
+        def signal(target):
+            pl.semaphore_signal(barrier, inc=1, device_id=target, device_id_type=MESH)
+
+        signal(self.at.sibling)
+        count = 1
+        if across:
+            signal(self.at.partner1)
+            signal(self.at.partner3)
+            count += 2
+
+        def chip(z):
+            signal(self.peer(z))
+            if both_cores:
+                signal(self.peer(z, True))
+
+        self.others(chip)
+        pl.semaphore_wait(barrier, count + (self.length - 1) * (2 if both_cores else 1))
+
+
+class Semaphores:
+    def __init__(self, ref, size):
+        self.ref, self.size = ref, size
+
+    def __call__(self, kind, index):
+        return self.ref.at[kind * self.size + index]
+
+
+HIDDEN_CHUNKS = ((0, 48), (48, 96), (96, 128), (128, 144))
+
+
+def hidden_chunks(rows):
+    return [(a, min(b, rows)) for a, b in HIDDEN_CHUNKS if a < rows] + (
+        [(HIDDEN_CHUNKS[-1][1], rows)] if rows > HIDDEN_CHUNKS[-1][1] else []
+    )
+
+
 def lstm_forward_kernel(
-    batch, x_ref, w_ref, h0_ref, c0_ref, keep_ref, *outs
+    batch, n, x_ref, w_ref, h0_ref, c0_ref, keep_ref, extra_ref, own_ref, *refs
 ):
-    hp_ref, cp_ref, i_ref, f_ref, u_ref, o_ref, t_ref, h_ref = outs
+    hp_ref, cp_ref, i_ref, f_ref, u_ref, o_ref, t_ref, hall_ref, part_ref = refs[:9]
+    hidden, soft_sems, hidden_sems = refs[9:]
+    line = Line(n)
+    at, length = line.at, line.length
+    rows_all = x_ref.shape[0]
+    chunks = hidden_chunks(rows_all)
+    RECV, TO_LINE, TO_NEAR, TO_LAST, LOCAL = range(5)
+    sem = Semaphores(soft_sems, n)
+    H_RECV, H_LINE, H_SIB = range(3)
+    hsem = Semaphores(hidden_sems, 2 * length * len(chunks))
+
+    def column(z):
+        return at.f + 4 * (z - at.z)
+
+    def to_line(z):
+        return remote(
+            own_ref.at[2 * z + at.c],
+            part_ref.at[at.f],
+            sem(TO_LINE, z),
+            sem(RECV, at.f),
+            line.peer(z),
+        )
+
+    def pass_on(kind, index, slot, target, own=False):
+        return remote(
+            own_ref.at[line.me] if own else part_ref.at[slot],
+            part_ref.at[slot],
+            sem(kind, index),
+            sem(RECV, slot),
+            target,
+        )
+
+    def landed(slot):
+        pass_on(TO_NEAR, 0, slot, at.partner1).wait_recv()
+
+    local = pltpu.make_async_copy(own_ref.at[line.me], part_ref.at[at.f], sem(LOCAL, 0))
+
+    def event_begin():
+        line.others(lambda z: to_line(z).start())
+        pass_on(TO_NEAR, at.z, at.f, at.partner1, True).start()
+        pass_on(TO_LAST, at.z, at.f, at.partner3, True).start()
+        local.start()
+
+    def event_line():
+        def chip(z):
+            landed(column(z))
+            pass_on(TO_NEAR, z, column(z), at.partner1).start()
+            pass_on(TO_LAST, z, column(z), at.partner3).start()
+
+        line.others(chip)
+
+    def event_near():
+        def chip(z):
+            slot = column(z) + at.flip1
+            landed(slot)
+            pass_on(TO_LAST, length + z, slot, at.partner3).start()
+
+        line.chips(chip)
+
+    def event_end():
+        def chip(z):
+            landed(column(z) + at.flip3)
+            landed(column(z) + at.flip1 + at.flip3)
+            pass_on(TO_NEAR, z, column(z), at.partner1).wait_send()
+            pass_on(TO_LAST, z, column(z), at.partner3).wait_send()
+            pass_on(TO_LAST, length + z, column(z), at.partner3).wait_send()
+
+        line.chips(chip)
+        line.others(lambda z: to_line(z).wait_send())
+        local.wait()
+
+    def chunk_copy(k, member, kind, index, target):
+        begin, end = chunks[k]
+        here = hall_ref.at[member, pl.ds(begin, end - begin), :]
+        return remote(
+            here,
+            here,
+            hsem(kind, index * len(chunks) + k),
+            hsem(H_RECV, member * len(chunks) + k),
+            target,
+        )
+
+    def chunk_out(k):
+        begin, end = chunks[k]
+        hall_ref[line.me, begin:end, :] = hidden[begin:end, :].astype(BF)
+        line.others(lambda z: chunk_copy(k, line.me, H_LINE, z, line.peer(z)).start())
+        chunk_copy(k, line.me, H_SIB, at.z, at.sibling).start()
+
+    def chunk_pass(k):
+        def chip(z):
+            member = 2 * z + at.c
+            chunk_copy(k, member, H_SIB, z, at.sibling).wait_recv()
+            chunk_copy(k, member, H_SIB, z, at.sibling).start()
+
+        line.others(chip)
+
+    def chunk_end(k):
+        def chip(z):
+            chunk_copy(k, 2 * z + 1 - at.c, H_SIB, z, at.sibling).wait_recv()
+            chunk_copy(k, 2 * z + at.c, H_SIB, z, at.sibling).wait_send()
+
+        line.chips(chip)
+        line.others(lambda z: chunk_copy(k, line.me, H_LINE, z, line.peer(z)).wait_send())
+
+    line.greet(True, False)
+    event_begin()
     per_tile = 8 // batch
+    tiles = rows_all // 8
     row = lax.broadcasted_iota(jnp.int32, (8, HP), 0)
-    lane = lax.broadcasted_iota(jnp.int32, (8, HP), 1)
+    lane = lax.broadcasted_iota(jnp.int32, (8, LANE), 1)
+    last = HP - LANE
 
     def tile(step, carried):
         h, c = carried
@@ -850,22 +1021,177 @@
             c = f * cp + i * u
             t = jnp.tanh(c)
             h = (o * t).astype(BF).astype(F32)
-            now = (hp, cp, i, f, u, o, t, jnp.where(lane < H, h, jnp.where(lane == H, 1.0, 0.0)))
+            now = (hp, cp, i, f, u, o, t, h)
             if saved is None:
                 saved = now
             else:
                 saved = tuple(jnp.where(row >= part * batch, b, a) for a, b in zip(saved, now))
             h, c = pltpu.roll(h, batch, 0), pltpu.roll(c, batch, 0)
-        for ref, value in zip((hp_ref, cp_ref, i_ref, f_ref, u_ref, o_ref, t_ref, h_ref), saved):
+        for ref, value in zip((hp_ref, cp_ref, i_ref, f_ref, u_ref, o_ref, t_ref), saved):
             ref[rows, :] = value
+        hidden[rows, :last] = saved[-1][:, :last]
+        hidden[rows, last:] = jnp.where(lane < H - last, saved[-1][:, last:], extra_ref[rows, :])
+
+        pl.when(step == tiles // 3)(event_line)
+        pl.when(step == tiles * 2 // 3)(event_near)
+        for k, (_, end) in enumerate(chunks):
+            pl.when(step == end // 8 - 1)(functools.partial(chunk_out, k))
         return h, c
 
-    lax.fori_loop(0, x_ref.shape[0] // 8, tile, (h0_ref[...], c0_ref[...]))
+    lax.fori_loop(0, tiles, tile, (h0_ref[...], c0_ref[...]))
+    for k in range(len(chunks)):
+        chunk_pass(k)
+    event_end()
+    for k in range(len(chunks)):
+        chunk_end(k)
+
+
+def lstm_forward(batch, plan, x, recur, h0, c0, keep, extra, own, collective_id):
+    rows, n = x.shape[0], plan.fsdp
+    members = plan.parts
+    chunks = len(hidden_chunks(rows))
+    vmem = pl.BlockSpec(memory_space=pltpu.VMEM)
+    anywhere = pl.BlockSpec(memory_space=pl.ANY)
+    return pl.pallas_call(
+        functools.partial(lstm_forward_kernel, batch, n),
+        out_shape=[jax.ShapeDtypeStruct((rows, HP), F32)] * 7
+        + [
+            jax.ShapeDtypeStruct((members, rows, HP), BF),
+            jax.ShapeDtypeStruct((n,) + plan.block, BF),
+        ],
+        in_specs=[vmem] * 6 + [anywhere],
+        out_specs=[vmem] * 8 + [anywhere],
+        scratch_shapes=[
+            pltpu.VMEM((rows, HP), F32),
+            pltpu.SemaphoreType.DMA((5 * n,)),
+            pltpu.SemaphoreType.DMA((3 * members * chunks,)),
+        ],
+        compiler_params=pltpu.CompilerParams(
+            collective_id=collective_id, has_side_effects=True, vmem_limit_bytes=48 * 2**20
+        ),
+    )(x, recur, h0, c0, keep, extra, own)
 
 
 def lstm_backward_kernel(
-    batch, dh_ref, w_ref, keep_ref, cp_ref, i_ref, f_ref, u_ref, o_ref, t_ref, dz_ref
+    batch,
+    n,
+    dh_ref,
+    w_ref,
+    keep_ref,
+    cp_ref,
+    i_ref,
+    f_ref,
+    u_ref,
+    o_ref,
+    t_ref,
+    grad_ref,
+    dz_ref,
+    out_ref,
+    held_near,
+    held_line,
+    from_last,
+    from_near,
+    sems,
 ):
+    line = Line(n)
+    at, length = line.at, line.length
+    LAST, LAST_RECV, NEAR, NEAR_RECV, TO_LINE, LINE_RECV, SIB, SIB_RECV = range(8)
+    sem = Semaphores(sems, 2 * length)
+
+    def slot(z, b1, b3):
+        return 4 * z + at.stride1 * b1 + at.stride3 * b3
+
+    def to_last(z, b1):
+        return remote(
+            grad_ref.at[slot(z, b1, 1 - at.last)],
+            from_last.at[2 * z + b1],
+            sem(LAST, 2 * z + b1),
+            sem(LAST_RECV, 2 * z + b1),
+            at.partner3,
+        )
+
+    def to_near(z):
+        return remote(
+            held_near.at[z], from_near.at[z], sem(NEAR, z), sem(NEAR_RECV, z), at.partner1
+        )
+
+    def to_line(z):
+        return remote(
+            held_line.at[z], out_ref.at[line.me], sem(TO_LINE, z), sem(LINE_RECV, at.z), line.peer(z)
+        )
+
+    def line_arrived(z):
+        here = out_ref.at[2 * z + at.c]
+        remote(here, here, sem(TO_LINE, z), sem(LINE_RECV, z), line.peer(z)).wait_recv()
+
+    def to_sibling(z, other=False):
+        here = out_ref.at[2 * z + (1 - at.c if other else at.c)]
+        return remote(here, here, sem(SIB, z), sem(SIB_RECV, z), at.sibling)
+
+    def event_begin():
+        def chip(z):
+            to_last(z, 1 - at.first).start()
+
+        line.chips(chip)
+
+        def chip_own(z):
+            to_last(z, at.first).start()
+
+        line.chips(chip_own)
+
+    def event_last():
+        def chip(z):
+            b1 = 1 - at.first
+            to_last(z, b1).wait_recv()
+            held_near[z] = (
+                grad_ref[slot(z, b1, at.last)].astype(F32) + from_last[2 * z + b1].astype(F32)
+            ).astype(BF)
+            to_near(z).start()
+
+        line.chips(chip)
+
+    def event_near():
+        def chip(z):
+            to_last(z, at.first).wait_recv()
+            to_near(z).wait_recv()
+            total = (
+                grad_ref[slot(z, at.first, at.last)].astype(F32)
+                + from_last[2 * z + at.first].astype(F32)
+                + from_near[z].astype(F32)
+            ).astype(BF)
+            held_line[z] = total
+
+            @pl.when(z == at.z)
+            def _():
+                out_ref[line.me] = total
+
+            @pl.when(z != at.z)
+            def _():
+                to_line(z).start()
+
+        line.chips(chip)
+        to_sibling(at.z).start()
+
+    def event_line():
+        def chip(z):
+            line_arrived(z)
+            to_sibling(z).start()
+
+        line.others(chip)
+
+    def event_end():
+        def chip(z):
+            to_sibling(z, True).wait_recv()
+            to_sibling(z).wait_send()
+            to_near(z).wait_send()
+            to_last(z, 0).wait_send()
+            to_last(z, 1).wait_send()
+
+        line.chips(chip)
+        line.others(lambda z: to_line(z).wait_send())
+
+    line.greet(True, False)
+    event_begin()
     per_tile = 8 // batch
     tiles = dh_ref.shape[0] // 8
     row = lax.broadcasted_iota(jnp.int32, (8, dz_ref.shape[1]), 0)
@@ -896,121 +1222,260 @@
                 pltpu.roll(dc_carry, 8 - batch, 0),
             )
         dz_ref[rows, :] = saved
+        pl.when(step == tiles // 3)(event_last)
+        pl.when(step == tiles * 2 // 3)(event_near)
+        pl.when(step == tiles - 2)(event_line)
         return dh_carry, dc_carry
 
     zero = jnp.zeros((8, HP), F32)
     lax.fori_loop(0, tiles, tile, (zero, zero))
-
-
-def in_vmem(kernel, out_shapes, *operands):
+    event_end()
+
+
+def lstm_backward(batch, plan, columns, dh, recur_t, keep, states, grad, collective_id):
+    rows, n = dh.shape[0], plan.fsdp
+    length = n // 4
+    vmem = pl.BlockSpec(memory_space=pltpu.VMEM)
     return pl.pallas_call(
-        kernel,
-        out_shape=out_shapes,
-        in_specs=[pl.BlockSpec(memory_space=pltpu.VMEM)] * len(operands),
-        out_specs=jax.tree.map(lambda _: pl.BlockSpec(memory_space=pltpu.VMEM), out_shapes),
-        compiler_params=pltpu.CompilerParams(vmem_limit_bytes=48 * 2**20),
-    )(*operands)
+        functools.partial(lstm_backward_kernel, batch, n),
+        out_shape=[
+            jax.ShapeDtypeStruct((rows, columns), F32),
+            jax.ShapeDtypeStruct((plan.parts,) + plan.block, BF),
+        ],
+        in_specs=[vmem] * 10,
+        out_specs=[vmem] * 2,
+        scratch_shapes=[
+            pltpu.VMEM((length,) + plan.block, BF),
+            pltpu.VMEM((length,) + plan.block, BF),
+            pltpu.VMEM((2 * length,) + plan.block, BF),
+            pltpu.VMEM((length,) + plan.block, BF),
+            pltpu.SemaphoreType.DMA((8 * 2 * length,)),
+        ],
+        compiler_params=pltpu.CompilerParams(
+            collective_id=collective_id, has_side_effects=True, vmem_limit_bytes=48 * 2**20
+        ),
+    )(dh, recur_t, keep, *states, grad)
 
 
 def softmax_kernel(
     vocab,
-    blocks,
+    n,
     h_ref,
-    h_back_ref,
     w_ref,
-    target_ref,
-    scale_ref,
+    map_ref,
+    map_back_ref,
     loss_ref,
     grad_h_ref,
     grad_w_ref,
+    spread_back,
     logits,
-    top,
-    total,
-    picked,
+    grads,
+    stats,
+    for_sibling,
+    from_sibling,
+    for_line,
+    from_line,
+    own_total,
+    sems,
 ):
-    phase, at = pl.program_id(0), pl.program_id(1)
+    line = Line(n)
+    at, length, me = line.at, line.length, line.me
+    members, rows, _ = h_ref.shape
     width = w_ref.shape[-1]
-    rows = h_ref.shape[0]
     w = w_ref[...].reshape(-1, width)
-    column = at * width + lax.broadcasted_iota(jnp.int32, (rows, width), 1)
-    where = pl.ds(pl.multiple_of(at * width, width), width)
-    hit = column == target_ref[...]
-
-    @pl.when((phase == 0) & (at == 0))
-    def _():
-        top[...] = jnp.full_like(top, -1e30)
-        total[...] = jnp.zeros_like(total)
-        picked[...] = jnp.zeros_like(picked)
-
-    @pl.when(phase == 0)
-    def _():
-        now = jnp.where(column < vocab, dot(h_ref[...], w), -1e30)
-        logits[:, where] = now
-        before = top[...]
-        after = jnp.maximum(before, jnp.max(now, axis=1, keepdims=True))
-        total[...] = total[...] * jnp.exp(before - after) + jnp.sum(
-            jnp.exp(now - after), axis=1, keepdims=True
-        )
-        top[...] = after
-        picked[...] += jnp.sum(jnp.where(hit, now, 0.0), axis=1, keepdims=True)
-
-    @pl.when((phase == 1) & (at == 0))
-    def _():
-        log_total = top[...] + jnp.log(total[...])
-        loss_ref[...] = log_total - picked[...]
-        top[...] = log_total
-        grad_h_ref[...] = jnp.zeros_like(grad_h_ref)
-
-    @pl.when(phase == 1)
-    def _():
-        share = jnp.exp(logits[:, where] - top[...])
-        grad = ((share - hit.astype(F32)) * scale_ref[...]).astype(BF)
-        grad_w_ref[...] = dot_rows(h_back_ref[...], grad).astype(BF).reshape(grad_w_ref.shape)
-        grad_h_ref[...] += dot_cols(grad, w)
-
-
-def word_softmax(plan, h, h_back, weights, target, scale):
-    rows, depth = h.shape
+    STAT, STAT_RECV, SIB, SIB_RECV, TO_LINE, LINE_RECV = range(6)
+    sem = Semaphores(sems, members)
+    column = me * width + lax.broadcasted_iota(jnp.int32, (rows, width), 1)
+    real_column = column.astype(F32)
+    words = up_to(rows, LANE)
+    lane = lax.broadcasted_iota(jnp.int32, (rows, LANE), 1)
+    aside = HP - LANE
+
+    def pieces(b):
+        tail = h_ref[b, :, aside:].astype(F32)
+        first = H + 1 - aside
+        target = tail[:, first : first + 1] * 256.0 + tail[:, first + 1 : first + 2]
+        scale = (
+            tail[:, first + 2 : first + 3]
+            + tail[:, first + 3 : first + 4]
+            + tail[:, first + 4 : first + 5]
+        )
+        return target, scale
+
+    line.greet(False, True)
+
+    def forward(b, _):
+        h = h_ref[b]
+        wide = dot(h, map_ref[...]).astype(BF)
+        spread_back[b] = dot(h, map_back_ref[...]).astype(BF)
+        now = jnp.where(column < vocab, dot(wide, w), -1e30)
+        logits[b] = now
+        target, _ = pieces(b)
+        top = jnp.max(now, axis=1, keepdims=True)
+        log_sum = top + jnp.log(jnp.sum(jnp.exp(now - top), axis=1, keepdims=True))
+        picked = jnp.sum(jnp.where(real_column == target, now, 0.0), axis=1, keepdims=True)
+        both = jnp.where(lane == 0, log_sum, jnp.where(lane == 1, picked, 0.0))
+        both = jnp.concatenate([both, jnp.zeros((words - rows, LANE), F32)], axis=0).T
+        stats[me, 0, pl.ds(b, 1), :] = both[0:1, :]
+        stats[me, 1, pl.ds(b, 1), :] = both[1:2, :]
+        return 0
+
+    lax.fori_loop(0, members, forward, 0)
+
+    def stat(member, target):
+        here = stats.at[member]
+        return remote(here, here, sem(STAT, member), sem(STAT_RECV, member), target)
+
+    def stat_out(z):
+        return [
+            remote(
+                stats.at[me], stats.at[me], sem(STAT, 2 * z + core), sem(STAT_RECV, me), target
+            )
+            for core, target in ((at.c, line.peer(z)), (1 - at.c, line.peer(z, True)))
+        ]
+
+    def send_stats(z):
+        for copy in stat_out(z):
+            copy.start()
+
+    line.others(send_stats)
+    to_pair = remote(
+        stats.at[me], stats.at[me], sem(STAT, 2 * at.z + 1 - at.c), sem(STAT_RECV, me), at.sibling
+    )
+    to_pair.start()
+
+    def stats_in(z):
+        for core in (at.c, 1 - at.c):
+            stat(2 * z + core, at.sibling).wait_recv()
+
+    line.others(stats_in)
+    stat(2 * at.z + 1 - at.c, at.sibling).wait_recv()
+    top = stats[0, 0]
+    for q in range(1, members):
+        top = jnp.maximum(top, stats[q, 0])
+    total = jnp.zeros_like(top)
+    picked = jnp.zeros_like(top)
+    for q in range(members):
+        total += jnp.exp(stats[q, 0] - top)
+        picked += stats[q, 1]
+    log_total = top + jnp.log(total)
+    loss_ref[...] = log_total - picked
+    log_columns = jnp.concatenate(
+        [log_total, jnp.zeros((LANE - members, words), F32)], axis=0
+    ).T[:rows]
+
+    def to_sibling(z):
+        return remote(
+            for_sibling.at[z], from_sibling.at[z], sem(SIB, z), sem(SIB_RECV, z), at.sibling
+        )
+
+    def to_line(z):
+        return remote(
+            for_line.at[z], from_line.at[at.z], sem(TO_LINE, z), sem(LINE_RECV, at.z), line.peer(z)
+        )
+
+    def backward(k, _):
+        z = lax.rem(k, length)
+        mine = k >= length
+        b = 2 * z + jnp.where(mine, at.c, 1 - at.c)
+        target, scale = pieces(b)
+        log_sum = jnp.sum(jnp.where(lane == b, log_columns, 0.0), axis=1, keepdims=True)
+        share = jnp.exp(logits[b] - log_sum)
+        grad = ((share - (real_column == target).astype(F32)) * scale).astype(BF)
+        grads[b] = grad
+        back = dot_cols(grad, w)
+
+        @pl.when(jnp.logical_not(mine))
+        def _():
+            for_sibling[z] = back.astype(BF)
+            to_sibling(z).start()
+
+        @pl.when(mine)
+        def _():
+            to_sibling(z).wait_recv()
+            total = back + from_sibling[z].astype(F32)
+
+            @pl.when(z == at.z)
+            def _():
+                own_total[...] = total
+
+            @pl.when(z != at.z)
+            def _():
+                for_line[z] = total.astype(BF)
+                to_line(z).start()
+
+        return 0
+
+    lax.fori_loop(0, 2 * length, backward, 0)
+
+    depth = map_ref.shape[1]
+    unit = 256
+    everything = grads[...].reshape(members * rows, width)
+
+    def weight_grad(m, _):
+        left = spread_back[:, :, pl.ds(pl.multiple_of(m * unit, unit), unit)]
+        result = dot_rows(left.reshape(members * rows, unit), everything).astype(BF)
+        grad_w_ref[pl.ds(m * unit, unit), :] = result
+        return 0
+
+    lax.fori_loop(0, depth // unit, weight_grad, 0)
+
+    def arrived(z):
+        remote(
+            from_line.at[z], from_line.at[z], sem(TO_LINE, z), sem(LINE_RECV, z), line.peer(z)
+        ).wait_recv()
+        own_total[...] += from_line[z].astype(F32)
+
+    line.others(arrived)
+    spread_grad = own_total[...]
+    high = spread_grad.astype(BF)
+    low = (spread_grad - high.astype(F32)).astype(BF)
+    grad_h_ref[...] = dot_cols(high, map_ref[...]) + dot_cols(low, map_ref[...])
+
+    def finish(z):
+        for copy in stat_out(z):
+            copy.wait_send()
+        to_line(z).wait_send()
+
+    line.others(finish)
+    line.chips(lambda z: to_sibling(z).wait_send())
+    to_pair.wait_send()
+
+
+def word_softmax(plan, h, weights, mapping, mapping_back, collective_id):
+    members, rows, depth = h.shape
     n = plan.fsdp
-    per_slot, half = plan.block
-    width = 512
-    while half % width:
-        width -= LANE
-    per_half = half // width
-    whole = lambda p, j: (0, 0)
-    return pl.pallas_call(
-        functools.partial(softmax_kernel, plan.width, 2 * per_half),
+    spread = mapping.shape[1]
+    per_slot, width = plan.block
+    words = up_to(rows, LANE)
+    length = members // 2
+    vmem = pl.BlockSpec(memory_space=pltpu.VMEM)
+    loss, grad_h, grad_w = pl.pallas_call(
+        functools.partial(softmax_kernel, plan.width, n),
         out_shape=[
-            jax.ShapeDtypeStruct((rows, 1), F32),
+            jax.ShapeDtypeStruct((members, words), F32),
             jax.ShapeDtypeStruct((rows, depth), F32),
-            jax.ShapeDtypeStruct(plan.shape, BF),
+            jax.ShapeDtypeStruct((spread, width), BF),
         ],
-        grid=(2, 2 * per_half),
-        in_specs=[
-            pl.BlockSpec((rows, depth), whole),
-            pl.BlockSpec((rows, depth), whole),
-            pl.BlockSpec(
-                (n, 1, per_slot, width), lambda p, j: (0, j // per_half, 0, j % per_half)
-            ),
-            pl.BlockSpec((rows, 1), whole),
-            pl.BlockSpec((rows, 1), whole),
+        in_specs=[vmem] * 4,
+        out_specs=[vmem] * 3,
+        scratch_shapes=[
+            pltpu.VMEM((members, rows, spread), BF),
+            pltpu.VMEM((members, rows, width), F32),
+            pltpu.VMEM((members, rows, width), BF),
+            pltpu.VMEM((members, 2, members, words), F32),
+            pltpu.VMEM((length, rows, spread), BF),
+            pltpu.VMEM((length, rows, spread), BF),
+            pltpu.VMEM((length, rows, spread), BF),
+            pltpu.VMEM((length, rows, spread), BF),
+            pltpu.VMEM((rows, spread), F32),
+            pltpu.SemaphoreType.DMA((6 * members,)),
         ],
-        out_specs=[
-            pl.BlockSpec((rows, 1), whole),
-            pl.BlockSpec((rows, depth), whole),
-            pl.BlockSpec(
-                (1, n, per_slot, width),
-                lambda p, j: (p * (j // per_half), 0, 0, p * (j % per_half)),
-            ),
-        ],
-        scratch_shapes=[
-            pltpu.VMEM((rows, 2 * half), F32),
-            pltpu.VMEM((rows, 1), F32),
-            pltpu.VMEM((rows, 1), F32),
-            pltpu.VMEM((rows, 1), F32),
-        ],
-        compiler_params=pltpu.CompilerParams(vmem_limit_bytes=48 * 2**20),
-    )(h, h_back, weights, target, scale)
+        compiler_params=pltpu.CompilerParams(
+            collective_id=collective_id, has_side_effects=True, vmem_limit_bytes=56 * 2**20
+        ),
+    )(h, weights, mapping, mapping_back)
+    return loss, grad_h, grad_w.reshape((n,) + plan.block)
 
 
 def shards(
@@ -1044,7 +1509,10 @@
     lstm = Windows(
         lstm_flat.shape[0] * fsdp_count, 4 * H, lstm_used, fsdp_count, dp_count, False
     )
-    soft = Windows(soft_flat.shape[0] * fsdp_count, V, H + 1, fsdp_count, dp_count, False)
+    soft = Windows(
+        soft_flat.shape[0] * fsdp_count, V, H + 1, fsdp_count, dp_count, False, fsdp_count // 2
+    )
+    member = 2 * (fsdp_at // 4) + lax.rem(dp_at, 2)
 
     soft_own = soft.from_flat(soft_flat, fsdp_at)
     highway_all, lstm_all = gather(
@@ -1052,8 +1520,6 @@
         [highway.from_flat(highway_flat, fsdp_at), lstm.from_flat(lstm_flat, fsdp_at)],
         1,
     )
-    highway_all, soft_own = lax.optimization_barrier((highway_all, soft_own))
-    soft_all = lax.all_gather(soft_own, "fsdp", axis=0)
     highway_all = highway_all.reshape(-1, highway.columns)
     lstm_all = lstm_all.reshape(2, -1, lstm.columns // 2)
 
@@ -1184,51 +1650,56 @@
     keep = pad_rows(by_step(1 - resets).astype(F32))[:, None]
     start = init_state.reshape(batch, 2, H)
     start = jnp.pad(start, ((0, 8 - batch), (0, 0), (0, HP - H)))
-    states = [jax.ShapeDtypeStruct((rows, HP), F32)] * 8
-    hp, cp, gate_i, gate_f, gate_u, gate_o, tanh_c, hidden = in_vmem(
-        functools.partial(lstm_forward_kernel, batch),
-        states,
+    row_scale = jnp.broadcast_to(
+        window_grad.reshape(1, batch) / step_count, (step_count, batch)
+    ).reshape(words)
+    goal = by_step(targets)
+    scale_high = lax.reduce_precision(row_scale, 8, 7)
+    scale_mid = lax.reduce_precision(row_scale - scale_high, 8, 7)
+    extra = jnp.stack(
+        [
+            jnp.ones((words,), F32),
+            (goal // 256).astype(F32),
+            (goal % 256).astype(F32),
+            scale_high,
+            scale_mid,
+            row_scale - scale_high - scale_mid,
+        ],
+        axis=1,
+    )
+    aside = H - (HP - LANE)
+    extra = jnp.pad(extra, ((0, rows - words), (aside, LANE - aside - extra.shape[1])))
+    *states, hidden_all, soft_part = lstm_forward(
+        batch,
+        soft,
         from_input,
         recur,
         start[:, 0].astype(BF).astype(F32),
         start[:, 1],
         keep,
-    )
-
-    hidden = hidden.astype(BF)
-    soft_map = one_hot_map(HP, soft.gathered)
-    spread_h = dot(hidden, soft_map).astype(BF)
-    spread_h_back = dot(hidden, one_hot_map(HP, soft.reduced)).astype(BF)
-    row_scale = jnp.broadcast_to(
-        window_grad.reshape(1, batch) / step_count, (step_count, batch)
-    ).reshape(words, 1)
-    word_loss, grad_spread, soft_grad = word_softmax(
+        extra,
+        soft_own,
+        4,
+    )
+    hp = states[0]
+
+    word_loss, grad_hidden, soft_grad = word_softmax(
         soft,
-        spread_h,
-        spread_h_back,
-        soft_all,
-        pad_rows(by_step(targets), -1)[:, None],
-        pad_rows(row_scale),
-    )
-    window_loss = jnp.mean(word_loss[:words, 0].reshape(step_count, batch), axis=0).reshape(
+        hidden_all,
+        soft_part,
+        one_hot_map(HP, soft.gathered),
+        one_hot_map(HP, soft.reduced),
+        5,
+    )
+    word_loss = lax.dynamic_index_in_dim(word_loss, member, 0, keepdims=False)
+    window_loss = jnp.mean(word_loss[:words].reshape(step_count, batch), axis=0).reshape(
         micro_count, streams
     )
-    grad_hidden = compress(grad_spread, soft_map)
-    soft_part = reduce_scatter([soft], [soft_grad], 2)[0]
-
-    dz = in_vmem(
-        functools.partial(lstm_backward_kernel, batch),
-        jax.ShapeDtypeStruct((rows, lstm.columns), F32),
-        grad_hidden,
-        recur_t,
-        keep,
-        cp,
-        gate_i,
-        gate_f,
-        gate_u,
-        gate_o,
-        tanh_c,
-    ).astype(BF)
+
+    dz, soft_part = lstm_backward(
+        batch, soft, lstm.columns, grad_hidden, recur_t, keep, states[1:], soft_grad, 6
+    )
+    dz = dz.astype(BF)
     half = lstm.columns // 2
     lstm_in = jnp.concatenate(
         [
@@ -1307,12 +1778,19 @@
     def own_window(plan, part):
         if dp_count > 2:
             groups = [list(range(h, dp_count, 2)) for h in range(2)]
-            part = lax.psum(part, "dp", axis_index_groups=groups)
+            part = lax.psum(part.astype(F32), "dp", axis_index_groups=groups)
         if plan.by_rows:
             at = dp_at // 2
         else:
-            part = jnp.concatenate([part[0], part[1]], axis=1)
             at = dp_at
+            part = jnp.concatenate(
+                [
+                    lax.dynamic_slice_in_dim(part[p], at * plan.rows, plan.rows, 0)
+                    for p in range(plan.parts)
+                ],
+                axis=1,
+            ).astype(F32)
+            return plan.to_flat(part, dp_at, fsdp_at)
         window = lax.dynamic_slice_in_dim(part, at * plan.rows, plan.rows, 0)
         return plan.to_flat(window, dp_at, fsdp_at)
 

time: 755 us -> 607 us (0.80)
  the two profiles are of different devices: /device:TPU:21 before, /device:TPU:0 now
where the time goes in v3:
time: 607 us; the launch traced here: 597 us
  Pallas kernels  418 us (69%)
  matrix products  81.4 us (13%)
  local copies, waits for them, and re-layouts  68.8 us (11%)
  other arithmetic  26.1 us (4%)
    pallas_call x1, Pallas kernels, tail(): pl.pallas_call(functools.partial(tail_kernel, plans, words // WORD_BLOCK)...  170 us
    pallas_call x1, Pallas kernels, gather(): pl.pallas_call(functools.partial(gather_kernel, plans), out_shape=[jax.Sh...  99.2 us
    pallas_call x1, Pallas kernels, lstm_backward(): pl.pallas_call(functools.partial(lstm_backward_kernel, batch, n), out_sha...  44.5 us
    pallas_call x1, Pallas kernels, word_softmax(): pl.pallas_call(functools.partial(softmax_kernel, plan.width, n), out_shap...  44.5 us
    pallas_call x1, Pallas kernels, lstm_forward(): pl.pallas_call(functools.partial(lstm_forward_kernel, batch, n), out_shap...  44.3 us
    dot_general x12, matrix products, dot(): return jnp.dot(left, right, preferred_element_type=F32)  39 us
    dynamic_update_slice x6, local copies, waits for them, and re-layouts, from_flat(): lax.dynamic_update_slice(jnp.zeros((self.rows * self.width,), BF), flat[j...  22.3 us
    dot_general x3, matrix products, dot_rows(): lax.dot_general(left, right, (((0,), (0,)), ((), ())), preferred_element_...  19.3 us

profile of v3, /device:TPU:0, one launch (start us, length us, event | category | flops | bytes accessed | tf_op | source)
XLA Modules:
  0.0 597.3 jit_solution(158826239365133684)
XLA Ops:
  0.7 1.1 slice_bitcast_fusion.21
  1.8 2.7 dynamic_update_slice.21
  5.0 2.7 dynamic_update_slice.20
  9.3 2.9 dynamic_update_slice.19
  12.9 2.9 dynamic_update_slice.18
  17.4 99.2 %shard_map.370 = (bf16[16,2,144,1152]{3,2,1,0:T(8,128)(2,1)}, bf16[2,16,112,1408]{3,2,1,0:T(8,128)(2,1)}) custom-call(bf16[2,144,1152]{2,1,0:T(8,128)(2,1)} %bitcast.161, bf16[2,112,1408]{2,1,0:T(8,128)(2,1)} %pad_maximum_fusion.4.refs_1_), custom_call_target="tpu_custom_call" | custom-call | tf_op jit(solution)/shard_map/pallas_call | solution.py:337
  116.6 3.5 convolution_convert_fusion.5
  120.2 3.7 convolution_convert_fusion.6
  123.8 2.3 pad_maximum_fusion.1.w_ref
  126.3 2.8 slice.287
  136.0 14.9 %shard_map.369 = bf16[144,1152]{1,0:T(8,128)(2,1)S(1)} custom-call(s32[3456,8]{1,0:T(8,128)S(1)} %copy.91.index_ref.refs_2_, s32[144,1]{1,0:T(8,128)S(1)} %copy.92.length_ref.refs_3_, bf16[384,128]{1,0:T(8,128)(2,1)S(1)} %pad.95.table_ref.refs_4_, bf16[128,1152]{1,0:T(8,128)(2,1)S(1)} %fusion.118.kernel_ref.refs_5_, s32[1,1152]{1,0:T(1,128)S(1)} %copy-done.5), custom_call_target="tpu_custom_call" | custom-call | tf_op jit(solution)/shard_map/pallas_call | solution.py:1577
  151.0 2.5 multiply_convert_fusion.7
  153.5 4.5 fusion.48
  159.6 2.7 multiply_convert_fusion.5
  162.3 2.1 fusion.26
  166.2 2.8 fusion.33
  169.0 8.5 %fusion.147 = (bf16[1,16,112,1408]{3,2,1,0:T(8,128)(2,1)}, bf16[1,16,112,1408]{3,2,1,0:T(8,128)(2,1)}) fusion(bf16[2,16,112,1408]{3,2,1,0:T(8,128)(2,1)} %get-tuple-element.39), kind=kLoop, calls=%fused_computation.275 | loop fusion | bytes 20185088 | tf_op jit(solution)/shard_map/slice | solution.py:1632
  177.6 3.6 fusion.151
  182.7 1.2 slice_bitcast_fusion.13
  183.9 3.8 dynamic_update_slice.23
  189.3 7.3 %dynamic_update_slice.22 = bf16[240000]{0:T(1024)(128)(2,1)} dynamic-update-slice(bf16[240000]{0:T(1024)(128)(2,1)} %broadcast.248.clone.1, bf16[203520]{0:T(1024)(128)(2,1)S(1)} %get-tuple-element.92, s32[]{:T(128)S(6)} %select_n.158) | dynamic-update-slice | bytes 814084 | tf_op jit(solution)/shard_map/dynamic_update_slice | solution.py:89
  196.6 1.7 reshape.397
  199.7 44.3 %shard_map.371 = (f32[144,768]{1,0:T(8,128)S(1)}, f32[144,768]{1,0:T(8,128)S(1)}, f32[144,768]{1,0:T(8,128)S(1)}, f32[144,768]{1,0:T(8,128)S(1)}, f32[144,768]{1...) custom-call(f32[144,2816]{1,0:T(8,128)S(1)} %pad_maximum_fusion.3.x_, ...), custom_call_target="tpu_custom_call" | custom-call | tf_op jit(solution)/shard_map/pallas_call | solution.py:1055
  244.0 2.3 fusion.34
  246.3 44.5 %shard_map.372 = (f32[8,256]{1,0:T(8,128)}, f32[144,768]{1,0:T(8,128)}, bf16[768,1280]{1,0:T(8,128)(2,1)}) custom-call(bf16[8,144,768]{2,1,0:T(8,128)(2,1)} %get-tuple-element.40.h_ref, bf16[16,48,1280]{2,1,0:T(8,128)(2,1)} %get-tuple-element.41.w_ref, bf16[768,768]{1,0:T(8,128)(2,1)} %get-tuple-element.121.map_ref, ...), custom_call_target="tpu_custom_call" | custom-call | tf_op jit(solution)/shard_map/pallas_call | solution.py:1453
  290.8 3.5 convolution_convert_fusion.3
  294.3 3.5 convolution_convert_fusion.4
  297.7 2.4 pad_maximum_fusion.2.w_ref
  300.1 44.5 %shard_map.373 = (f32[144,2816]{1,0:T(8,128)S(1)}, bf16[8,48,1280]{2,1,0:T(8,128)(2,1)S(1)}) custom-call(f32[144,768]{1,0:T(8,128)S(1)} %copy-done.4, bf16[2816,768]{1,0:T(8,128)(2,1)} %pad_maximum_fusion.2.w_ref, f32[144,1]{1,0:T(8,128)S(1)} %copy.97.keep_ref, f32[144,768]{1,0:T(8,128)S(1)} %get-tuple-element.44.cp_ref, ...), custom_call_target="tpu_custom_call" | custom-call | tf_op jit(solution)/shard_map/pallas_call | solution.py:1239
  351.4 1.6 reshape.412
  353.0 2.5 dynamic-slice_bitcast_fusion
  355.6 3.1 fusion.28
  358.8 3.1 reduce-precision_convert_fusion.2
  361.9 1.3 fusion.23
  364.7 2.1 fusion.24
  367.6 2.5 fusion.4
  371.4 1.9 fusion.100
  374.1 2.0 fusion.8
  376.2 1.1 fusion.81.refs_7_
  377.7 2.8 fusion.32
  380.5 4.0 convolution_convert_fusion.2
  384.5 3.9 convolution_convert_fusion.1
  388.4 8.7 %pad_maximum_fusion.refs_1_ = bf16[2,16,112,1408]{3,2,1,0:T(8,128)(2,1)} fusion(bf16[1,16,112,1408]{3,2,1,0:T(8,128)(2,1)} %bitcast.147, bf16[1,16,112,1408]{3,2,1,0:T(8,128)(2,1)} %bitcast.146), kind=kLoop, calls=%fused_computation.17 | loop fusion | flops 5046272 | bytes 20185088 | tf_op jit(solution)/shard_map/stack | solution.py:1714
  397.2 4.8 multiply_convert_fusion.1
  402.1 5.0 multiply_convert_fusion.3
  407.1 11.4 %convolution_convert_fusion = bf16[4608,1152]{1,0:T(8,128)(2,1)} fusion(bf16[144,4608]{1,0:T(8,128)(2,1)S(1)} %get-tuple-element.74, bf16[144,4608]{1,0:T(8,128)(2,1)S(1)} %get-tuple-element.73, bf16[144,4608]{1,0:T(8,128)(2,1)S(1)} %get-tuple-element.72, bf16[144,4608]{1,0:T(8,128)(2,1)S(1)} %get-tuple-element.71, bf16[144,1152]{1,0:T(8,128)(2,1)S(1)} %copy-done.27, ...), kind=kOutput, calls=%fused_computation.4 | convolution fusion | flops 6147145728 | bytes 17252352 | tf_op jit(solution)/shard_map/dot_general | solution.py:33
  418.5 170.3 %shard_map.374 = (f32[2,16,8,640]{3,2,1,0:T(8,128)}, f32[144,1152]{1,0:T(8,128)}, f32[2,112,1408]{2,1,0:T(8,128)}) custom-call(bf16[16,2,144,1152]{3,2,1,0:T(8,128)(2,1)} %bitcast.150, bf16[2,16,112,1408]{3,2,1,0:T(8,128)(2,1)} %pad_maximum_fusion.refs_1_, s32[3456,8]{1,0:T(8,128)} %copy-done, s32[144,1]{1,0:T(8,128)} %copy-done.3, ...), custom_call_target="tpu_custom_call" | custom-call | tf_op jit(solution)/shard_map/pallas_call | solution.py:784
  588.8 1.4 fusion.148
  (282 shorter events, 36.1 us)
Async XLA Ops:
  5.0 4.2 copy-start.17
  12.2 104.4 %copy-start.63 = (s32[672]{0:T(1024)S(1)}, s32[672]{0:T(1024)}, u32[]{:S(2)}) copy-start(s32[672]{0:T(1024)} %constant.234.clone) | copy-start | bytes 8068
  120.1 6.0 %slice-start.2 = ((s8[10616832]{0:T(1024)(128)(4,1)}), s8[4194304]{0:T(1024)(128)(4,1)S(1)}, s32[]{:S(2)}) async-start(s8[10616832]{0:T(1024)(128)(4,1)} %bitcast.162), calls=%async_computation.2 | async-start | bytes 8388608
  120.1 6.0 %slice-start.3 = ((s8[10616832]{0:T(1024)(128)(4,1)}), s8[4194304]{0:T(1024)(128)(4,1)S(1)}, s32[]{:S(2)}) async-start(s8[10616832]{0:T(1024)(128)(4,1)} %bitcast.162), calls=%async_computation.3 | async-start | bytes 8388608
  123.8 2.5 slice-start.4
  126.3 2.8 copy-start.47
  126.3 3.0 copy-start.33
  129.1 6.7 %copy-start.18 = (pred[105,1100]{1,0:T(8,128)(4,1)S(1)}, pred[105,1100]{1,0:T(8,128)(4,1)}, u32[]{:S(2)}) copy-start(pred[105,1100]{1,0:T(8,128)(4,1)} %constant.225.clone) | copy-start | bytes 346504
  129.1 6.8 %copy-start.32 = (bf16[105,1100]{1,0:T(8,128)(2,1)S(1)}, bf16[105,1100]{1,0:T(8,128)(2,1)}, u32[]{:S(2)}) copy-start(bf16[105,1100]{1,0:T(8,128)(2,1)} %param.43) | copy-start | bytes 693004
  129.6 6.4 %copy-start.44 = (bf16[1100]{0:T(1024)(128)(2,1)S(1)}, bf16[1100]{0:T(1024)(128)(2,1)}, u32[]{:S(2)}) copy-start(bf16[1100]{0:T(1024)(128)(2,1)} %param.44) | copy-start | bytes 6604
  129.8 6.2 %copy-start.5 = (s32[1,1152]{1,0:T(1,128)S(1)}, s32[1,1152]{1,0:T(1,128)}, u32[]{:S(2)}) copy-start(s32[1,1152]{1,0:T(1,128)} %constant.297.width_ref.refs_6_) | copy-start | bytes 13828
  131.4 22.1 %copy-start = (s32[3456,8]{1,0:T(8,128)}, s32[3456,8]{1,0:T(8,128)S(1)}, u32[]{:S(2)}) copy-start(s32[3456,8]{1,0:T(8,128)S(1)} %copy.91.index_ref.refs_2_) | copy-start | bytes 331780
  131.5 19.5 %copy-start.35 = (f32[2304]{0:T(1024)S(1)}, f32[2304]{0:T(1024)}, u32[]{:S(2)}) copy-start(f32[2304]{0:T(1024)} %constant.228.clone) | copy-start | bytes 27652
  131.5 19.5 %copy-start.36 = (f32[2304]{0:T(1024)S(1)}, f32[2304]{0:T(1024)}, u32[]{:S(2)}) copy-start(f32[2304]{0:T(1024)} %constant.229.clone) | copy-start | bytes 27652
  131.5 19.5 %copy-start.56 = (s32[2304]{0:T(1024)S(1)}, s32[2304]{0:T(1024)}, u32[]{:S(2)}) copy-start(s32[2304]{0:T(1024)} %constant.227.clone) | copy-start | bytes 27652
  135.8 17.7 %copy-start.2 = (bf16[384,128]{1,0:T(8,128)(2,1)}, bf16[384,128]{1,0:T(8,128)(2,1)S(1)}, u32[]{:S(2)}) copy-start(bf16[384,128]{1,0:T(8,128)(2,1)S(1)} %pad.95.table_ref.refs_4_) | copy-start | bytes 294916
  135.9 17.6 %copy-start.3 = (s32[144,1]{1,0:T(8,128)}, s32[144,1]{1,0:T(8,128)S(1)}, u32[]{:S(2)}) copy-start(s32[144,1]{1,0:T(8,128)S(1)} %copy.92.length_ref.refs_3_) | copy-start | bytes 1732
  136.0 17.5 %copy-start.1 = (bf16[128,1152]{1,0:T(8,128)(2,1)}, bf16[128,1152]{1,0:T(8,128)(2,1)S(1)}, u32[]{:S(2)}) copy-start(bf16[128,1152]{1,0:T(8,128)(2,1)S(1)} %fusion.118.kernel_ref.refs_5_) | copy-start | bytes 884740
  151.0 11.3 %slice-start.5 = ((s8[10616832]{0:T(1024)(128)(4,1)}), s8[4194304]{0:T(1024)(128)(4,1)S(1)}, s32[]{:S(2)}) async-start(s8[10616832]{0:T(1024)(128)(4,1)} %bitcast.164), calls=%async_computation.5 | async-start | bytes 8388608
  153.5 8.8 %slice-start.6 = ((s8[10616832]{0:T(1024)(128)(4,1)}), s8[4194304]{0:T(1024)(128)(4,1)S(1)}, s32[]{:S(2)}) async-start(s8[10616832]{0:T(1024)(128)(4,1)} %bitcast.164), calls=%async_computation.6 | async-start | bytes 8388608
  159.2 3.2 slice-start.7
  159.5 2.7 copy-start.13
  165.5 3.5 copy-start.11
  165.5 3.5 copy-start.20
  165.6 3.5 copy-start.22
  177.6 3.9 copy-start.6
  199.7 44.3 %copy-start.42 = (s32[768]{0:T(1024)S(1)}, s32[768]{0:T(1024)}, u32[]{:S(2)}) copy-start(s32[768]{0:T(1024)} %constant.235.clone) | copy-start | bytes 9220
  199.7 44.3 %copy-start.43 = (s32[768]{0:T(1024)S(1)}, s32[768]{0:T(1024)}, u32[]{:S(2)}) copy-start(s32[768]{0:T(1024)} %constant.236.clone) | copy-start | bytes 9220
  246.3 44.5 %copy-start.64 = (s32[672]{0:T(1024)S(1)}, s32[672]{0:T(1024)}, u32[]{:S(2)}) copy-start(s32[672]{0:T(1024)} %constant.234.clone) | copy-start | bytes 8068
  353.0 11.6 %slice-start.8 = ((s8[10616832]{0:T(1024)(128)(4,1)}), s8[4194304]{0:T(1024)(128)(4,1)S(1)}, s32[]{:S(2)}) async-start(s8[10616832]{0:T(1024)(128)(4,1)} %bitcast.167), calls=%async_computation.8 | async-start | bytes 8388608
  355.6 9.0 %slice-start.9 = ((s8[10616832]{0:T(1024)(128)(4,1)}), s8[4194304]{0:T(1024)(128)(4,1)S(1)}, s32[]{:S(2)}) async-start(s8[10616832]{0:T(1024)(128)(4,1)} %bitcast.167), calls=%async_computation.9 | async-start | bytes 8388608
  358.8 3.1 copy-start.61
  361.9 2.8 slice-start.10
  363.7 3.2 copy-start.24
  366.9 4.6 slice-start
  367.6 2.5 copy-start.8
  367.6 3.9 slice-start.1
  388.4 8.7 %copy-start.53 = (s32[4608]{0:T(1024)S(1)}, s32[4608]{0:T(1024)}, u32[]{:S(2)}) copy-start(s32[4608]{0:T(1024)} %constant.239.clone) | copy-start | bytes 55300
  388.4 8.7 %copy-start.54 = (f32[4608]{0:T(1024)S(1)}, f32[4608]{0:T(1024)}, u32[]{:S(2)}) copy-start(f32[4608]{0:T(1024)} %constant.240.clone) | copy-start | bytes 55300
  388.4 8.7 %copy-start.55 = (f32[4608]{0:T(1024)S(1)}, f32[4608]{0:T(1024)}, u32[]{:S(2)}) copy-start(f32[4608]{0:T(1024)} %constant.241.clone) | copy-start | bytes 55300
  397.2 4.8 copy-start.50
  397.2 4.8 copy-start.51
  397.2 4.8 copy-start.52
  402.0 5.0 copy-start.25
  402.0 5.0 copy-start.27
  402.1 5.0 copy-start.29
  402.1 5.0 copy-start.31
  590.7 2.6 copy-start.15
  (28 other events, 43.0 us)

commit v4 on v3

--- a/solution.py
+++ b/solution.py
@@ -14,6 +14,7 @@
 LANE = 128
 HP = 768
 SLOTS = 24
+CHARS = 51
 HOT = 384
 FILTER_CUTS = (1, 3, 6, 10, 14, 18)
 MESH = pl.DeviceIdType.MESH
@@ -38,33 +39,32 @@
 
 
 class Windows:
+    dtype = BF
+
     def __init__(self, flat_rows, width, used, fsdp, dp, by_rows, parts=2):
         owners = fsdp * dp
         self.parts = parts
-        self.width, self.by_rows, self.fsdp, self.dp = width, by_rows, fsdp, dp
+        self.width, self.by_rows, self.fsdp, self.dp, self.used = width, by_rows, fsdp, dp, used
         self.entries = flat_rows * LANE // owners
-        starts = [o * self.entries // width for o in range(owners)]
-        spans = [
+        self.starts = [o * self.entries // width for o in range(owners)]
+        self.spans = [
             (o * self.entries % width + self.entries - 1) // width + 1 for o in range(owners)
         ]
-        rows = max(spans)
-        while (dp * rows) % 16 or (by_rows and (dp // 2 * rows) % 16):
-            rows += 1
+        unit = 16 if by_rows else 8
+        rows = up_to(max(self.spans), unit)
+        while (dp * rows) % 16:
+            rows += unit
         self.rows = rows
+        self.total = owners * rows
         self.columns = up_to(width, LANE) if by_rows else parts * up_to(-(-width // parts), LANE)
         self.block = (
             (dp // 2 * rows, self.columns) if by_rows else (dp * rows, self.columns // parts)
         )
-        self.shape = (fsdp, 2) + self.block if by_rows else (parts, fsdp) + self.block
-
-        def row_map(order):
-            rows_of = [
-                [starts[o] + i if i < spans[o] and starts[o] + i < used else -1 for i in range(rows)]
-                for o in order
-            ]
-            return np.array(rows_of, np.int32).reshape(-1)
-
-        self.gathered = row_map(range(owners))
+        self.shape = (
+            (self.total, self.columns)
+            if by_rows
+            else (parts, self.total, self.columns // parts)
+        )
         if by_rows:
             order = [
                 (2 * jj + h) * fsdp + f
@@ -74,12 +74,33 @@
             ]
         else:
             order = [d * fsdp + f for f in range(fsdp) for d in range(dp)]
-        self.reduced = row_map(order)
-
-    dtype = BF
+        self.position = [order.index(o) for o in range(owners)]
+        self.gathered = self.row_map(range(owners))
+        self.reduced = self.row_map(order)
+
+    def row_map(self, order):
+        rows_of = [
+            [
+                self.starts[o] + i if i < self.spans[o] and self.starts[o] + i < self.used else -1
+                for i in range(self.rows)
+            ]
+            for o in order
+        ]
+        return np.array(rows_of, np.int32).reshape(-1)
 
     def pick(self, ref, half, slot):
-        return ref.at[slot, half] if self.by_rows else ref.at[half, slot]
+        depth = self.block[0]
+        if self.by_rows:
+            return ref.at[pl.ds(pl.multiple_of((2 * slot + half) * depth, 16), depth)]
+        return ref.at[half, pl.ds(pl.multiple_of(slot * depth, 16), depth)]
+
+    def meeting(self, begin, end):
+        found = []
+        for o, (start, span) in enumerate(zip(self.starts, self.spans)):
+            first, last = max(0, begin - start), min(span, end - start)
+            if first < last:
+                found.append((o, first, last))
+        return found
 
     def from_flat(self, shard, fsdp_at):
         parts = []
@@ -110,14 +131,6 @@
     ).astype(BF)
 
 
-def compress(spread, mapping):
-    high = lax.reduce_precision(spread, 8, 7)
-    both = jnp.concatenate([high.astype(BF), (spread - high).astype(BF)], axis=0)
-    product = dot_cols(both, mapping)
-    count = spread.shape[0]
-    return product[:count] + product[count:]
-
-
 def greet(place_of, lengthwise):
     d, f, z = place_of.d, place_of.f, place_of.z
     barrier = pltpu.get_barrier_semaphore()
@@ -273,96 +286,81 @@
 
             pl.when((z >= 0) & (z < self.lengthwise))(take)
 
-    def steps(self):
-        count = len(self.plans)
-        steps = [functools.partial(self.near, a) for a in range(count)]
+    def steps(self, a):
+        steps = [functools.partial(self.near, a)]
         for distance in range(1, self.lengthwise):
-            steps += [functools.partial(self.line, a, distance) for a in range(count)]
-            steps += [functools.partial(self.across, a, distance - 1) for a in range(count)]
-        steps += [functools.partial(self.across, a, self.lengthwise - 1) for a in range(count)]
-        return steps
-
-    def finish(self):
+            steps += [functools.partial(self.line, a, distance)]
+            steps += [functools.partial(self.across, a, distance - 1)]
+        return steps + [functools.partial(self.across, a, self.lengthwise - 1)]
+
+    def from_sibling(self, a):
+        def block_in(block, _):
+            if self.shared:
+
+                @pl.when(jnp.logical_not(block == self.at.f))
+                def _():
+                    self.arrived(a, block, self.SIB_RECV)
+
+            else:
+                self.arrived(a, block, self.SIB_RECV)
+            return 0
+
+        lax.fori_loop(0, self.n, block_in, 0)
+        if self.shared:
+            for half in (0, 1):
+                self.local(a, half).wait()
+        else:
+            self.local(a, self.at.c).wait()
+
+    def finish(self, a):
         at = self.at
-        for a in range(len(self.plans)):
-
-            def block_done(block, _, a=a):
-                z = block // 4
-
-                def from_sibling():
-                    self.arrived(a, block, self.SIB_RECV)
-                    self.sent(self.SIB, a, block)
-
-                if self.shared:
-                    pl.when(jnp.logical_not(block == at.f))(from_sibling)
-                else:
-                    from_sibling()
-
-                @pl.when(at.last_bit(block) == at.last)
+
+        def block_done(block, _):
+            z = block // 4
+            if self.shared:
+                pl.when(jnp.logical_not(block == at.f))(lambda: self.sent(self.SIB, a, block))
+            else:
+                self.sent(self.SIB, a, block)
+
+            @pl.when(at.last_bit(block) == at.last)
+            def _():
+                self.sent(self.LAST, a, block)
+
+                @pl.when((z <= at.z) & (at.z < self.lengthwise - 1))
                 def _():
-                    self.sent(self.LAST, a, block)
-
-                    @pl.when((z <= at.z) & (at.z < self.lengthwise - 1))
-                    def _():
-                        self.sent(self.UP, a, block)
-
-                    @pl.when((z >= at.z) & (at.z > 0))
-                    def _():
-                        self.sent(self.DOWN, a, block)
-
-                return 0
-
-            lax.fori_loop(0, self.n, block_done, 0)
-            self.sent(self.ONE, a, at.f)
-            if self.shared:
-                for half in (0, 1):
-                    self.local(a, half).wait()
-            else:
-                self.local(a, at.c).wait()
-
-
-def gather_kernel(plans, *refs):
-    count = len(plans)
-    work = Gather(plans, refs[:count], refs[count : 2 * count], refs[2 * count], True)
-    greet(work.at, work.lengthwise)
-    for a in range(count):
-        work.begin(a)
-    for step in work.steps():
-        step()
-    work.finish()
-
-
-def gather(plans, shards, collective_id):
-    count = len(plans)
-    return pl.pallas_call(
-        functools.partial(gather_kernel, plans),
-        out_shape=[jax.ShapeDtypeStruct(plan.shape, plan.dtype) for plan in plans],
-        in_specs=[pl.BlockSpec(memory_space=pl.ANY)] * count,
-        out_specs=[pl.BlockSpec(memory_space=pl.ANY)] * count,
-        scratch_shapes=[Gather.semaphores(plans)],
-        compiler_params=pltpu.CompilerParams(collective_id=collective_id, has_side_effects=True),
-    )(*shards)
+                    self.sent(self.UP, a, block)
+
+                @pl.when((z >= at.z) & (at.z > 0))
+                def _():
+                    self.sent(self.DOWN, a, block)
+
+            return 0
+
+        lax.fori_loop(0, self.n, block_done, 0)
+        self.sent(self.ONE, a, at.f)
 
 
 class Reduce:
     SIB, SIB_RECV, LOAD, NEAR, NEAR_RECV, UP, UP_RECV, DOWN, DOWN_RECV, END = range(10)
 
-    def __init__(self, plans, ins, totals, scratch):
+    def __init__(self, plans, ins, totals, scratch, in_place=False):
         count = len(plans)
-        self.plans, self.ins, self.totals = plans, ins, totals
-        self.held, self.landed, self.flow_up, self.flow_down, self.close, self.cross = (
-            scratch[k * count : (k + 1) * count] for k in range(6)
-        )
-        self.sems = scratch[6 * count]
+        self.plans, self.ins, self.totals, self.in_place = plans, ins, totals, in_place
+        self.held = [None] * count if in_place else scratch[:count]
+        scratch = scratch if in_place else scratch[count:]
+        self.landed, self.flow_up, self.flow_down, self.close, self.cross = (
+            scratch[k * count : (k + 1) * count] for k in range(5)
+        )
+        self.sems = scratch[5 * count]
         self.n = plans[0].fsdp
         self.lengthwise = self.n // 4
         self.at = Place()
 
     @staticmethod
-    def scratch(plans):
+    def scratch(plans, in_place=False):
         n = plans[0].fsdp
         return (
-            [pltpu.VMEM((n,) + plan.block, plan.dtype) for plan in plans] * 2
+            [pltpu.VMEM((n,) + plan.block, plan.dtype) for plan in plans] * (1 if in_place else 2)
             + [pltpu.VMEM((n // 2,) + plan.block, plan.dtype) for plan in plans] * 3
             + [pltpu.VMEM(plan.block, plan.dtype) for plan in plans]
             + [pltpu.SemaphoreType.DMA((10 * len(plans) * n,))]
@@ -375,10 +373,19 @@
         return 4 * z + self.at.stride1 * b1 + self.at.stride3 * b3
 
     def item(self, t):
-        pair, b3 = t // 2, lax.rem(t, 2)
-        half = pair // 2
-        z = jnp.where(lax.rem(pair, 2) == 0, half, self.lengthwise - 1 - half)
+        length = self.lengthwise
+        pair, b3 = t // 2, t % 2
+        z = jnp.int32(0)
+        for here in range(length):
+            order = sorted(range(length), key=lambda there: (-abs(there - here), there))
+            for k, there in enumerate(order):
+                z = jnp.where((self.at.z == here) & (pair == k), there, z)
         return z, b3
+
+    def hold(self, a, block):
+        if self.in_place:
+            return self.plans[a].pick(self.ins[a], self.at.c, block)
+        return self.held[a].at[block]
 
     def to_sibling(self, a, block):
         return remote(
@@ -398,7 +405,7 @@
 
     def to_near(self, a, z, b3):
         return remote(
-            self.held[a].at[self.slot(z, 1 - self.at.first, b3)],
+            self.hold(a, self.slot(z, 1 - self.at.first, b3)),
             self.close[a].at[2 * z + b3],
             self.sem(self.NEAR, a, 2 * z + b3),
             self.sem(self.NEAR_RECV, a, 2 * z + b3),
@@ -407,7 +414,7 @@
 
     def along(self, up, a, z, b3):
         return remote(
-            self.held[a].at[self.slot(z, self.at.first, b3)],
+            self.hold(a, self.slot(z, self.at.first, b3)),
             (self.flow_up if up else self.flow_down)[a].at[2 * z + b3],
             self.sem(self.UP if up else self.DOWN, a, 2 * z + b3),
             self.sem(self.UP_RECV if up else self.DOWN_RECV, a, 2 * z + b3),
@@ -416,7 +423,7 @@
 
     def to_cross(self, a):
         return remote(
-            self.held[a].at[self.slot(self.at.z, self.at.first, 1 - self.at.last)],
+            self.hold(a, self.slot(self.at.z, self.at.first, 1 - self.at.last)),
             self.cross[a],
             self.sem(self.END, a, 0),
             self.sem(self.END, a, 1),
@@ -436,13 +443,13 @@
             lax.fori_loop(0, self.plans[a].block[0] // unit, step, 0)
 
     def add(self, a, block, sources):
-        held = self.held[a]
+        held = self.hold(a, block)
 
         def body(where):
-            total = held[block, where, :].astype(F32)
+            total = held[where, :].astype(F32)
             for ref, at in sources:
                 total += ref[at, where, :].astype(F32)
-            held[block, where, :] = total.astype(held.dtype)
+            held[where, :] = total.astype(held.dtype)
 
         self.rows(a, body)
 
@@ -454,7 +461,8 @@
                 z, b3 = self.item(t)
                 block = self.slot(z, b1, b3)
                 self.to_sibling(a, block).start()
-                self.load(a, block).start()
+                if not self.in_place:
+                    self.load(a, block).start()
                 return 0
 
             lax.fori_loop(0, 2 * self.lengthwise, start, 0)
@@ -462,7 +470,8 @@
     def first_leg(self, a, t):
         z, b3 = self.item(t)
         block = self.slot(z, 1 - self.at.first, b3)
-        self.load(a, block).wait()
+        if not self.in_place:
+            self.load(a, block).wait()
         self.to_sibling(a, block).wait_recv()
         self.add(a, block, [(self.landed[a], block)])
         self.to_near(a, z, b3).start()
@@ -472,7 +481,8 @@
         block = self.slot(z, self.at.first, b3)
         flow = 2 * z + b3
         base = [(self.landed[a], block), (self.close[a], flow)]
-        self.load(a, block).wait()
+        if not self.in_place:
+            self.load(a, block).wait()
         self.to_sibling(a, block).wait_recv()
         self.to_near(a, z, b3).wait_recv()
 
@@ -519,7 +529,7 @@
         block = self.slot(self.at.z, self.at.first, self.at.last)
 
         def body(where):
-            total = self.held[a][block, where, :].astype(F32) + self.cross[a][where, :].astype(F32)
+            total = self.hold(a, block)[where, :].astype(F32) + self.cross[a][where, :].astype(F32)
             self.totals[a][where, :] = total
 
         self.rows(a, body)
@@ -554,88 +564,48 @@
     return copies
 
 
-def reduce_kernel(plans, *refs):
-    count = len(plans)
-    ins, outs, scratch = refs[:count], refs[count : 2 * count], refs[2 * count :]
-    totals = [out if plan.by_rows else out.at[Place().c] for plan, out in zip(plans, outs)]
-    work = Reduce(plans, ins, totals, scratch[:-1])
-    at, items = work.at, 2 * work.lengthwise
-    greet(at, work.lengthwise)
-    for a in range(count):
-        work.begin(a)
-
-    def leg(body, a, begin, end):
-        def step(t, _):
-            body(a, t)
-            return 0
-
-        lax.fori_loop(begin, end, step, 0)
-
-    for a in range(count):
-        leg(work.first_leg, a, 0, items)
-    for a in range(count):
-        leg(work.middle_leg, a, 0, items)
-    for a in range(count):
-        work.cross_over(a)
-    copies = pair_exchange(plans, totals, outs, scratch[-1], at)
-    for a in range(count):
-        work.last_leg(a)
-    for copy in copies:
-        copy.start()
-    for a in range(count):
-        work.finish(a)
-    for copy in copies:
-        copy.wait()
-
-
 def reduce_out(plan):
     return jax.ShapeDtypeStruct(plan.block if plan.by_rows else (2,) + plan.block, F32)
 
 
-def reduce_scatter(plans, grads, collective_id):
-    count = len(plans)
-    return pl.pallas_call(
-        functools.partial(reduce_kernel, plans),
-        out_shape=[reduce_out(plan) for plan in plans],
-        in_specs=[pl.BlockSpec(memory_space=pl.ANY)] * count,
-        out_specs=[pl.BlockSpec(memory_space=pltpu.VMEM)] * count,
-        scratch_shapes=Reduce.scratch(plans) + [pltpu.SemaphoreType.DMA((2 * count,))],
-        compiler_params=pltpu.CompilerParams(
-            collective_id=collective_id, has_side_effects=True, vmem_limit_bytes=60 * 2**20
-        ),
-    )(*grads)
-
-
-def hot_rows(index):
-    lane = lax.broadcasted_iota(jnp.int32, (index.shape[0], HOT), 1)
-    hit = lane == index[:, 0:1]
-    for q in range(1, KMAX + 1):
-        hit = jnp.logical_or(hit, lane == index[:, q : q + 1])
+def hot_rows(codes):
+    count = codes.shape[0]
+    slot = lax.rem(lax.broadcasted_iota(jnp.int32, (count, 1), 0), SLOTS)
+    lane = lax.broadcasted_iota(jnp.int32, (count, HOT), 1)
+    hit = lane == KMAX * CHARS
+    for q in range(KMAX):
+        moved = codes if q == 0 else pltpu.roll(codes, count - q, 0)
+        moved = jnp.where((moved >= 0) & (slot + q < SLOTS), moved + q * CHARS, -1)
+        hit = jnp.logical_or(hit, lane == moved)
     return hit.astype(F32).astype(BF)
 
 
-def conv_forward_kernel(filters, index_ref, length_ref, table_ref, kernel_ref, width_ref, out_ref):
-    words = length_ref.shape[0]
-    windows = dot(hot_rows(index_ref[...]), table_ref[...]).astype(BF)
+def conv_forward_block(filters, codes, lengths, refs, out_ref, where):
+    table_ref, kernel_ref, width_ref = refs
+    words = lengths.shape[0]
+    windows = dot(hot_rows(codes), table_ref[...]).astype(BF)
     chunk = 384
     for at in range(0, kernel_ref.shape[1], chunk):
         columns = slice(at, at + chunk)
         activated = jnp.tanh(dot(windows, kernel_ref[:, columns])).reshape(words, SLOTS, chunk)
-        counts = jnp.maximum(length_ref[...] - width_ref[:, columns] + 1, 1)
+        counts = jnp.maximum(lengths - width_ref[:, columns] + 1, 1)
         position = lax.broadcasted_iota(jnp.int32, (words, SLOTS, chunk), 1)
         inside = position < counts[:, None, :]
         totals = jnp.sum(jnp.where(inside, jnp.exp(activated), 0.0), axis=1)
         pooled = jnp.log(totals) - jnp.log(counts.astype(F32))
         lane = at + lax.broadcasted_iota(jnp.int32, (words, chunk), 1)
-        out_ref[:, columns] = jnp.where(
-            lane < filters, pooled, jnp.where(lane == filters, 1.0, 0.0)
-        ).astype(BF)
-
-
-def conv_backward_block(index, lengths, refs, grad_ref, where, kernel_grad_ref, hot_grad_ref):
+        out_ref[where, columns] = keep_feature(pooled, lane, filters)
+
+
+def keep_feature(value, lane, filters):
+    value = value.astype(BF).astype(F32)
+    return jnp.where(lane < filters, value, jnp.where(lane == filters, 1.0, 0.0))
+
+
+def conv_backward_block(codes, lengths, refs, grad_ref, where, kernel_grad_ref, hot_grad_ref):
     table_ref, kernel_ref, width_ref = refs
     words = lengths.shape[0]
-    hot = hot_rows(index)
+    hot = hot_rows(codes)
     windows = dot(hot, table_ref[...]).astype(BF)
     chunk = 384
     grad_windows = jnp.zeros(windows.shape, F32)
@@ -654,16 +624,6 @@
     hot_grad_ref[...] += dot_rows(hot, grad_windows.astype(BF))
 
 
-def conv_specs(words, filters_padded):
-    return [
-        pl.BlockSpec((words * SLOTS, 8), lambda i: (i, 0)),
-        pl.BlockSpec((words, 1), lambda i: (i, 0)),
-        pl.BlockSpec((HOT, LANE), lambda i: (0, 0)),
-        pl.BlockSpec((LANE, filters_padded), lambda i: (0, 0)),
-        pl.BlockSpec((1, filters_padded), lambda i: (0, 0)),
-    ]
-
-
 class Dense:
     by_rows = False
     dtype = F32
@@ -685,7 +645,7 @@
     conv, rest = plans[0], plans[1:]
     count = len(plans)
     ins, refs = refs[: count - 1], refs[count - 1 :]
-    index_ref, length_ref, table_ref, kernel_ref, width_ref, grad_ref, mask_ref, fold_ref = refs[:8]
+    codes_ref, length_ref, table_ref, kernel_ref, width_ref, grad_ref, mask_ref, fold_ref = refs[:8]
     outs, refs = refs[8 : 8 + count], refs[8 + count :]
     conv_out, rest_outs = outs[0], outs[1:]
     kernel_grad, hot_grad, conv_in, conv_total = refs[:4]
@@ -707,7 +667,7 @@
         words = pl.ds(pl.multiple_of(i * WORD_BLOCK, WORD_BLOCK), WORD_BLOCK)
         slots = pl.ds(pl.multiple_of(i * WORD_BLOCK * SLOTS, WORD_BLOCK * SLOTS), WORD_BLOCK * SLOTS)
         conv_backward_block(
-            index_ref[slots, :],
+            codes_ref[slots, :],
             length_ref[words, :],
             (table_ref, kernel_ref, width_ref),
             grad_ref,
@@ -716,24 +676,27 @@
             hot_grad,
         )
 
-    lead = 2
+    def leg(body, a):
+        def step(t, _):
+            body(a, t)
+            return 0
+
+        lax.fori_loop(0, items, step, 0)
+
+    for a in range(1, count):
+        leg(work.first_leg, a)
 
     def together(t, _):
+        pl.when(t < blocks)(functools.partial(compute, t))
+
         @pl.when(t < items)
         def _():
             for a in range(1, count):
-                work.first_leg(a, t)
-
-        pl.when(t < blocks)(functools.partial(compute, t))
-
-        @pl.when((t >= lead) & (t < items + lead))
-        def _():
-            for a in range(1, count):
-                work.middle_leg(a, t - lead)
+                work.middle_leg(a, t)
 
         return 0
 
-    lax.fori_loop(0, max(items + lead, blocks), together, 0)
+    lax.fori_loop(0, max(items, blocks), together, 0)
 
     wide = kernel_ref.shape[1]
     kernel_grad[:, wide:] = jnp.dot(
@@ -750,15 +713,8 @@
             ]
     work.begin(0)
 
-    def leg(body):
-        def step(t, _):
-            body(0, t)
-            return 0
-
-        lax.fori_loop(0, items, step, 0)
-
-    leg(work.first_leg)
-    leg(work.middle_leg)
+    leg(work.first_leg, 0)
+    leg(work.middle_leg, 0)
     for a in range(count):
         work.cross_over(a)
     work.last_leg(0)
@@ -769,9 +725,10 @@
         work.last_leg(a)
     for copy in copies:
         copy.start()
-    for step in spread.steps():
+    for step in spread.steps(0):
         step()
-    spread.finish()
+    spread.from_sibling(0)
+    spread.finish(0)
     for a in range(count):
         work.finish(a)
     for copy in copies:
@@ -1255,6 +1212,412 @@
             collective_id=collective_id, has_side_effects=True, vmem_limit_bytes=48 * 2**20
         ),
     )(dh, recur_t, keep, *states, grad)
+
+
+def turned(value, lanes):
+    rows = value.shape[0]
+    if rows < lanes:
+        value = jnp.concatenate([value, jnp.zeros((lanes - rows, value.shape[1]), F32)], axis=0)
+    return value.T
+
+
+def copy_windows(plan, source, target, base, found, place):
+    target[...] = jnp.zeros_like(target)
+    for o, first, last in found:
+        start, to = plan.starts[o] - base, place(o) * plan.rows
+        target[to + first : to + last, :] = source[start + first : start + last, :]
+
+
+def add_windows(plan, source, target, base, found, begin):
+    for o, first, last in found:
+        start, at = plan.starts[o] - base, o * plan.rows - begin
+        target[start + first : start + last, :] += source[at + first : at + last, :]
+
+
+def matrices_of(plan, filters):
+    result = []
+    for m in range(4):
+        base = m * (filters + 1)
+        found = plan.meeting(base, base + filters + 1)
+        result.append((base, found, found[0][0] * plan.rows, (found[-1][0] + 1) * plan.rows))
+    return result
+
+
+def head_kernel(plans, filters, blocks, *refs):
+    highway, lstm = plans
+    owns = refs[:2]
+    codes_ref, length_ref, table_ref, kernel_ref, width_ref = refs[2:7]
+    highway_out, lstm_out, x_ref, recur_ref = refs[7:11]
+    features, trans_refs, gate_refs = refs[11:14], refs[14:16], refs[16:18]
+    highway_w, lstm_w, turned_ref, wide, recur_sum, gather_sems, out_sems = refs[18:]
+    rows, fp = features[0].shape
+    words = turned_ref.shape[1]
+    work = Gather(plans, owns, (highway_w, lstm_w), gather_sems, True)
+    length = work.lengthwise
+    greet(work.at, length)
+
+    def conv(begin, end):
+        def block(i, _):
+            at = pl.ds(pl.multiple_of(i * WORD_BLOCK, WORD_BLOCK), WORD_BLOCK)
+            slots = pl.ds(
+                pl.multiple_of(i * WORD_BLOCK * SLOTS, WORD_BLOCK * SLOTS), WORD_BLOCK * SLOTS
+            )
+            conv_forward_block(
+                filters,
+                codes_ref[slots, :],
+                length_ref[at, :],
+                (table_ref, kernel_ref, width_ref),
+                features[0],
+                at,
+            )
+            return 0
+
+        lax.fori_loop(begin, end, block, 0)
+
+    chunk = 384
+
+    def layer_sum(m, wide=wide):
+        base, found, begin, end = matrices[m]
+        copy_windows(
+            highway, turned_ref, wide.at[: end - begin], base, found, lambda o: o - found[0][0]
+        )
+        target = (trans_refs if m % 2 == 0 else gate_refs)[m // 2]
+
+        def columns(j, _):
+            where = pl.ds(pl.multiple_of(j * chunk, chunk), chunk)
+            left = wide[: end - begin, :].astype(BF)
+            target[:, where] = dot_rows(left, highway_w[begin:end, where])[:rows]
+            return 0
+
+        lax.fori_loop(0, fp // chunk, columns, 0)
+
+    def layer(l):
+        turned_ref[:fp, :] = turned(features[l][...], words)
+        layer_sum(2 * l)
+
+    def layer_end(l):
+        layer_sum(2 * l + 1)
+        trans, gate = trans_refs[l][...], jax.nn.sigmoid(gate_refs[l][...])
+        gate_refs[l][...] = gate
+        value = gate * trans * jax.nn.sigmoid(trans) + (1.0 - gate) * features[l][...]
+        lane = lax.broadcasted_iota(jnp.int32, (rows, fp), 1)
+        features[l + 1][...] = keep_feature(value, lane, filters)
+
+    matrices = matrices_of(highway, filters)
+    of_highway, of_lstm = work.steps(0), work.steps(1)
+    count = len(of_highway)
+    work.begin(0)
+    third = -(-blocks // 3)
+    for k in range(3):
+        conv(k * third, min((k + 1) * third, blocks))
+        if k < count:
+            of_highway[k]()
+    late = count - 4
+    for k in range(3, count):
+        if k == max(late, 3):
+            work.begin(1)
+        of_highway[k]()
+    work.from_sibling(0)
+    out_copies = [
+        pltpu.make_async_copy(highway_w, highway_out, out_sems.at[0]),
+        pltpu.make_async_copy(lstm_w, lstm_out, out_sems.at[1]),
+    ]
+    out_copies[0].start()
+    of_lstm[0]()
+    compute = [
+        functools.partial(layer, 0),
+        functools.partial(layer_end, 0),
+        functools.partial(layer, 1),
+        functools.partial(layer_end, 1),
+    ]
+    for k in range(1, max(count, 5)):
+        if k <= 4:
+            compute[k - 1]()
+        if k < count:
+            of_lstm[k]()
+
+    turned_ref[...] = jnp.zeros_like(turned_ref)
+    sub = lax.broadcasted_iota(jnp.int32, (fp, words), 0)
+    turned_ref[:fp, :] = jnp.where(sub < filters, turned(features[2][...], words), 0.0)
+    turned_ref[lstm.used - 1 : lstm.used, :] = jnp.ones((1, words), F32)
+    wide = wide.at[: lstm.total]
+    copy_windows(lstm, turned_ref, wide, 0, lstm.meeting(0, lstm.used), lambda o: o)
+    work.from_sibling(1)
+    out_copies[1].start()
+    left = wide[...].astype(BF)
+    half = lstm.block[1]
+    for h in range(2):
+        x_ref[:, h * half : (h + 1) * half] = dot_rows(left, lstm_w[h])[:rows]
+
+    recur_sum[...] = jnp.zeros_like(recur_sum)
+    depth = lstm.block[0]
+    for h in range(2):
+        for slot in sorted({o // lstm.dp for o, _, _ in lstm.meeting(filters, filters + H)}):
+            piece = lstm_w[h, slot * depth : (slot + 1) * depth, :].astype(F32)
+            for o, first, last in lstm.meeting(filters, filters + H):
+                if o // lstm.dp == slot:
+                    start, at = lstm.starts[o] - filters, (o % lstm.dp) * lstm.rows
+                    recur_sum[start + first : start + last, h * half : (h + 1) * half] += piece[
+                        at + first : at + last
+                    ]
+    recur_ref[...] = recur_sum[...].astype(BF)
+    for a in range(2):
+        work.finish(a)
+    for copy in out_copies:
+        copy.wait()
+
+
+def head(plans, filters, own, conv_inputs, rows, fp, collective_id):
+    highway, lstm = plans
+    words = up_to(rows, 2 * LANE)
+    vmem = pl.BlockSpec(memory_space=pltpu.VMEM)
+    anywhere = pl.BlockSpec(memory_space=pl.ANY)
+    feature = jax.ShapeDtypeStruct((rows, fp), F32)
+    matrices = matrices_of(highway, filters)
+    longest = max([lstm.total] + [end - begin for _, _, begin, end in matrices])
+    return pl.pallas_call(
+        functools.partial(head_kernel, plans, filters, rows // WORD_BLOCK),
+        out_shape=[
+            jax.ShapeDtypeStruct(highway.shape, BF),
+            jax.ShapeDtypeStruct(lstm.shape, BF),
+            jax.ShapeDtypeStruct((rows, lstm.columns), F32),
+            jax.ShapeDtypeStruct((HP, lstm.columns), BF),
+        ]
+        + [feature] * 7,
+        in_specs=[anywhere] * 2 + [vmem] * 5,
+        out_specs=[anywhere] * 2 + [vmem] * 9,
+        scratch_shapes=[
+            pltpu.VMEM(highway.shape, BF),
+            pltpu.VMEM(lstm.shape, BF),
+            pltpu.VMEM((up_to(max(lstm.used, fp), LANE), words), F32),
+            pltpu.VMEM((longest, words), F32),
+            pltpu.VMEM((HP, lstm.columns), F32),
+            Gather.semaphores(plans),
+            pltpu.SemaphoreType.DMA((2,)),
+        ],
+        compiler_params=pltpu.CompilerParams(
+            collective_id=collective_id, has_side_effects=True, vmem_limit_bytes=60 * 2**20
+        ),
+    )(*own, *conv_inputs)
+
+
+def highway_backward_kernel(plans, filters, *refs):
+    highway, lstm = plans
+    dz_ref, hp_ref = refs[:2]
+    features, trans_refs, gate_refs = refs[2:5], refs[5:7], refs[7:9]
+    highway_all, lstm_all = refs[9:11]
+    grad_out, feature_grad, total_out = refs[11:14]
+    lstm_grad, highway_w, lstm_w, turned_ref, wide, back, dz, pairs = refs[14:22]
+    staged, carry, load_sems, pair_sems, out_sems = refs[22:27]
+    rows, fp = features[0].shape
+    words = turned_ref.shape[1]
+    at = Place()
+    work = Reduce([lstm], [lstm_grad], [total_out.at[at.c]], refs[27:], True)
+    length, items = work.lengthwise, 2 * work.lengthwise
+    matrices = matrices_of(highway, filters)
+    half = lstm.block[1]
+    of_input = lstm.meeting(0, filters)
+    input_rows = lstm_w.shape[0]
+
+    def layer_rows(l):
+        begin, end = matrices[2 * l][2], matrices[2 * l + 1][3]
+        return begin, end
+
+    def load_layer(l):
+        begin, end = layer_rows(l)
+        return pltpu.make_async_copy(
+            highway_all.at[pl.ds(begin, end - begin)],
+            highway_w.at[pl.ds(0, end - begin)],
+            load_sems.at[l],
+        )
+
+    def load_lstm(h):
+        return pltpu.make_async_copy(
+            lstm_all.at[h, pl.ds(0, input_rows)], lstm_w, load_sems.at[2 + h]
+        )
+
+    load_layer(1).start()
+    load_lstm(0).start()
+    greet(at, length)
+
+    dz[...] = jnp.zeros_like(dz)
+    dz[:rows, :] = dz_ref[...].astype(BF)
+    lane = lax.broadcasted_iota(jnp.int32, (rows, HP), 1)
+    hidden = jnp.where(lane < H, hp_ref[...], jnp.where(lane == H, 1.0, 0.0))
+    sub = lax.broadcasted_iota(jnp.int32, (fp, words), 0)
+    turned_ref[:fp, :] = jnp.where(sub < filters, turned(features[2][...], words), 0.0)
+    kept = up_to(H + 1, 8)
+    turned_ref[filters : filters + kept, :] = turned(hidden, words)[:kept]
+    copy_windows(
+        lstm,
+        turned_ref,
+        wide.at[: lstm.total],
+        0,
+        lstm.meeting(0, lstm.used),
+        lambda o: lstm.position[o],
+    )
+    unit = lstm.total // (2 * length)
+
+    def lstm_weights(i, _):
+        where = pl.ds(pl.multiple_of(i * unit, unit), unit)
+        left = wide[where, :].astype(BF)
+        for h in range(2):
+            lstm_grad[h, where, :] = dot(left, dz[:, h * half : (h + 1) * half]).astype(BF)
+        return 0
+
+    lax.fori_loop(0, 2 * length, lstm_weights, 0)
+    work.begin(0)
+
+    lane = lax.broadcasted_iota(jnp.int32, (rows, fp), 1)
+    back[...] = jnp.zeros_like(back)
+    for h in range(2):
+        load_lstm(h).wait()
+        wide[:input_rows, :] = dot_cols(lstm_w[...], dz[:, h * half : (h + 1) * half])
+        if h == 0:
+            load_lstm(1).start()
+        add_windows(lstm, wide, back, 0, of_input, 0)
+    grad = jnp.where(lane < filters, back[...].T[:rows], 0.0)
+
+    def legs(body, begin, end):
+        def step(t, _):
+            body(0, t)
+            return 0
+
+        lax.fori_loop(begin, end, step, 0)
+
+    legs(work.first_leg, 0, items)
+    spots = 8
+
+    def middle(k):
+        legs(work.middle_leg, k * items // spots, (k + 1) * items // spots)
+
+    pairs[...] = jnp.zeros_like(pairs)
+    for l in (1, 0):
+        trans, gate = trans_refs[l][...], gate_refs[l][...]
+        sig = jax.nn.sigmoid(trans)
+        pairs[2 * l, :rows, :] = (grad * gate * sig * (1.0 + trans * (1.0 - sig))).astype(BF)
+        pairs[2 * l + 1, :rows, :] = (
+            grad * (trans * sig - features[l][...]) * gate * (1.0 - gate)
+        ).astype(BF)
+        load_layer(l).wait()
+        back[...] = jnp.zeros_like(back)
+        begin = layer_rows(l)[0]
+        for m in (2 * l, 2 * l + 1):
+            base, found, low, high = matrices[m]
+            result = dot_cols(highway_w[low - begin : high - begin, :], pairs[m])
+            add_windows(highway, result, back, base, found, low)
+            if m % 2 and l:
+                load_layer(0).start()
+            middle(2 * (1 - l) + m % 2)
+        grad = grad * (1.0 - gate) + back[...].T[:rows]
+        grad = jnp.where(lane < filters, grad, 0.0)
+    feature_grad[...] = grad
+
+    chunk = 384
+    size = highway.rows
+    pending, shared = [], None
+    empty = [o for o in range(len(highway.starts)) if all(o != f[0] for m in matrices for f in m[1])]
+    for m in range(4):
+        base, found, low, high = matrices[m]
+        if m % 2 == 0:
+            turned_ref[:fp, :] = turned(features[m // 2][...], words)
+        copy_windows(
+            highway, turned_ref, wide.at[: high - low], base, found, lambda o: o - found[0][0]
+        )
+        for copy in pending:
+            copy.wait()
+        adds = shared == found[0][0]
+        shares = m < 3 and matrices[m + 1][1][0][0] == found[-1][0]
+        count = len(found)
+
+        def columns(j, _):
+            where = pl.ds(pl.multiple_of(j * chunk, chunk), chunk)
+            result = dot(wide[: high - low, :].astype(BF), pairs[m, :, where])
+            if adds:
+                first = result[:size] + carry[:, where]
+                staged[:size, where] = first.astype(BF)
+                staged[size : high - low, where] = result[size:].astype(BF)
+            else:
+                staged[: high - low, where] = result.astype(BF)
+            if shares:
+                carry[:, where] = result[(count - 1) * size :]
+            return 0
+
+        lax.fori_loop(0, fp // chunk, columns, 0)
+        shared = found[-1][0] if shares else None
+        sent = found[:-1] if shares else found
+        pending = [
+            pltpu.make_async_copy(
+                staged.at[pl.ds(k * size, size)],
+                grad_out.at[pl.ds(highway.position[o] * size, size)],
+                out_sems.at[k],
+            )
+            for k, (o, _, _) in enumerate(sent)
+        ]
+        for copy in pending:
+            copy.start()
+        middle(4 + m)
+    for copy in pending:
+        copy.wait()
+    if empty:
+        staged[:size, :] = jnp.zeros((size, fp), BF)
+        for o in empty:
+            copy = pltpu.make_async_copy(
+                staged.at[pl.ds(0, size)],
+                grad_out.at[pl.ds(highway.position[o] * size, size)],
+                out_sems.at[0],
+            )
+            copy.start()
+            copy.wait()
+    work.cross_over(0)
+    work.last_leg(0)
+    copy = remote(
+        total_out.at[at.c], total_out.at[at.c], pair_sems.at[0], pair_sems.at[1], at.sibling
+    )
+    copy.start()
+    work.finish(0)
+    copy.wait()
+
+
+def highway_backward(plans, filters, dz, hp, features, trans, gates, everywhere, collective_id):
+    highway, lstm = plans
+    rows, fp = features[0].shape
+    words = up_to(rows, 2 * LANE)
+    vmem = pl.BlockSpec(memory_space=pltpu.VMEM)
+    anywhere = pl.BlockSpec(memory_space=pl.ANY)
+    matrices = matrices_of(highway, filters)
+    longest = max([lstm.total] + [end - begin for _, _, begin, end in matrices])
+    layer = max(matrices[2 * l + 1][3] - matrices[2 * l][2] for l in range(2))
+    input_rows = up_to((lstm.meeting(0, filters)[-1][0] + 1) * lstm.rows, 16)
+    return pl.pallas_call(
+        functools.partial(highway_backward_kernel, plans, filters),
+        out_shape=[
+            jax.ShapeDtypeStruct(highway.shape, BF),
+            jax.ShapeDtypeStruct((rows, fp), F32),
+            jax.ShapeDtypeStruct((2,) + lstm.block, F32),
+        ],
+        in_specs=[vmem] * 9 + [anywhere] * 2,
+        out_specs=[anywhere] + [vmem] * 2,
+        scratch_shapes=[
+            pltpu.VMEM(lstm.shape, BF),
+            pltpu.VMEM((layer, highway.columns), BF),
+            pltpu.VMEM((input_rows, lstm.block[1]), BF),
+            pltpu.VMEM((up_to(max(lstm.used + 8, fp), LANE), words), F32),
+            pltpu.VMEM((longest, words), F32),
+            pltpu.VMEM((fp, words), F32),
+            pltpu.VMEM((words, lstm.columns), BF),
+            pltpu.VMEM((4, words, fp), BF),
+            pltpu.VMEM((max(end - begin for _, _, begin, end in matrices), fp), BF),
+            pltpu.VMEM((highway.rows, fp), F32),
+            pltpu.SemaphoreType.DMA((4,)),
+            pltpu.SemaphoreType.DMA((2,)),
+            pltpu.SemaphoreType.DMA((max(len(found) for _, found, _, _ in matrices),)),
+        ]
+        + Reduce.scratch([lstm], True),
+        compiler_params=pltpu.CompilerParams(
+            collective_id=collective_id, has_side_effects=True, vmem_limit_bytes=62 * 2**20
+        ),
+    )(dz, hp, *features, *trans, *gates, *everywhere)
 
 
 def softmax_kernel(
@@ -1472,7 +1835,7 @@
             pltpu.SemaphoreType.DMA((6 * members,)),
         ],
         compiler_params=pltpu.CompilerParams(
-            collective_id=collective_id, has_side_effects=True, vmem_limit_bytes=56 * 2**20
+            collective_id=collective_id, has_side_effects=True, vmem_limit_bytes=62 * 2**20
         ),
     )(h, weights, mapping, mapping_back)
     return loss, grad_h, grad_w.reshape((n,) + plan.block)
@@ -1505,23 +1868,13 @@
     highway = Windows(
         highway_flat.shape[0] * fsdp_count, filters, 4 * (filters + 1), fsdp_count, dp_count, True
     )
-    lstm_used = filters + H + 1
     lstm = Windows(
-        lstm_flat.shape[0] * fsdp_count, 4 * H, lstm_used, fsdp_count, dp_count, False
+        lstm_flat.shape[0] * fsdp_count, 4 * H, filters + H + 1, fsdp_count, dp_count, False
     )
     soft = Windows(
         soft_flat.shape[0] * fsdp_count, V, H + 1, fsdp_count, dp_count, False, fsdp_count // 2
     )
     member = 2 * (fsdp_at // 4) + lax.rem(dp_at, 2)
-
-    soft_own = soft.from_flat(soft_flat, fsdp_at)
-    highway_all, lstm_all = gather(
-        [highway, lstm],
-        [highway.from_flat(highway_flat, fsdp_at), lstm.from_flat(lstm_flat, fsdp_at)],
-        1,
-    )
-    highway_all = highway_all.reshape(-1, highway.columns)
-    lstm_all = lstm_all.reshape(2, -1, lstm.columns // 2)
 
     def by_step(array):
         return jnp.moveaxis(array.reshape((batch, step_count) + array.shape[3:]), 1, 0).reshape(
@@ -1539,17 +1892,8 @@
     word_lengths = pad_rows(by_step(lengths))[:, None]
     position = jnp.arange(letters, dtype=jnp.int32)[None, :]
     codes = jnp.where(position < word_lengths, word_chars, -1)
-    codes = jnp.pad(codes, ((0, 0), (0, SLOTS + KMAX - letters)), constant_values=-1)
-    index = jnp.stack(
-        [
-            jnp.where(
-                codes[:, q : q + SLOTS] >= 0, codes[:, q : q + SLOTS] + q * char_count, -1
-            )
-            for q in range(KMAX)
-        ]
-        + [jnp.full((rows, SLOTS), KMAX * char_count, jnp.int32)],
-        axis=2,
-    ).reshape(rows * SLOTS, KMAX + 1)
+    codes = jnp.pad(codes, ((0, 0), (0, SLOTS - letters)), constant_values=-1)
+    codes = codes.reshape(rows * SLOTS, 1)
     column = np.arange(fp)
     widths = np.ones((fp,), np.int32)
     for cut_at in FILTER_CUTS:
@@ -1572,81 +1916,21 @@
         axis=0,
     )
     spread_table = jnp.pad(spread_table, ((0, HOT - KMAX * char_count - 1), (0, 0)))
-    conv_inputs = (index, word_lengths, spread_table, kernel, jnp.asarray(widths)[None, :])
-    word_block = WORD_BLOCK
-    feature = pl.pallas_call(
-        functools.partial(conv_forward_kernel, filters),
-        out_shape=jax.ShapeDtypeStruct((rows, fp), BF),
-        grid=(rows // word_block,),
-        in_specs=conv_specs(word_block, fp),
-        out_specs=pl.BlockSpec((word_block, fp), lambda i: (i, 0)),
-        compiler_params=pltpu.CompilerParams(vmem_limit_bytes=48 * 2**20),
-    )(*conv_inputs)
-
-    filter_lane = jnp.arange(fp)[None, :]
-    each_layer = 2 * (filters + 1)
-    owner_rows = highway.rows
-
-    def layer_map(row_map, layer):
-        at = row_map - layer * each_layer
-        inside = (row_map >= 0) & (at >= 0) & (at < each_layer)
-        is_gate = inside & (at >= filters + 1)
-        source = np.where(inside, np.where(is_gate, at - filters - 1, at), -1)
-        return source.astype(np.int32), inside & ~is_gate, is_gate
-
-    layers = []
-    for layer in range(2):
-        source, is_trans, is_gate = layer_map(highway.gathered, layer)
-        live = np.nonzero(source.reshape(-1, owner_rows).max(axis=1) >= 0)[0]
-        begin, end = int(live[0]) * owner_rows, (int(live[-1]) + 1) * owner_rows
-        begin = begin // 16 * 16
-        end = min(up_to(end, 16), source.shape[0])
-        weights = highway_all[begin:end]
-        mapping = one_hot_map(fp, source[begin:end])
-        trans_mask = jnp.asarray(is_trans[begin:end].astype(np.float32))[None, :]
-        gate_mask = jnp.asarray(is_gate[begin:end].astype(np.float32))[None, :]
-        spread = dot(feature, mapping)
-        both = jnp.concatenate([spread * trans_mask, spread * gate_mask], axis=0).astype(BF)
-        sums = dot(both, weights)
-        trans, gate = sums[:rows], jax.nn.sigmoid(sums[rows:])
-        layers.append((feature, trans, gate, weights, mapping, trans_mask, gate_mask))
-        value = gate * jax.nn.silu(trans) + (1.0 - gate) * feature.astype(F32)
-        feature = jnp.where(
-            filter_lane < filters, value, jnp.where(filter_lane == filters, 1.0, 0.0)
-        ).astype(BF)
-
-    lp = up_to(lstm_used, LANE)
-    first_h = np.nonzero(lstm.gathered >= filters)[0][0] // 16 * 16
-    last_x = min(up_to(int(np.nonzero((lstm.gathered >= 0) & (lstm.gathered < filters))[0][-1]) + 1, 16), lstm.gathered.shape[0])
-    lstm_map = one_hot_map(lp, lstm.gathered)
-    no_hidden = jnp.concatenate(
-        [
-            feature[:, :filters],
-            jnp.zeros((rows, H), BF),
-            jnp.ones((rows, 1), BF),
-            jnp.zeros((rows, lp - lstm_used), BF),
-        ],
-        axis=1,
-    )
-    spread_x = dot(no_hidden, lstm_map).astype(BF)
-    from_input = jnp.concatenate([dot(spread_x, lstm_all[0]), dot(spread_x, lstm_all[1])], axis=1)
-    hidden_source = lstm.gathered[first_h:] - filters
-    hidden_map = one_hot_map(HP, np.where((hidden_source >= 0) & (hidden_source < H), hidden_source, -1))
-    recur = jnp.concatenate(
-        [dot(hidden_map, lstm_all[h, first_h:]).astype(BF) for h in range(2)], axis=1
-    )
-    recur_t = jnp.concatenate(
-        [
-            lax.dot_general(
-                lstm_all[h, first_h:],
-                hidden_map,
-                (((0,), (1,)), ((), ())),
-                preferred_element_type=F32,
-            ).astype(BF)
-            for h in range(2)
-        ],
-        axis=0,
-    )
+    conv_inputs = (codes, word_lengths, spread_table, kernel, jnp.asarray(widths)[None, :])
+
+    highway_all, lstm_all, from_input, recur, *kept = head(
+        [highway, lstm],
+        filters,
+        [highway.from_flat(highway_flat, fsdp_at), lstm.from_flat(lstm_flat, fsdp_at)],
+        conv_inputs,
+        rows,
+        fp,
+        1,
+    )
+    features, trans, gates = kept[:3], kept[3:5], kept[5:7]
+
+    soft_own = soft.from_flat(soft_flat, fsdp_at)
+    recur_t = recur.T
     keep = pad_rows(by_step(1 - resets).astype(F32))[:, None]
     start = init_state.reshape(batch, 2, H)
     start = jnp.pad(start, ((0, 8 - batch), (0, 0), (0, HP - H)))
@@ -1699,56 +1983,10 @@
     dz, soft_part = lstm_backward(
         batch, soft, lstm.columns, grad_hidden, recur_t, keep, states[1:], soft_grad, 6
     )
-    dz = dz.astype(BF)
-    half = lstm.columns // 2
-    lstm_in = jnp.concatenate(
-        [
-            feature[:, :filters],
-            hp[:, :H].astype(BF),
-            jnp.ones((rows, 1), BF),
-            jnp.zeros((rows, lp - lstm_used), BF),
-        ],
-        axis=1,
-    )
-    lstm_in = dot(lstm_in, one_hot_map(lp, lstm.reduced)).astype(BF)
-    lstm_grad = jnp.stack(
-        [dot_rows(lstm_in, dz[:, h * half : (h + 1) * half]).astype(BF) for h in range(2)]
-    ).reshape(lstm.shape)
-    grad_spread = dot_cols(dz[:, :half], lstm_all[0, :last_x]) + dot_cols(
-        dz[:, half:], lstm_all[1, :last_x]
-    )
-    input_source = lstm.gathered[:last_x]
-    grad = compress(
-        grad_spread, one_hot_map(fp, np.where(input_source < filters, input_source, -1))
-    )
-
-    grads_of, inputs_of = [], []
-    for layer in (1, 0):
-        layer_in, trans, gate, weights, mapping, trans_mask, gate_mask = layers[layer]
-        sig = jax.nn.sigmoid(trans)
-        silu = trans * sig
-        grad = jnp.where(filter_lane < filters, grad, 0.0)
-        grad_trans = (grad * gate * sig * (1.0 + trans * (1.0 - sig))).astype(BF)
-        grad_gate = (grad * (silu - layer_in.astype(F32)) * gate * (1.0 - gate)).astype(BF)
-        pair = jnp.concatenate([grad_trans, grad_gate], axis=0)
-        spread = dot_cols(pair, weights)
-        grad = grad * (1.0 - gate) + compress(
-            spread[:rows] * trans_mask + spread[rows:] * gate_mask, mapping
-        )
-        source, is_trans, is_gate = layer_map(highway.reduced, layer)
-        spread_in = dot(layer_in, one_hot_map(fp, source))
-        inputs_of = [
-            (spread_in * jnp.asarray(is_trans.astype(np.float32))[None, :]).astype(BF),
-            (spread_in * jnp.asarray(is_gate.astype(np.float32))[None, :]).astype(BF),
-        ] + inputs_of
-        grads_of = [pair] + grads_of
-    highway_grad = (
-        dot_rows(jnp.concatenate(inputs_of, axis=0), jnp.concatenate(grads_of, axis=0))
-        .astype(BF)
-        .reshape(highway.shape)
-    )
-
-    grad = jnp.where(filter_lane < filters, grad, 0.0)
+    highway_grad, grad, lstm_part = highway_backward(
+        [highway, lstm], filters, dz, hp, features, trans, gates, (highway_all, lstm_all), 7
+    )
+
     hot_row, hot_lane = np.arange(HOT), np.arange(LANE)
     hot_mask = (hot_row[:, None] // char_count == hot_lane[None, :] // embed_dim) & (
         hot_row[:, None] < KMAX * char_count
@@ -1757,9 +1995,9 @@
         hot_row[None, :] < KMAX * char_count
     )
     conv = Dense(LANE, up_to(fp + LANE, 2 * LANE), fsdp_count)
-    conv_grad, highway_part, lstm_part = tail(
-        [conv, highway, lstm],
-        [highway_grad, lstm_grad],
+    conv_grad, highway_part = tail(
+        [conv, highway],
+        [highway_grad],
         conv_inputs,
         grad,
         jnp.asarray(hot_mask.astype(np.float32)),

time: 607 us -> 492 us (0.81)
  matrix products: 81.4 us -> 0 us
  other arithmetic: 26.1 us -> 8.04 us
  local copies, waits for them, and re-layouts: 68.8 us -> 52.9 us
    dot_general x24 -> x0, matrix products: 81.4 us -> none  [the longest x12 39 us: dot(): return jnp.dot(left, right, preferred_element_type=F32)]
    pallas_call x2, Pallas kernels: 114 us -> 182 us  [the longest x1 116 us: head(): pl.pallas_call(functools.partial(head_kernel, plans, filters, rows // WOR...]
    pallas_call x1, Pallas kernels: 170 us -> 107 us  [tail(): pl.pallas_call(functools.partial(tail_kernel, plans, words // WORD_BLOCK)...]
    slice x3 -> x0, local copies, waits for them, and re-layouts: 11.4 us -> none  [the longest x1 8.53 us: shards(): lstm_all[0]]
    another operation x3 -> x2, other arithmetic: 9.56 us -> 0.64 us  [the longest x1 8.74 us: shards(): jnp.stack([dot_rows(lstm_in, dz[:, h * half:(h + 1) * half]).astype(BF) f...]
    pallas_call x0 -> x1, local copies, waits for them, and re-layouts: none -> 6.93 us  [head(): pl.pallas_call(functools.partial(head_kernel, plans, filters, rows // WOR...]
where the time goes in v4:
time: 492 us; the launch traced here: 485 us
  Pallas kernels  421 us (86%)
  local copies, waits for them, and re-layouts  52.9 us (11%)
  other arithmetic  8.04 us (2%)
    pallas_call x1, Pallas kernels, head(): pl.pallas_call(functools.partial(head_kernel, plans, filters, rows // WOR...  116 us
    pallas_call x1, Pallas kernels, tail(): pl.pallas_call(functools.partial(tail_kernel, plans, words // WORD_BLOCK)...  107 us
    pallas_call x1, Pallas kernels, highway_backward(): pl.pallas_call(functools.partial(highway_backward_kernel, plans, filters)...  65.6 us
    pallas_call x1, Pallas kernels, lstm_backward(): pl.pallas_call(functools.partial(lstm_backward_kernel, batch, n), out_sha...  44.3 us
    pallas_call x1, Pallas kernels, word_softmax(): pl.pallas_call(functools.partial(softmax_kernel, plan.width, n), out_shap...  44.1 us
    pallas_call x1, Pallas kernels, lstm_forward(): pl.pallas_call(functools.partial(lstm_forward_kernel, batch, n), out_shap...  43.9 us
    dynamic_update_slice x6, local copies, waits for them, and re-layouts, from_flat(): lax.dynamic_update_slice(jnp.zeros((self.rows * self.width,), BF), flat[j...  18.8 us

profile of v4, /device:TPU:0, one launch (start us, length us, event | category | flops | bytes accessed | tf_op | source)
XLA Modules:
  0.0 485.1 jit_solution(1916468020833292087)
XLA Ops:
  0.7 1.2 slice_bitcast_fusion.1
  1.9 3.8 dynamic_update_slice.23
  5.8 0.7 reshape.337
  6.5 3.8 dynamic_update_slice.22
  10.3 0.7 reshape.336
  11.3 0.8 copy-done.10
  12.1 2.7 dynamic_update_slice.21
  14.8 0.5 reshape.324
  15.3 2.7 dynamic_update_slice.20
  18.0 0.5 reshape.323
  18.6 0.9 pad_maximum_fusion.refs_1_
  19.7 2.9 dynamic_update_slice.19
  22.6 0.6 reshape.321
  23.3 2.9 dynamic_update_slice.18
  26.3 0.6 reshape.320
  26.9 0.9 fusion.9
  28.0 0.6 and_reduce_fusion
  29.3 0.6 slice.162
  29.9 0.8 scatter.4
  30.7 1.0 concatenate.28
  31.7 0.6 pad.99.refs_4_.refs_3_
  32.9 1.8 reshape.351.refs_2_.refs_1_
  34.6 0.7 copy.73.refs_3_.refs_2_
  35.5 0.8 fusion.18.refs_5_.refs_4_
  36.2 116.1 %shard_map.225 = (bf16[4608,1152]{1,0:T(8,128)(2,1)}, bf16[2,1792,1408]{2,1,0:T(8,128)(2,1)}, f32[144,2816]{1,0:T(8,128)}, bf16[768,2816]{1,0:T(8,128)(2,1)}, f3...) custom-call(bf16[2,144,1152]{2,1,0:T(8,128)(2,1)} %bitcast.106, ...), custom_call_target="tpu_custom_call" | custom-call | tf_op jit(solution)/shard_map/pallas_call | solution.py:1378
  153.4 1.4 copy-done.1
  154.8 43.9 %shard_map.226 = (f32[144,768]{1,0:T(8,128)S(1)}, f32[144,768]{1,0:T(8,128)S(1)}, f32[144,768]{1,0:T(8,128)S(1)}, f32[144,768]{1,0:T(8,128)S(1)}, f32[144,768]{1...) custom-call(f32[144,2816]{1,0:T(8,128)S(1)} %copy-done.1, ...), custom_call_target="tpu_custom_call" | custom-call | tf_op jit(solution)/shard_map/pallas_call | solution.py:1012
  198.8 0.8 copy-done.2
  199.5 0.8 copy-done.3
  200.3 0.8 copy-done.5
  201.0 2.3 fusion
  203.3 44.1 %shard_map.227 = (f32[8,256]{1,0:T(8,128)}, f32[144,768]{1,0:T(8,128)}, bf16[768,1280]{1,0:T(8,128)(2,1)}) custom-call(bf16[8,144,768]{2,1,0:T(8,128)(2,1)} %get-tuple-element.51.h_ref, bf16[16,48,1280]{2,1,0:T(8,128)(2,1)} %get-tuple-element.52.w_ref, bf16[768,768]{1,0:T(8,128)(2,1)} %get-tuple-element.111.map_ref, ...), custom_call_target="tpu_custom_call" | custom-call | tf_op jit(solution)/shard_map/pallas_call | solution.py:1816
  247.5 6.9 %copy.79 = bf16[768,2816]{0,1:T(8,128)(2,1)} copy(bf16[768,2816]{1,0:T(8,128)(2,1)} %get-tuple-element.50.w_ref) | data formatting | bytes 8650752 | tf_op jit(solution)/shard_map/pallas_call | solution.py:1378
  254.4 44.3 %shard_map.228 = (f32[144,2816]{1,0:T(8,128)S(1)}, bf16[8,48,1280]{2,1,0:T(8,128)(2,1)S(1)}) custom-call(f32[144,768]{1,0:T(8,128)S(1)} %copy-done.7, bf16[2816,768]{1,0:T(8,128)(2,1)} %bitcast.105, f32[144,1]{1,0:T(8,128)S(1)} %copy.78.keep_ref, f32[144,768]{1,0:T(8,128)S(1)} %get-tuple-element.55.cp_ref, f32[144,768]{1,0:T(8,128)S(1)} %get-tuple-element.56.i_ref, ...), custom_call_target="tpu_custom_call" | custom-call | tf_op jit(solution)/shard_map/pallas_call | solution.py:1196
  298.8 1.1 copy-done
  300.2 0.7 reshape.350
  300.9 1.2 dynamic-slice_bitcast_fusion
  302.1 65.6 %shard_map.229 = (bf16[4608,1152]{1,0:T(8,128)(2,1)}, f32[144,1152]{1,0:T(8,128)}, f32[2,112,1408]{2,1,0:T(8,128)}) custom-call(f32[144,2816]{1,0:T(8,128)} %copy-done, f32[144,768]{1,0:T(8,128)} %copy-done.2, f32[144,1152]{1,0:T(8,128)} %get-tuple-element.64.refs_2_, f32[144,1152]{1,0:T(8,128)} %get-tuple-element.65.refs_3_, ...), custom_call_target="tpu_custom_call" | custom-call | tf_op jit(solution)/shard_map/pallas_call | solution.py:1592
  367.7 1.4 fusion.34
  369.6 1.0 dynamic-slice_bitcast_fusion.2
  370.6 107.5 %shard_map.230 = (f32[2,16,8,640]{3,2,1,0:T(8,128)}, f32[144,1152]{1,0:T(8,128)}) custom-call(bf16[4608,1152]{1,0:T(8,128)(2,1)} %get-tuple-element.73.refs_0_, s32[3456,1]{1,0:T(8,128)} %reshape.351.refs_2_.refs_1_, s32[144,1]{1,0:T(8,128)} %copy.73.refs_3_.refs_2_, bf16[384,128]{1,0:T(8,128)(2,1)} %pad.99.refs_4_.refs_3_, ...), custom_call_target="tpu_custom_call" | custom-call | tf_op jit(solution)/shard_map/pallas_call | solution.py:741
  478.2 1.2 slice_bitcast_fusion.2
  479.4 0.6 fusion.30
  480.0 0.8 fusion.15
  481.3 1.1 dynamic-slice_bitcast_fusion.1
  482.5 0.6 reduce_sum.19
  483.1 0.7 fusion.31
  484.0 0.6 div.41
  (115 shorter events, 3.9 us)
Async XLA Ops:
  11.0 1.1 copy-start.10
  18.5 1.1 copy-start.9
  22.6 5.2 %copy-start.18 = (bf16[51,15]{0,1:T(8,128)(2,1)S(1)}, bf16[51,15]{0,1:T(8,128)(2,1)}, u32[]{:S(2)}) copy-start(bf16[51,15]{0,1:T(8,128)(2,1)} %param.26) | copy-start | bytes 4594
  23.3 9.0 %copy-start.20 = (s32[2,2,35]{2,1,0:T(2,128)S(1)}, s32[2,2,35]{2,1,0:T(2,128)}, u32[]{:S(2)}) copy-start(s32[2,2,35]{2,1,0:T(2,128)} %param.21) | copy-start | bytes 1684
  23.3 9.2 %copy-start.13 = (s32[2,2,35,21]{2,1,3,0:T(2,128)S(1)}, s32[2,2,35,21]{2,1,3,0:T(2,128)}, u32[]{:S(2)}) copy-start(s32[2,2,35,21]{2,1,3,0:T(2,128)} %param.20) | copy-start | bytes 35284
  27.8 7.6 %copy-start.11 = (pred[105,1100]{1,0:T(8,128)(4,1)S(1)}, pred[105,1100]{1,0:T(8,128)(4,1)}, u32[]{:S(2)}) copy-start(pred[105,1100]{1,0:T(8,128)(4,1)} %constant.170.clone) | copy-start | bytes 346504
  27.8 7.6 %copy-start.12 = (bf16[105,1100]{1,0:T(8,128)(2,1)S(1)}, bf16[105,1100]{1,0:T(8,128)(2,1)}, u32[]{:S(2)}) copy-start(bf16[105,1100]{1,0:T(8,128)(2,1)} %param.27) | copy-start | bytes 693004
  32.4 3.0 copy-start.17
  36.2 116.1 %copy-start.21 = (s32[2,2,35]{2,1,0:T(2,128)S(1)}, s32[2,2,35]{2,1,0:T(2,128)}, u32[]{:S(2)}) copy-start(s32[2,2,35]{2,1,0:T(2,128)} %param.22) | copy-start | bytes 1684
  36.2 116.3 %copy-start.22 = (f32[2,2]{1,0:T(2,128)S(1)}, f32[2,2]{1,0:T(2,128)}, u32[]{:S(2)}) copy-start(f32[2,2]{1,0:T(2,128)} %param.25) | copy-start | bytes 52
  36.2 116.8 %copy-start.19 = (s32[2,2,35]{2,1,0:T(2,128)S(1)}, s32[2,2,35]{2,1,0:T(2,128)}, u32[]{:S(2)}) copy-start(s32[2,2,35]{2,1,0:T(2,128)} %param.23) | copy-start | bytes 1684
  36.2 117.1 %copy-start.14 = (f32[2,2,2,650]{3,2,1,0:T(2,128)S(1)}, f32[2,2,2,650]{3,2,1,0:T(2,128)}, u32[]{:S(2)}) copy-start(f32[2,2,2,650]{3,2,1,0:T(2,128)} %param.24) | copy-start | bytes 62404
  153.4 1.4 copy-start.1
  154.8 46.2 %copy-start.15 = (s32[768]{0:T(1024)S(1)}, s32[768]{0:T(1024)}, u32[]{:S(2)}) copy-start(s32[768]{0:T(1024)} %constant.172.clone) | copy-start | bytes 9220
  154.8 46.2 %copy-start.16 = (s32[768]{0:T(1024)S(1)}, s32[768]{0:T(1024)}, u32[]{:S(2)}) copy-start(s32[768]{0:T(1024)} %constant.173.clone) | copy-start | bytes 9220
  198.7 0.8 copy-start.2
  199.5 0.8 copy-start.3
  200.3 0.8 copy-start.5
  247.4 7.0 %copy-start.4 = (f32[144,768]{1,0:T(8,128)S(1)}, f32[144,768]{1,0:T(8,128)}, u32[]{:S(2)}) copy-start(f32[144,768]{1,0:T(8,128)} %copy-done.3) | copy-start | bytes 1327108
  247.4 7.0 %copy-start.6 = (f32[144,768]{1,0:T(8,128)S(1)}, f32[144,768]{1,0:T(8,128)}, u32[]{:S(2)}) copy-start(f32[144,768]{1,0:T(8,128)} %copy-done.5) | copy-start | bytes 1327108
  247.5 7.0 %copy-start.7 = (f32[144,768]{1,0:T(8,128)S(1)}, f32[144,768]{1,0:T(8,128)}, u32[]{:S(2)}) copy-start(f32[144,768]{1,0:T(8,128)} %get-tuple-element.54.dh_ref) | copy-start | bytes 1327108
  298.8 1.2 copy-start
  478.2 2.7 copy-start.8

commit v5 on v4

--- a/solution.py
+++ b/solution.py
@@ -102,18 +102,47 @@
                 found.append((o, first, last))
         return found
 
-    def from_flat(self, shard, fsdp_at):
-        parts = []
-        flat = shard.reshape(-1)
+    @property
+    def lines(self):
+        return up_to(-(-self.rows * self.width // LANE), 16) + 32
+
+    def place_blocks(self, shard_ref, out_ref):
+        fsdp_at = lax.axis_index("fsdp")
+        count = self.entries // LANE
+        out_ref[...] = jnp.zeros_like(out_ref)
         for j in range(self.dp):
             shift = lax.rem((fsdp_at * self.dp + j) * self.entries, self.width)
-            piece = lax.dynamic_update_slice(
-                jnp.zeros((self.rows * self.width,), BF),
-                flat[j * self.entries : (j + 1) * self.entries],
-                (shift,),
-            ).reshape(self.rows, self.width)
-            parts.append(jnp.pad(piece, ((0, 0), (0, self.columns - self.width))))
-        joined = jnp.concatenate(parts, axis=0)
+            lanes, lines = lax.rem(shift, LANE), lax.rem(shift // LANE, 16)
+            block = shard_ref[j].astype(F32)
+            extra = up_to(count, 16) + 16 - count
+            block = jnp.concatenate([block, jnp.zeros((extra, LANE), F32)], axis=0)
+            block = pltpu.roll(block, lanes, 1)
+            lane = lax.broadcasted_iota(jnp.int32, block.shape, 1)
+            block = jnp.where(lane < lanes, pltpu.roll(block, 1, 0), block)
+            for step in (1, 2, 4, 8):
+                moved = lax.rem(lines // step, 2) == 1
+                block = jnp.where(moved, pltpu.roll(block, step, 0), block)
+            begin = pl.multiple_of(shift // (16 * LANE) * 16, 16)
+            out_ref[j, pl.ds(begin, count + extra), :] = block.astype(BF)
+
+    def placed_shape(self):
+        return jax.ShapeDtypeStruct((self.dp, self.lines, LANE), BF)
+
+    def blocks_of(self, shard):
+        return shard.reshape(self.dp, self.entries // LANE, LANE)
+
+    def from_placed(self, placed):
+        size = self.rows * self.width
+        joined = jnp.concatenate(
+            [
+                jnp.pad(
+                    placed[j].reshape(-1)[:size].reshape(self.rows, self.width),
+                    ((0, 0), (0, self.columns - self.width)),
+                )
+                for j in range(self.dp)
+            ],
+            axis=0,
+        )
         if self.by_rows:
             return joined.reshape((2,) + self.block)
         part = self.columns // self.parts
@@ -348,10 +377,10 @@
         self.plans, self.ins, self.totals, self.in_place = plans, ins, totals, in_place
         self.held = [None] * count if in_place else scratch[:count]
         scratch = scratch if in_place else scratch[count:]
-        self.landed, self.flow_up, self.flow_down, self.close, self.cross = (
-            scratch[k * count : (k + 1) * count] for k in range(5)
-        )
-        self.sems = scratch[5 * count]
+        self.landed, self.flow, self.close, self.cross = (
+            scratch[k * count : (k + 1) * count] for k in range(4)
+        )
+        self.sems = scratch[4 * count]
         self.n = plans[0].fsdp
         self.lengthwise = self.n // 4
         self.at = Place()
@@ -361,7 +390,8 @@
         n = plans[0].fsdp
         return (
             [pltpu.VMEM((n,) + plan.block, plan.dtype) for plan in plans] * (1 if in_place else 2)
-            + [pltpu.VMEM((n // 2,) + plan.block, plan.dtype) for plan in plans] * 3
+            + [pltpu.VMEM((n // 2 + 2,) + plan.block, plan.dtype) for plan in plans]
+            + [pltpu.VMEM((n // 2,) + plan.block, plan.dtype) for plan in plans]
             + [pltpu.VMEM(plan.block, plan.dtype) for plan in plans]
             + [pltpu.SemaphoreType.DMA((10 * len(plans) * n,))]
         )
@@ -412,10 +442,15 @@
             self.at.partner1,
         )
 
+    def flow_at(self, up, here, z, b3):
+        if up:
+            return 2 * z + b3
+        return jnp.where(z == here, self.n // 2 + b3, 2 * z + b3)
+
     def along(self, up, a, z, b3):
         return remote(
             self.hold(a, self.slot(z, self.at.first, b3)),
-            (self.flow_up if up else self.flow_down)[a].at[2 * z + b3],
+            self.flow[a].at[self.flow_at(up, self.at.z + (1 if up else -1), z, b3)],
             self.sem(self.UP if up else self.DOWN, a, 2 * z + b3),
             self.sem(self.UP_RECV if up else self.DOWN_RECV, a, 2 * z + b3),
             (self.at.d, self.at.f + (4 if up else -4)),
@@ -492,8 +527,7 @@
             @pl.when(incoming)
             def _():
                 self.along(up, a, z, b3).wait_recv()
-                flows = self.flow_up if up else self.flow_down
-                self.add(a, block, base + [(flows[a], flow)])
+                self.add(a, block, base + [(self.flow[a], self.flow_at(up, self.at.z, z, b3))])
 
             @pl.when(jnp.logical_not(incoming))
             def _():
@@ -516,8 +550,7 @@
             @pl.when(z > 0 if up else z < self.lengthwise - 1)
             def _(up=up):
                 self.along(up, a, z, b3).wait_recv()
-                flows = self.flow_up if up else self.flow_down
-                self.add(a, block, [(flows[a], 2 * z + b3)])
+                self.add(a, block, [(self.flow[a], self.flow_at(up, z, z, b3))])
 
     def cross_over(self, a):
         self.own(a, 1 - self.at.last)
@@ -624,6 +657,23 @@
     hot_grad_ref[...] += dot_rows(hot, grad_windows.astype(BF))
 
 
+def place_kernel(plans, *refs):
+    for plan, shard, out in zip(plans, refs[: len(plans)], refs[len(plans) :]):
+        plan.place_blocks(shard, out)
+
+
+def place_all(plans, shards):
+    vmem = pl.BlockSpec(memory_space=pltpu.VMEM)
+    placed = pl.pallas_call(
+        functools.partial(place_kernel, plans),
+        out_shape=[plan.placed_shape() for plan in plans],
+        in_specs=[vmem] * len(plans),
+        out_specs=[vmem] * len(plans),
+        compiler_params=pltpu.CompilerParams(vmem_limit_bytes=48 * 2**20),
+    )(*[plan.blocks_of(shard) for plan, shard in zip(plans, shards)])
+    return [plan.from_placed(each) for plan, each in zip(plans, placed)]
+
+
 class Dense:
     by_rows = False
     dtype = F32
@@ -641,122 +691,74 @@
 WORD_BLOCK = 16
 
 
-def tail_kernel(plans, blocks, *refs):
-    conv, rest = plans[0], plans[1:]
-    count = len(plans)
-    ins, refs = refs[: count - 1], refs[count - 1 :]
-    codes_ref, length_ref, table_ref, kernel_ref, width_ref, grad_ref, mask_ref, fold_ref = refs[:8]
-    outs, refs = refs[8 : 8 + count], refs[8 + count :]
-    conv_out, rest_outs = outs[0], outs[1:]
-    kernel_grad, hot_grad, conv_in, conv_total = refs[:4]
-    pair_sems, gather_sems = refs[4:6]
-    at = Place()
-    totals = [conv_total] + [
-        out if plan.by_rows else out.at[at.c] for plan, out in zip(rest, rest_outs)
-    ]
-    work = Reduce(plans, [conv_in] + list(ins), totals, refs[6:])
+def tail_kernel(plans, conv_ref, grad_ref, conv_out, total_out, conv_in, conv_total, gather_sems, *scratch):
+    conv, highway = plans
+    work = Reduce(plans, [conv_in, grad_ref], [conv_total, total_out], scratch)
     items = 2 * work.lengthwise
-    greet(at, work.lengthwise)
-    for a in range(1, count):
-        work.begin(a)
-    kernel_grad[...] = jnp.zeros_like(kernel_grad)
-    hot_grad[...] = jnp.zeros_like(hot_grad)
+    greet(work.at, work.lengthwise)
     conv_in[...] = jnp.zeros_like(conv_in)
-
-    def compute(i):
-        words = pl.ds(pl.multiple_of(i * WORD_BLOCK, WORD_BLOCK), WORD_BLOCK)
-        slots = pl.ds(pl.multiple_of(i * WORD_BLOCK * SLOTS, WORD_BLOCK * SLOTS), WORD_BLOCK * SLOTS)
-        conv_backward_block(
-            codes_ref[slots, :],
-            length_ref[words, :],
-            (table_ref, kernel_ref, width_ref),
-            grad_ref,
-            words,
-            kernel_grad,
-            hot_grad,
-        )
-
-    def leg(body, a):
+    depth, half = conv.block
+    for block in range(conv.filled // depth):
+        for h in range(2):
+            conv_in[h, block] = conv_ref[
+                block * depth : (block + 1) * depth, h * half : (h + 1) * half
+            ]
+    work.begin(0)
+    work.begin(1)
+
+    def legs(body, a, begin, end):
         def step(t, _):
             body(a, t)
             return 0
 
-        lax.fori_loop(0, items, step, 0)
-
-    for a in range(1, count):
-        leg(work.first_leg, a)
-
-    def together(t, _):
-        pl.when(t < blocks)(functools.partial(compute, t))
-
-        @pl.when(t < items)
-        def _():
-            for a in range(1, count):
-                work.middle_leg(a, t)
-
-        return 0
-
-    lax.fori_loop(0, max(items, blocks), together, 0)
-
-    wide = kernel_ref.shape[1]
-    kernel_grad[:, wide:] = jnp.dot(
-        fold_ref[...],
-        hot_grad[...] * mask_ref[...],
-        precision=lax.Precision.HIGHEST,
-        preferred_element_type=F32,
-    )
-    depth, half = conv.block
-    for block in range(conv.filled // depth):
-        for h in range(2):
-            conv_in[h, block] = kernel_grad[
-                block * depth : (block + 1) * depth, h * half : (h + 1) * half
-            ]
-    work.begin(0)
-
-    leg(work.first_leg, 0)
-    leg(work.middle_leg, 0)
-    for a in range(count):
-        work.cross_over(a)
+        lax.fori_loop(begin, end, step, 0)
+
+    legs(work.first_leg, 0, 0, items)
+    legs(work.first_leg, 1, 0, items // 2)
+    legs(work.middle_leg, 0, 0, items)
+    legs(work.first_leg, 1, items // 2, items)
+    work.cross_over(0)
+    legs(work.middle_leg, 1, 0, 1)
     work.last_leg(0)
     spread = Gather([conv], [conv_total], [conv_out], gather_sems, False)
     spread.begin(0)
-    copies = pair_exchange(rest, totals[1:], rest_outs, pair_sems, at)
-    for a in range(1, count):
-        work.last_leg(a)
-    for copy in copies:
-        copy.start()
-    for step in spread.steps(0):
+    steps = spread.steps(0)
+    for k in range(1, max(items, len(steps))):
+        if k < items:
+            legs(work.middle_leg, 1, k, k + 1)
+        if k - 1 < len(steps):
+            steps[k - 1]()
+    work.cross_over(1)
+    for step in steps[max(items, len(steps)) - 1 :]:
         step()
+    work.last_leg(1)
     spread.from_sibling(0)
     spread.finish(0)
-    for a in range(count):
+    for a in range(2):
         work.finish(a)
-    for copy in copies:
-        copy.wait()
-
-
-def tail(plans, grads, conv_inputs, grad, mask, fold, collective_id):
-    conv, rest = plans[0], plans[1:]
-    words = grad.shape[0]
+
+
+def tail(plans, conv_grad, highway_grad, collective_id):
+    conv, highway = plans
+    vmem = pl.BlockSpec(memory_space=pltpu.VMEM)
     return pl.pallas_call(
-        functools.partial(tail_kernel, plans, words // WORD_BLOCK),
-        out_shape=[jax.ShapeDtypeStruct(conv.shape, F32)] + [reduce_out(plan) for plan in rest],
-        in_specs=[pl.BlockSpec(memory_space=pl.ANY)] * len(rest)
-        + [pl.BlockSpec(memory_space=pltpu.VMEM)] * 8,
-        out_specs=[pl.BlockSpec(memory_space=pltpu.VMEM)] * len(plans),
+        functools.partial(tail_kernel, plans),
+        out_shape=[
+            jax.ShapeDtypeStruct(conv.shape, F32),
+            jax.ShapeDtypeStruct(highway.block, F32),
+        ],
+        in_specs=[vmem, pl.BlockSpec(memory_space=pl.ANY)],
+        out_specs=[vmem] * 2,
         scratch_shapes=[
-            pltpu.VMEM((conv.filled, 2 * conv.block[1]), F32),
-            pltpu.VMEM((HOT, LANE), F32),
             pltpu.VMEM(conv.shape, F32),
             pltpu.VMEM(conv.block, F32),
-            pltpu.SemaphoreType.DMA((2 * len(rest),)),
             Gather.semaphores([conv]),
         ]
         + Reduce.scratch(plans),
         compiler_params=pltpu.CompilerParams(
-            collective_id=collective_id, has_side_effects=True, vmem_limit_bytes=60 * 2**20
+            collective_id=collective_id, has_side_effects=True, vmem_limit_bytes=48 * 2**20
         ),
-    )(*grads, *conv_inputs, grad, mask, fold)
+    )(conv_grad, highway_grad)
 
 
 def gate_parts(sums):
@@ -1243,13 +1245,13 @@
     return result
 
 
-def head_kernel(plans, filters, blocks, *refs):
+def head_kernel(plans, soft, filters, blocks, *refs):
     highway, lstm = plans
     owns = refs[:2]
-    codes_ref, length_ref, table_ref, kernel_ref, width_ref = refs[2:7]
-    highway_out, lstm_out, x_ref, recur_ref = refs[7:11]
-    features, trans_refs, gate_refs = refs[11:14], refs[14:16], refs[16:18]
-    highway_w, lstm_w, turned_ref, wide, recur_sum, gather_sems, out_sems = refs[18:]
+    codes_ref, length_ref, table_ref, kernel_ref, width_ref, soft_ref = refs[2:8]
+    highway_out, lstm_out, x_ref, recur_ref, soft_out = refs[8:13]
+    features, trans_refs, gate_refs = refs[13:16], refs[16:18], refs[18:20]
+    highway_w, lstm_w, turned_ref, wide, recur_sum, gather_sems, out_sems = refs[20:]
     rows, fp = features[0].shape
     words = turned_ref.shape[1]
     work = Gather(plans, owns, (highway_w, lstm_w), gather_sems, True)
@@ -1312,6 +1314,7 @@
         conv(k * third, min((k + 1) * third, blocks))
         if k < count:
             of_highway[k]()
+    soft.place_blocks(soft_ref, soft_out)
     late = count - 4
     for k in range(3, count):
         if k == max(late, 3):
@@ -1367,7 +1370,7 @@
         copy.wait()
 
 
-def head(plans, filters, own, conv_inputs, rows, fp, collective_id):
+def head(plans, soft, filters, own, conv_inputs, soft_flat, rows, fp, collective_id):
     highway, lstm = plans
     words = up_to(rows, 2 * LANE)
     vmem = pl.BlockSpec(memory_space=pltpu.VMEM)
@@ -1376,16 +1379,17 @@
     matrices = matrices_of(highway, filters)
     longest = max([lstm.total] + [end - begin for _, _, begin, end in matrices])
     return pl.pallas_call(
-        functools.partial(head_kernel, plans, filters, rows // WORD_BLOCK),
+        functools.partial(head_kernel, plans, soft, filters, rows // WORD_BLOCK),
         out_shape=[
             jax.ShapeDtypeStruct(highway.shape, BF),
             jax.ShapeDtypeStruct(lstm.shape, BF),
             jax.ShapeDtypeStruct((rows, lstm.columns), F32),
             jax.ShapeDtypeStruct((HP, lstm.columns), BF),
+            soft.placed_shape(),
         ]
         + [feature] * 7,
-        in_specs=[anywhere] * 2 + [vmem] * 5,
-        out_specs=[anywhere] * 2 + [vmem] * 9,
+        in_specs=[anywhere] * 2 + [vmem] * 6,
+        out_specs=[anywhere] * 2 + [vmem] * 10,
         scratch_shapes=[
             pltpu.VMEM(highway.shape, BF),
             pltpu.VMEM(lstm.shape, BF),
@@ -1398,21 +1402,23 @@
         compiler_params=pltpu.CompilerParams(
             collective_id=collective_id, has_side_effects=True, vmem_limit_bytes=60 * 2**20
         ),
-    )(*own, *conv_inputs)
-
-
-def highway_backward_kernel(plans, filters, *refs):
+    )(*own, *conv_inputs, soft.blocks_of(soft_flat))
+
+
+def highway_backward_kernel(plans, filters, blocks, *refs):
     highway, lstm = plans
     dz_ref, hp_ref = refs[:2]
     features, trans_refs, gate_refs = refs[2:5], refs[5:7], refs[7:9]
-    highway_all, lstm_all = refs[9:11]
-    grad_out, feature_grad, total_out = refs[11:14]
-    lstm_grad, highway_w, lstm_w, turned_ref, wide, back, dz, pairs = refs[14:22]
-    staged, carry, load_sems, pair_sems, out_sems = refs[22:27]
+    codes_ref, length_ref, table_ref, kernel_ref, width_ref, mask_ref, fold_ref = refs[9:16]
+    highway_all, lstm_all = refs[16:18]
+    grad_out, kernel_grad, total_out = refs[18:21]
+    refs = refs[21:]
+    lstm_grad, highway_w, lstm_w, turned_ref, wide, back, dz, pairs = refs[:8]
+    staged, carry, feature_grad, hot_grad, load_sems, pair_sems, out_sems = refs[8:15]
     rows, fp = features[0].shape
     words = turned_ref.shape[1]
     at = Place()
-    work = Reduce([lstm], [lstm_grad], [total_out.at[at.c]], refs[27:], True)
+    work = Reduce([lstm], [lstm_grad], [total_out.at[at.c]], refs[15:], True)
     length, items = work.lengthwise, 2 * work.lengthwise
     matrices = matrices_of(highway, filters)
     half = lstm.block[1]
@@ -1486,7 +1492,7 @@
         lax.fori_loop(begin, end, step, 0)
 
     legs(work.first_leg, 0, items)
-    spots = 8
+    spots = 4 + blocks
 
     def middle(k):
         legs(work.middle_leg, k * items // spots, (k + 1) * items // spots)
@@ -1513,6 +1519,33 @@
         grad = jnp.where(lane < filters, grad, 0.0)
     feature_grad[...] = grad
 
+    kernel_grad[...] = jnp.zeros_like(kernel_grad)
+    hot_grad[...] = jnp.zeros_like(hot_grad)
+
+    def conv_block(i, _):
+        where = pl.ds(pl.multiple_of(i * WORD_BLOCK, WORD_BLOCK), WORD_BLOCK)
+        slots = pl.ds(pl.multiple_of(i * WORD_BLOCK * SLOTS, WORD_BLOCK * SLOTS), WORD_BLOCK * SLOTS)
+        conv_backward_block(
+            codes_ref[slots, :],
+            length_ref[where, :],
+            (table_ref, kernel_ref, width_ref),
+            feature_grad,
+            where,
+            kernel_grad,
+            hot_grad,
+        )
+        middle(4 + i)
+        return 0
+
+    lax.fori_loop(0, blocks, conv_block, 0)
+    kernel_grad[:, fp:] = jnp.dot(
+        fold_ref[...],
+        hot_grad[...] * mask_ref[...],
+        precision=lax.Precision.HIGHEST,
+        preferred_element_type=F32,
+    )
+    work.cross_over(0)
+
     chunk = 384
     size = highway.rows
     pending, shared = [], None
@@ -1556,7 +1589,6 @@
         ]
         for copy in pending:
             copy.start()
-        middle(4 + m)
     for copy in pending:
         copy.wait()
     if empty:
@@ -1569,7 +1601,6 @@
             )
             copy.start()
             copy.wait()
-    work.cross_over(0)
     work.last_leg(0)
     copy = remote(
         total_out.at[at.c], total_out.at[at.c], pair_sems.at[0], pair_sems.at[1], at.sibling
@@ -1579,7 +1610,9 @@
     copy.wait()
 
 
-def highway_backward(plans, filters, dz, hp, features, trans, gates, everywhere, collective_id):
+def highway_backward(
+    plans, filters, dz, hp, features, trans, gates, conv_inputs, everywhere, collective_id
+):
     highway, lstm = plans
     rows, fp = features[0].shape
     words = up_to(rows, 2 * LANE)
@@ -1590,13 +1623,13 @@
     layer = max(matrices[2 * l + 1][3] - matrices[2 * l][2] for l in range(2))
     input_rows = up_to((lstm.meeting(0, filters)[-1][0] + 1) * lstm.rows, 16)
     return pl.pallas_call(
-        functools.partial(highway_backward_kernel, plans, filters),
+        functools.partial(highway_backward_kernel, plans, filters, rows // WORD_BLOCK),
         out_shape=[
             jax.ShapeDtypeStruct(highway.shape, BF),
-            jax.ShapeDtypeStruct((rows, fp), F32),
+            jax.ShapeDtypeStruct((LANE, up_to(fp + LANE, 2 * LANE)), F32),
             jax.ShapeDtypeStruct((2,) + lstm.block, F32),
         ],
-        in_specs=[vmem] * 9 + [anywhere] * 2,
+        in_specs=[vmem] * 16 + [anywhere] * 2,
         out_specs=[anywhere] + [vmem] * 2,
         scratch_shapes=[
             pltpu.VMEM(lstm.shape, BF),
@@ -1609,15 +1642,17 @@
             pltpu.VMEM((4, words, fp), BF),
             pltpu.VMEM((max(end - begin for _, _, begin, end in matrices), fp), BF),
             pltpu.VMEM((highway.rows, fp), F32),
+            pltpu.VMEM((rows, fp), F32),
+            pltpu.VMEM((HOT, LANE), F32),
             pltpu.SemaphoreType.DMA((4,)),
             pltpu.SemaphoreType.DMA((2,)),
             pltpu.SemaphoreType.DMA((max(len(found) for _, found, _, _ in matrices),)),
         ]
         + Reduce.scratch([lstm], True),
         compiler_params=pltpu.CompilerParams(
-            collective_id=collective_id, has_side_effects=True, vmem_limit_bytes=62 * 2**20
+            collective_id=collective_id, has_side_effects=True, vmem_limit_bytes=255 * 2**18
         ),
-    )(dz, hp, *features, *trans, *gates, *everywhere)
+    )(dz, hp, *features, *trans, *gates, *conv_inputs, *everywhere)
 
 
 def softmax_kernel(
@@ -1912,24 +1947,26 @@
             jnp.pad(char_table, ((0, 0), (q * embed_dim, LANE - (q + 1) * embed_dim)))
             for q in range(KMAX)
         ]
-        + [jnp.zeros((1, LANE), BF).at[0, ones_row].set(1.0)],
+        + [jnp.asarray((np.arange(LANE) == ones_row)[None, :].astype(np.float32)).astype(BF)],
         axis=0,
     )
     spread_table = jnp.pad(spread_table, ((0, HOT - KMAX * char_count - 1), (0, 0)))
     conv_inputs = (codes, word_lengths, spread_table, kernel, jnp.asarray(widths)[None, :])
 
-    highway_all, lstm_all, from_input, recur, *kept = head(
+    highway_all, lstm_all, from_input, recur, soft_placed, *kept = head(
         [highway, lstm],
+        soft,
         filters,
-        [highway.from_flat(highway_flat, fsdp_at), lstm.from_flat(lstm_flat, fsdp_at)],
+        place_all([highway, lstm], [highway_flat, lstm_flat]),
         conv_inputs,
+        soft_flat,
         rows,
         fp,
         1,
     )
     features, trans, gates = kept[:3], kept[3:5], kept[5:7]
 
-    soft_own = soft.from_flat(soft_flat, fsdp_at)
+    soft_own = soft.from_placed(soft_placed)
     recur_t = recur.T
     keep = pad_rows(by_step(1 - resets).astype(F32))[:, None]
     start = init_state.reshape(batch, 2, H)
@@ -1983,10 +2020,6 @@
     dz, soft_part = lstm_backward(
         batch, soft, lstm.columns, grad_hidden, recur_t, keep, states[1:], soft_grad, 6
     )
-    highway_grad, grad, lstm_part = highway_backward(
-        [highway, lstm], filters, dz, hp, features, trans, gates, (highway_all, lstm_all), 7
-    )
-
     hot_row, hot_lane = np.arange(HOT), np.arange(LANE)
     hot_mask = (hot_row[:, None] // char_count == hot_lane[None, :] // embed_dim) & (
         hot_row[:, None] < KMAX * char_count
@@ -1994,16 +2027,24 @@
     hot_fold = (hot_row[None, :] % char_count == np.arange(LANE)[:, None]) & (
         hot_row[None, :] < KMAX * char_count
     )
-    conv = Dense(LANE, up_to(fp + LANE, 2 * LANE), fsdp_count)
-    conv_grad, highway_part = tail(
-        [conv, highway],
-        [highway_grad],
-        conv_inputs,
-        grad,
-        jnp.asarray(hot_mask.astype(np.float32)),
-        jnp.asarray(hot_fold.astype(np.float32)),
-        3,
-    )
+    highway_grad, conv_grad, lstm_part = highway_backward(
+        [highway, lstm],
+        filters,
+        dz,
+        hp,
+        features,
+        trans,
+        gates,
+        (
+            *conv_inputs,
+            jnp.asarray(hot_mask.astype(np.float32)),
+            jnp.asarray(hot_fold.astype(np.float32)),
+        ),
+        (highway_all, lstm_all),
+        7,
+    )
+    conv = Dense(LANE, conv_grad.shape[1], fsdp_count)
+    conv_grad, highway_part = tail([conv, highway], conv_grad, highway_grad, 3)
     conv_grad = jnp.concatenate(
         [conv_grad[h].reshape(-1, conv.block[1])[:LANE] for h in range(2)], axis=1
     )

time: 492 us -> 473 us (0.961)
  the two profiles are of different devices: /device:TPU:0 before, /device:TPU:28 now
where the time goes in v5:
time: 473 us; the launch traced here: 468 us
  Pallas kernels  422 us (89%)
  local copies, waits for them, and re-layouts  36.5 us (8%)
  other arithmetic  7.36 us (2%)
    pallas_call x1, Pallas kernels, head(): pl.pallas_call(functools.partial(head_kernel, plans, soft, filters, rows...  108 us
    pallas_call x1, Pallas kernels, tail(): pl.pallas_call(functools.partial(tail_kernel, plans), out_shape=[jax.Shap...  88.8 us
    pallas_call x1, Pallas kernels, highway_backward(): pl.pallas_call(functools.partial(highway_backward_kernel, plans, filters,...  84.7 us
    pallas_call x1, Pallas kernels, lstm_forward(): pl.pallas_call(functools.partial(lstm_forward_kernel, batch, n), out_shap...  50 us
    pallas_call x1, Pallas kernels, word_softmax(): pl.pallas_call(functools.partial(softmax_kernel, plan.width, n), out_shap...  49.5 us
    pallas_call x1, Pallas kernels, lstm_backward(): pl.pallas_call(functools.partial(lstm_backward_kernel, batch, n), out_sha...  40.3 us

profile of v5, /device:TPU:28, one launch (start us, length us, event | category | flops | bytes accessed | tf_op | source)
XLA Modules:
  0.0 467.8 jit_solution(365793338277879766)
XLA Ops:
  0.6 0.9 copy.66
  1.6 1.7 concatenate.26
  3.3 0.6 pad.95.refs_4_.refs_11_
  3.9 1.2 reshape.285.refs_0_
  5.1 1.3 shard_map.234
  6.5 0.5 reshape.290
  7.0 0.5 reshape.291
  7.6 0.9 pad_maximum_fusion.refs_1_
  8.7 0.6 reshape.287
  9.3 0.6 reshape.288
  10.0 0.9 fusion.9
  11.1 0.1 copy.65
  11.4 1.7 reshape.317.refs_2_.refs_9_
  13.2 0.8 copy.74.refs_3_.refs_10_
  14.0 0.8 fusion.18.refs_5_.refs_12_
  14.8 1.1 reshape.297.refs_7_
  15.8 107.7 %shard_map.235 = (bf16[4608,1152]{1,0:T(8,128)(2,1)}, bf16[2,1792,1408]{2,1,0:T(8,128)(2,1)}, f32[144,2816]{1,0:T(8,128)}, bf16[768,2816]{1,0:T(8,128)(2,1)}, bf...) custom-call(bf16[2,144,1152]{2,1,0:T(8,128)(2,1)} %bitcast.103, ...), custom_call_target="tpu_custom_call" | custom-call | tf_op jit(solution)/shard_map/pallas_call | solution.py:1381
  123.5 1.2 fusion.36
  124.7 0.7 reshape.302
  125.4 0.7 reshape.303
  126.4 0.4 copy-done.26
  127.9 50.0 %shard_map.236 = (f32[144,768]{1,0:T(8,128)S(1)}, f32[144,768]{1,0:T(8,128)S(1)}, f32[144,768]{1,0:T(8,128)S(1)}, f32[144,768]{1,0:T(8,128)S(1)}, f32[144,768]{1...) custom-call(f32[144,2816]{1,0:T(8,128)S(1)} %copy-done.1, ...), custom_call_target="tpu_custom_call" | custom-call | tf_op jit(solution)/shard_map/pallas_call | solution.py:1014
  177.9 0.8 copy-done.4
  178.7 0.8 copy-done.5
  179.4 0.8 copy-done.7
  180.2 0.8 copy-done.9
  181.0 0.8 copy-done.11
  181.7 0.8 copy-done.13
  182.5 2.3 fusion
  184.8 49.5 %shard_map.237 = (f32[8,256]{1,0:T(8,128)}, f32[144,768]{1,0:T(8,128)}, bf16[768,1280]{1,0:T(8,128)(2,1)}) custom-call(bf16[8,144,768]{2,1,0:T(8,128)(2,1)} %get-tuple-element.45.h_ref, bf16[16,48,1280]{2,1,0:T(8,128)(2,1)} %get-tuple-element.46.w_ref, bf16[768,768]{1,0:T(8,128)(2,1)} %get-tuple-element.105.map_ref, ...), custom_call_target="tpu_custom_call" | custom-call | tf_op jit(solution)/shard_map/pallas_call | solution.py:1851
  234.3 6.8 %copy.80 = bf16[768,2816]{0,1:T(8,128)(2,1)} copy(bf16[768,2816]{1,0:T(8,128)(2,1)} %get-tuple-element.43.w_ref) | data formatting | bytes 8650752 | tf_op jit(solution)/shard_map/pallas_call | solution.py:1381
  241.1 1.0 copy-done.15
  242.1 40.3 %shard_map.238 = (f32[144,2816]{1,0:T(8,128)S(1)}, bf16[8,48,1280]{2,1,0:T(8,128)(2,1)S(1)}) custom-call(f32[144,768]{1,0:T(8,128)S(1)} %copy-done.15, bf16[2816,768]{1,0:T(8,128)(2,1)} %bitcast.102, f32[144,1]{1,0:T(8,128)S(1)} %copy.79.keep_ref, f32[144,768]{1,0:T(8,128)S(1)} %get-tuple-element.49.cp_ref, f32[144,768]{1,0:T(8,128)S(1)} %copy-done.6, ...), custom_call_target="tpu_custom_call" | custom-call | tf_op jit(solution)/shard_map/pallas_call | solution.py:1198
  282.5 1.1 copy-done
  283.9 0.7 reshape.316
  284.6 1.2 dynamic-slice_bitcast_fusion
  285.8 84.7 %shard_map.239 = (bf16[4608,1152]{1,0:T(8,128)(2,1)}, f32[128,1280]{1,0:T(8,128)}, f32[2,112,1408]{2,1,0:T(8,128)}) custom-call(f32[144,2816]{1,0:T(8,128)} %copy-done, f32[144,768]{1,0:T(8,128)} %copy-done.4, f32[144,1152]{1,0:T(8,128)} %get-tuple-element.58.refs_2_, f32[144,1152]{1,0:T(8,128)} %get-tuple-element.59.refs_3_, ...), custom_call_target="tpu_custom_call" | custom-call | tf_op jit(solution)/shard_map/pallas_call | solution.py:1625
  370.5 1.4 fusion.34
  372.0 0.4 reshape.309
  372.4 1.0 dynamic-slice_bitcast_fusion.2
  373.5 88.8 %shard_map.240 = (f32[2,16,8,640]{3,2,1,0:T(8,128)S(1)}, f32[144,1152]{1,0:T(8,128)S(1)}) custom-call(f32[128,1280]{1,0:T(8,128)S(1)} %copy-done.2, bf16[4608,1152]{1,0:T(8,128)(2,1)} %get-tuple-element.68.grad_ref), custom_call_target="tpu_custom_call" | custom-call | tf_op jit(solution)/shard_map/pallas_call | solution.py:744
  462.4 0.6 fusion.30
  463.0 0.8 fusion.15
  463.8 0.5 reshape.307
  464.3 1.1 dynamic-slice_bitcast_fusion.1
  465.5 0.6 reduce_sum.19
  466.1 0.7 fusion.31
  467.0 0.6 div.41
  (115 shorter events, 2.7 us)
Async XLA Ops:
  0.6 4.5 copy-start.3
  8.6 2.2 copy-start.25
  8.7 2.5 copy-start.19
  10.9 3.1 copy-start.17
  10.9 3.1 copy-start.18
  11.0 3.0 copy-start.23
  11.4 3.4 copy-start.16
  126.1 0.7 copy-start.26
  126.1 0.9 copy-start.27
  126.2 1.3 copy-start.24
  126.2 1.6 copy-start.20
  126.2 1.7 copy-start.1
  127.9 54.6 %copy-start.21 = (s32[768]{0:T(1024)S(1)}, s32[768]{0:T(1024)}, u32[]{:S(2)}) copy-start(s32[768]{0:T(1024)} %constant.133.clone) | copy-start | bytes 9220
  127.9 54.6 %copy-start.22 = (s32[768]{0:T(1024)S(1)}, s32[768]{0:T(1024)}, u32[]{:S(2)}) copy-start(s32[768]{0:T(1024)} %constant.134.clone) | copy-start | bytes 9220
  177.9 0.8 copy-start.4
  178.7 0.8 copy-start.5
  179.4 0.8 copy-start.7
  180.2 0.8 copy-start.9
  181.0 0.8 copy-start.11
  181.7 0.8 copy-start.13
  234.2 6.8 %copy-start.6 = (f32[144,768]{1,0:T(8,128)S(1)}, f32[144,768]{1,0:T(8,128)}, u32[]{:S(2)}) copy-start(f32[144,768]{1,0:T(8,128)} %copy-done.5) | copy-start | bytes 1327108
  234.3 6.8 %copy-start.8 = (f32[144,768]{1,0:T(8,128)S(1)}, f32[144,768]{1,0:T(8,128)}, u32[]{:S(2)}) copy-start(f32[144,768]{1,0:T(8,128)} %copy-done.7) | copy-start | bytes 1327108
  234.3 6.8 %copy-start.10 = (f32[144,768]{1,0:T(8,128)S(1)}, f32[144,768]{1,0:T(8,128)}, u32[]{:S(2)}) copy-start(f32[144,768]{1,0:T(8,128)} %copy-done.9) | copy-start | bytes 1327108
  234.3 6.8 %copy-start.12 = (f32[144,768]{1,0:T(8,128)S(1)}, f32[144,768]{1,0:T(8,128)}, u32[]{:S(2)}) copy-start(f32[144,768]{1,0:T(8,128)} %copy-done.11) | copy-start | bytes 1327108
  234.3 6.8 %copy-start.14 = (f32[144,768]{1,0:T(8,128)S(1)}, f32[144,768]{1,0:T(8,128)}, u32[]{:S(2)}) copy-start(f32[144,768]{1,0:T(8,128)} %copy-done.13) | copy-start | bytes 1327108
  241.1 1.0 copy-start.15
  282.5 1.2 copy-start
  372.0 1.5 copy-start.2
